TPU v7x, 256 devices: a whole 4x4x8 slice. The times are simulated.
256 devices in a mesh: dom: 128 (over y, z, x), hid: 2 (over core).
Axes of the slice: x: 4, y: 4, z: 8, core: 2. Of those that a mesh axis runs over, the one named last changes fastest.
Arguments:
- feats: bfloat16 [524288, 256], P('dom', 'hid'), may hold values from -6 to 6
- adj_tiles: bfloat16 [32768, 128, 128], P('dom'), may hold values from -0.1875 to 0.1875
- adj_cols: int32 [4096, 8], P('dom'), may hold values from 0 to 63
- send_rows: int32 [16384, 32], P('dom'), may hold values from 0 to 4096, as said below
- weight: bfloat16 [256, 256], P('hid'), may hold values from -0.375 to 0.375
- bias: float32 [256], replicated, may hold values from -3 to 3
- cls_w: bfloat16 [256, 172], P('hid')
- labels: int32 [524288], P('dom'), may hold values from 0 to 171
Outputs:
- grad_feats: bfloat16 [524288, 256], P('dom', 'hid')
- grad_weight: float32 [256, 256], P('hid')
- grad_bias: float32 [256], replicated
- grad_cls: float32 [256, 172], P('hid')
Inputs may be any that keep to these rules, and one draw needn't show every extreme that they name: `send_rows`: an entry 4096 marks an empty slot, others name a local row of the sender; live slots come first in each row. For every sender, the row for the peer one index above it (with wrap) is full.
All inputs are finite; a program needn't handle non-finite values.
Results may differ from a plain program's by a relative error of at most 0.019.
The roundings to bfloat16 on the way count: a program that leaves them out, or rounds other values in their place, can miss the bound.
Values may be sent and summed in bfloat16 or wider, within the bound.
No kernel may reach another device: no remote copies, remote signals or barrier semaphores. Data moves between devices by JAX's collectives and lax.ppermute only.
A program may use at most 128 MiB of HBM per device.

v0:
```python
import jax
import jax.numpy as jnp
from jax import lax
from jax.sharding import PartitionSpec as P


def on_device(feats, adj_tiles, adj_cols, send_rows, weight, bias, cls_w, labels):
    row_count, half_width = feats.shape
    tile_size = adj_tiles.shape[1]
    blocks, nonzero = adj_cols.shape
    peer_count = lax.axis_size("dom")
    classes = cls_w.shape[1]
    padded = jnp.concatenate([feats, jnp.zeros((1, half_width), feats.dtype)], 0)
    outgoing = padded[send_rows]
    incoming = lax.all_to_all(outgoing, "dom", split_axis=0, concat_axis=0, tiled=True)
    extended = jnp.concatenate([feats, incoming.reshape(-1, half_width)], 0).reshape(
        -1, tile_size, half_width
    )
    ext_blocks = extended.shape[0]
    tile_blocks = adj_tiles.reshape(blocks, nonzero, tile_size, tile_size)
    selected = extended[adj_cols]
    aggregate = jnp.einsum(
        "rkij,rkjf->rif", tile_blocks, selected, preferred_element_type=jnp.float32
    )
    aggregate = aggregate.reshape(row_count, half_width).astype(jnp.bfloat16)
    onehot = (labels[:, None] == jnp.arange(classes, dtype=jnp.int32)[None, :]).astype(jnp.float32)
    hid_index = lax.axis_index("hid")
    preact_part = jnp.dot(aggregate, weight, preferred_element_type=jnp.float32)
    preact = lax.psum(preact_part, "hid") + bias
    hidden = jax.nn.relu(preact).astype(jnp.bfloat16)
    classifier = lax.all_gather(cls_w, "hid", axis=0, tiled=True)
    logits = jnp.dot(hidden, classifier, preferred_element_type=jnp.float32)
    logit_grad = (jax.nn.softmax(logits, axis=-1) - onehot).astype(jnp.bfloat16)
    hidden_grad = jnp.dot(logit_grad, classifier.T, preferred_element_type=jnp.float32)
    preact_grad = jnp.where(preact > 0, hidden_grad, 0.0).astype(jnp.bfloat16)
    own_hidden = lax.dynamic_slice_in_dim(hidden, hid_index * half_width, half_width, 1)
    weight_term = jnp.dot(aggregate.T, preact_grad, preferred_element_type=jnp.float32)
    class_term = jnp.dot(own_hidden.T, logit_grad, preferred_element_type=jnp.float32)
    bias_term = jnp.sum(preact_grad.astype(jnp.float32), 0)
    reduced = lax.psum((weight_term, class_term, bias_term), "dom")
    total_nodes = row_count * peer_count
    grad_weight = reduced[0] / total_nodes
    grad_cls = reduced[1] / total_nodes
    grad_bias = reduced[2] / total_nodes
    agg_grad = jnp.dot(preact_grad, weight.T, preferred_element_type=jnp.float32).astype(
        jnp.bfloat16
    )
    agg_grad = agg_grad.reshape(blocks, tile_size, half_width)
    contrib = jnp.einsum(
        "rkij,rif->rkjf", tile_blocks, agg_grad, preferred_element_type=jnp.float32
    )
    ext_grad = jax.ops.segment_sum(
        contrib.reshape(blocks * nonzero, tile_size, half_width),
        adj_cols.reshape(-1),
        num_segments=ext_blocks,
    )
    ext_grad = ext_grad.reshape(-1, half_width)
    local_grad = ext_grad[:row_count]
    returned = ext_grad[row_count:].reshape(peer_count, -1, half_width)
    arrived = lax.all_to_all(
        returned.astype(jnp.bfloat16), "dom", split_axis=0, concat_axis=0, tiled=True
    ).astype(returned.dtype)
    collected = (
        jnp.zeros((row_count + 1, half_width), jnp.float32)
        .at[send_rows.reshape(-1)]
        .add(arrived.reshape(-1, half_width))
    )
    grad_feats = (local_grad + collected[:row_count]).astype(jnp.bfloat16)
    return (grad_feats, grad_weight, grad_bias, grad_cls)


def solution(mesh):
    return jax.shard_map(
        on_device,
        mesh=mesh,
        in_specs=(
            P("dom", "hid"),
            P("dom", None, None),
            P("dom", None),
            P("dom", None),
            P("hid", None),
            P(),
            P("hid", None),
            P("dom"),
        ),
        out_specs=(P("dom", "hid"), P("hid", None), P(), P("hid", None)),
        check_vma=False,
    )
```

profile of v0, /device:TPU:2, one launch (start us, length us, event | category | flops | bytes accessed | tf_op | source)
XLA Modules:
  0.0 631.0 jit_solution(15079364341478518027)
XLA Ops:
  8.1 1.3 concatenate.6
  9.5 15.0 %gather_fusion = bf16[4096,128]{1,0:T(8,128)(2,1)} fusion(bf16[4097,128]{1,0:T(8,128)(2,1)S(1)} %concatenate.6, s32[4096]{0:T(1024)S(1)} %broadcast_clamp_fusion), kind=kCustom, calls=%fused_computation | custom fusion | bytes 2113536 | tf_op jit(solution)/shard_map/gather | solution.py:14
  24.5 15.4 %all-to-all-start = ((bf16[128,32,128]{2,1,0:T(8,128)(2,1)}), bf16[128,32,128]{2,1,0:T(8,128)(2,1)S(1)}, u32[]{:S(2)}, u32[]{:S(2)}) async-start(bf16[128,32,128]{2,1,0:T(8,128)(2,1)} %bitcast), calls=%async_computation | async-start | bytes 2097152 | tf_op jit(solution)/shard_map/all_to_all | solution.py:15
  40.2 29.0 %all-to-all-done = bf16[128,32,128]{2,1,0:T(8,128)(2,1)S(1)} async-done(((bf16[128,32,128]{2,1,0:T(8,128)(2,1)}), bf16[128,32,128]{2,1,0:T(8,128)(2,1)S(1)}, u32[]{:S(2)}, u32[]{:S(2)}) %all-to-all-start) | async-done | bytes 1048608 | tf_op jit(solution)/shard_map/all_to_all | solution.py:15
  70.2 1.4 pad_maximum_fusion
  71.5 8.6 %gather_fusion.1 = bf16[256,128,128]{2,1,0:T(8,128)(2,1)} fusion(bf16[64,128,128]{2,1,0:T(8,128)(2,1)S(1)} %bitcast.46, s32[1024]{0:T(1024)S(1)} %pad_clamp_fusion), kind=kCustom, calls=%fused_computation.1 | custom fusion | bytes 16778240 | tf_op jit(solution)/shard_map/gather | solution.py:21
  80.2 8.1 %bitcast_convert_fusion = bf16[32,128,128]{1,2,0:T(8,128)(2,1)S(1)} fusion(bf16[32,8,128,128]{3,2,1,0:T(8,128)(2,1)} %bitcast.41, bf16[32,8,128,128]{3,2,1,0:T(8,128)(2,1)} %bitcast.45), kind=kOutput, calls=%fused_computation.19 | convolution fusion | flops 1074266112 | bytes 17825792 | tf_op jit(solution)/shard_map/rkij,rkjf->rif/dot_general | solution.py:22
  88.3 2.7 fusion.10
  92.0 2.1 all_gather.3
  94.0 31.8 %all-reduce.5.cloned.1.call-done = f32[4096,256]{1,0:T(8,128)} async-done(((f32[4096,256]{1,0:T(8,128)}), f32[4096,256]{1,0:T(8,128)}) %all-reduce.5.cloned.1.call-update) | async-done | bytes 4194320 | tf_op jit(solution)/shard_map/psum | solution.py:29
  125.8 2.6 maximum_convert_fusion
  133.9 1.3 slice-done.1
  135.2 8.1 %fusion.11 = f32[32,128,8,128]{3,1,2,0:T(8,128)} fusion(bf16[32,128,128,1]{2,1,3,0:T(8,128)(2,1)S(1)} %bitcast.49, bf16[32,8,128,128]{3,2,1,0:T(8,128)(2,1)S(1)} %bitcast.44), kind=kOutput, calls=%fused_computation.34 | convolution fusion | flops 1073741824 | bytes 26214400 | tf_op jit(solution)/shard_map/rkij,rif->rkjf/dot_general | solution.py:49
  143.3 17.4 %copy.17 = f32[256,128,128]{2,1,0:T(8,128)} copy(f32[256,128,128]{1,2,0:T(8,128)} %bitcast.40) | data formatting | bytes 33554432 | tf_op jit(solution)/shard_map/reshape | solution.py:53
  160.8 2.4 broadcast_in_dim.9
  163.2 51.7 %scatter_fusion = f32[64,128,128]{2,1,0:T(8,128)} fusion(f32[64,128,128]{2,1,0:T(8,128)} %broadcast_in_dim.9, s32[256]{0:T(256)S(1)} %reshape.100, f32[256,128,128]{2,1,0:T(8,128)} %copy.17), kind=kCustom, calls=%fused_computation.2 | custom fusion | flops 4194304 | bytes 50332672 | tf_op jit(solution)/shard_map/scatter-add | solution.py:52
  214.9 2.7 slice.29
  217.7 14.3 %all-to-all-start.1 = ((bf16[128,32,128]{2,1,0:T(8,128)(2,1)}), bf16[128,32,128]{2,1,0:T(8,128)(2,1)}, u32[]{:S(2)}, u32[]{:S(2)}) async-start(bf16[128,32,128]{2,1,0:T(8,128)(2,1)} %bitcast.50), calls=%async_computation.1 | async-start | bytes 2097152 | tf_op jit(solution)/shard_map/all_to_all | solution.py:60
  232.1 3.3 slice.22
  237.8 355.4 %psum.30 = f32[256]{0:T(256)S(1)} all-reduce(f32[256]{0:T(256)S(1)} %get-tuple-element.8), channel_id=1, replica_groups=mesh['dom'=128,'hid'=2] {'dom'}, use_global_device_ids=true, to_apply=%region_7.8 | all-reduce | flops 256 | bytes 2048 | tf_op jit(solution)/shard_map/psum | solution.py:40
  593.7 1.5 broadcast_multiply_fusion.1
  595.3 1.6 broadcast_multiply_fusion
  596.9 24.5 %scatter_custom_fusion.1 = f32[4097,128]{1,0:T(8,128)S(1)} fusion(s32[4096]{0:T(1024)S(1)} %bitcast.52, bf16[4096,128]{1,0:T(8,128)(2,1)} %bitcast.21, f32[]{:T(128)} %constant.10.clone.1), kind=kCustom, calls=%fused_computation.17 | custom fusion | flops 1048576 | bytes 3146244 | tf_op jit(solution)/shard_map/scatter-add | solution.py:66
  621.4 2.8 fusion.2
  (59 shorter events, 11.7 us)
Async XLA Ops:
  7.2 81.1 %copy-start = (bf16[128,256]{1,0:T(8,128)(2,1)S(1)}, bf16[128,256]{1,0:T(8,128)(2,1)}, u32[]{:S(2)}) copy-start(bf16[128,256]{1,0:T(8,128)(2,1)} %param.12) | copy-start | bytes 196612
  9.4 30.5 %copy-start.12 = (s32[32,8]{0,1:T(8,128)S(1)}, s32[32,8]{0,1:T(8,128)}, u32[]{:S(2)}) copy-start(s32[32,8]{0,1:T(8,128)} %param.10) | copy-start | bytes 3076
  9.4 60.7 %copy-start.7 = (bf16[4096,128]{1,0:T(8,128)(2,1)S(1)}, bf16[4096,128]{1,0:T(8,128)(2,1)}, u32[]{:S(2)}) copy-start(bf16[4096,128]{1,0:T(8,128)(2,1)} %param.8) | copy-start | bytes 3145732
  24.5 44.7 %all-to-all-start = ((bf16[128,32,128]{2,1,0:T(8,128)(2,1)}), bf16[128,32,128]{2,1,0:T(8,128)(2,1)S(1)}, u32[]{:S(2)}, u32[]{:S(2)}) async-start(bf16[128,32,128]{2,1,0:T(8,128)(2,1)} %bitcast), calls=%async_computation | async-start | bytes 2097152 | tf_op jit(solution)/shard_map/all_to_all | solution.py:15
  39.9 85.9 %all-reduce.5.cloned.1.call-start = ((), (), s32[]{:S(2)}) async-start(), calls=%async_computation.2 | async-start | bytes 8388608 | tf_op jit(solution)/shard_map/psum | solution.py:29
  69.2 1.0 copy-start.8
  91.0 0.7 copy-start.9
  91.0 1.0 copy-start.10
  91.0 34.8 %copy-start.13 = (f32[256]{0:T(256)S(1)}, f32[256]{0:T(256)}, u32[]{:S(2)}) copy-start(f32[256]{0:T(256)} %param.13) | copy-start | bytes 3076
  129.3 0.7 copy-start.11
  129.3 2.2 copy-start.6
  130.0 3.9 slice-start
  131.5 1.1 copy-start.4
  131.5 3.8 slice-start.1
  132.6 1.4 copy-start.2
  217.7 379.2 %all-to-all-start.1 = ((bf16[128,32,128]{2,1,0:T(8,128)(2,1)}), bf16[128,32,128]{2,1,0:T(8,128)(2,1)}, u32[]{:S(2)}, u32[]{:S(2)}) async-start(bf16[128,32,128]{2,1,0:T(8,128)(2,1)} %bitcast.50), calls=%async_computation.1 | async-start | bytes 2097152 | tf_op jit(solution)/shard_map/all_to_all | solution.py:60
  232.0 361.8 %all-reduce.7.cloned.1.call-start = ((), (), s32[]{:S(2)}) async-start(), calls=%async_computation.3 | async-start | bytes 442368 | tf_op jit(solution)/shard_map/psum | solution.py:40
  232.0 3.3 copy-start.5
  232.1 4.5 copy-start.3
  596.9 27.3 %copy-start.1 = (bf16[128,256]{1,0:T(8,128)(2,1)S(1)}, bf16[128,256]{1,0:T(8,128)(2,1)}, u32[]{:S(2)}) copy-start(bf16[128,256]{1,0:T(8,128)(2,1)} %param.12) | copy-start | bytes 196612
Sparse Core Ops, SparseCore 0:
  91.1 34.6 all-reduce.4
  239.8 214.3 all-reduce.6
where the time goes:
time: 632 us; the launch traced here: 631 us
  blocking collectives  357 us (56%)
  other arithmetic  88.6 us (14%)
  waiting for transfers between devices  60.8 us (10%)
  local copies, waits for them, and re-layouts  56.2 us (9%)
  starting transfers between devices  29.8 us (5%)
  matrix products  23.9 us (4%)
  between operations  14.2 us (2%)
    psum x1, blocking collectives, on_device(): reduced = lax.psum((weight_term, class_term, bias_term), 'dom')  355 us
    scatter-add x1, other arithmetic, on_device(): jax.ops.segment_sum(contrib.reshape(blocks * nonzero, tile_size, half_wid...  51.7 us
    psum x1, waiting for transfers between devices, on_device(): preact = lax.psum(preact_part, 'hid') + bias  31.8 us
    all_to_all x1, waiting for transfers between devices, on_device(): lax.all_to_all(outgoing, 'dom', split_axis=0, concat_axis=0, tiled=True)  29 us
    scatter-add x1, other arithmetic, on_device(): collected = jnp.zeros((row_count + 1, half_width), jnp.float32).at[send_r...  24.5 us
    reshape x1, local copies, waits for them, and re-layouts, on_device(): contrib.reshape(blocks * nonzero, tile_size, half_width)  17.4 us
    all_to_all x1, starting transfers between devices, on_device(): lax.all_to_all(outgoing, 'dom', split_axis=0, concat_axis=0, tiled=True)  15.4 us
    gather x1, local copies, waits for them, and re-layouts, on_device(): outgoing = padded[send_rows]  15 us
  transfers between devices with their start and end apart: 4, of which 2 were waited for; matrix products, arithmetic and copies ran while one was open for 2% of the time, Pallas kernels for 0%

commit v1 on v0

v1 whole, which is shorter than its diff:
```python
import jax
import jax.numpy as jnp
from jax import lax
from jax.experimental import pallas as pl
from jax.experimental.pallas import tpu as pltpu
from jax.sharding import PartitionSpec as P

F32 = jnp.float32
BF16 = jnp.bfloat16
MIB = 1 << 20
VMEM = pl.BlockSpec(memory_space=pltpu.VMEM)
SMEM = pl.BlockSpec(memory_space=pltpu.SMEM)
ANY = pl.BlockSpec(memory_space=pl.ANY)
NX, NY, NZ = 4, 4, 8
LINE = 128
SPAN = 512


def contract(a, b, da, db):
    return lax.dot_general(a, b, (((da,), (db,)), ((), ())), preferred_element_type=F32)


def gather_kernel(rows, feats, out, table, picked):
    peers, cap = rows.shape
    count = feats.shape[0]
    table[pl.ds(0, count), :] = feats[...].astype(F32)
    table[pl.ds(count, 8), :] = jnp.zeros((8, table.shape[1]), F32)

    def one_peer(p, carry):
        base = pl.multiple_of(p * cap, cap)
        for c in range(cap):
            picked[pl.ds(base + c, 1), :] = table[pl.ds(rows[p, c], 1), :]
        return carry

    lax.fori_loop(0, peers, one_peer, 0)
    out[...] = picked[...].astype(BF16)


def gather_rows(send_rows, feats):
    count, width = feats.shape
    slots = send_rows.size
    return pl.pallas_call(
        gather_kernel,
        out_shape=jax.ShapeDtypeStruct((slots, width), BF16),
        in_specs=[SMEM, VMEM],
        out_specs=VMEM,
        scratch_shapes=[pltpu.VMEM((count + 8, width), F32), pltpu.VMEM((slots, width), F32)],
        compiler_params=pltpu.CompilerParams(vmem_limit_bytes=24 * MIB),
        name="gather_rows",
    )(send_rows, feats)


def aggregate_kernel(cols, feats, halo, adj, agg, ext, tiles, sems):
    blocks, nonzero = cols.shape
    steps = sems.shape[0] - 2
    span = adj.shape[0] // steps
    own_copy = pltpu.make_async_copy(feats, ext.at[pl.ds(0, blocks)], sems.at[0])
    halo_copy = pltpu.make_async_copy(halo, ext.at[pl.ds(blocks, halo.shape[0])], sems.at[1])

    def tile_copy(i):
        return pltpu.make_async_copy(
            adj.at[pl.ds(i * span, span)], tiles.at[pl.ds(i * span, span)], sems.at[2 + i]
        )

    own_copy.start()
    halo_copy.start()
    for i in range(steps):
        tile_copy(i).start()
    own_copy.wait()
    halo_copy.wait()

    def one_step(i, carry):
        tile_copy(i).wait()
        for j in range(span // nonzero):
            r = i * (span // nonzero) + j
            left = jnp.concatenate([tiles[r * nonzero + k] for k in range(nonzero)], 1)
            right = jnp.concatenate([ext[cols[r, k]] for k in range(nonzero)], 0)
            agg[r] = contract(left, right, 1, 0).astype(BF16)
        return carry

    lax.fori_loop(0, steps, one_step, 0)


def aggregate_blocks(cols, feats, halo, adj):
    steps = 8
    return pl.pallas_call(
        aggregate_kernel,
        out_shape=jax.ShapeDtypeStruct(feats.shape, BF16),
        in_specs=[SMEM, ANY, ANY, ANY],
        out_specs=VMEM,
        scratch_shapes=[
            pltpu.VMEM((feats.shape[0] + halo.shape[0],) + feats.shape[1:], BF16),
            pltpu.VMEM(adj.shape, BF16),
            pltpu.SemaphoreType.DMA((2 + steps,)),
        ],
        compiler_params=pltpu.CompilerParams(vmem_limit_bytes=24 * MIB),
        name="aggregate_blocks",
    )(cols, feats, halo, adj)


def backward_kernel(
    classes, total_nodes, ids, cols, agg, other, weight_t, weight, cls, cls_t, bias, labels, adj,
    halo_out, own_out, share0, share1, share2, share3,
    ext_grad, tiles, packed, sum_w, sum_c, sum_b, sems, own_sem,
):
    blocks, nonzero = cols.shape
    tile = adj.shape[1]
    steps = sems.shape[0]
    span = adj.shape[0] // steps
    per_step = SPAN // tile
    hid = ids[0]

    def tile_copy(i):
        return pltpu.make_async_copy(
            adj.at[pl.ds(i * span, span)], tiles.at[pl.ds(i * span, span)], sems.at[i]
        )

    for i in range(steps):
        tile_copy(i).start()
    ext_grad[...] = jnp.zeros_like(ext_grad)
    sum_w[...] = jnp.zeros_like(sum_w)
    sum_c[...] = jnp.zeros_like(sum_c)
    sum_b[...] = jnp.zeros_like(sum_b)
    class_rows = cls_t.shape[0]
    class_id = lax.broadcasted_iota(jnp.int32, (class_rows, SPAN), 0)
    first = hid == 0
    half = agg.shape[1]

    def one_step(i, carry):
        nodes = pl.ds(pl.multiple_of(i * SPAN, SPAN), SPAN)
        mine = agg[nodes, :]
        theirs = other[nodes, :]
        both = jnp.concatenate(
            [jnp.where(first, mine, theirs), jnp.where(first, theirs, mine)], 1
        )
        preact = contract(weight_t[...], both, 1, 1) + jnp.tile(bias[...], (1, SPAN // bias.shape[1]))
        hidden = jnp.maximum(preact, 0.0).astype(BF16)
        logits = contract(cls_t[...], hidden, 1, 0)
        logits = jnp.where(class_id < classes, logits, -jnp.inf)
        powers = jnp.exp(logits - jnp.max(logits, 0, keepdims=True))
        share = powers / jnp.sum(powers, 0, keepdims=True)
        label = labels[pl.ds(i, 1), :]
        logit_grad = (share - jnp.where(class_id == label, 1.0, 0.0)).astype(BF16)
        hidden_grad = contract(cls[...], logit_grad, 1, 0)
        preact_grad = jnp.where(preact > 0, hidden_grad, 0.0).astype(BF16)
        own_hidden = jnp.where(first, hidden[:half], hidden[half:])
        sum_w[...] += contract(preact_grad, mine, 1, 0)
        sum_c[...] += contract(logit_grad, own_hidden, 1, 1)
        sum_b[...] += contract(jnp.ones((8, SPAN), BF16), preact_grad, 1, 1)
        agg_grad = contract(weight[...], preact_grad, 1, 0).astype(BF16)
        tile_copy(i).wait()
        for j in range(per_step):
            r = i * per_step + j
            right = jnp.concatenate([tiles[r * nonzero + k] for k in range(nonzero)], 1)
            term = contract(agg_grad[:, j * tile : (j + 1) * tile], right, 1, 0)
            for k in range(nonzero):
                ext_grad[cols[r, k]] += term[:, k * tile : (k + 1) * tile]
        return carry

    lax.fori_loop(0, steps, one_step, 0)
    own_copy = pltpu.make_async_copy(ext_grad.at[pl.ds(0, blocks)], own_out, own_sem)
    own_copy.start()

    def one_halo(b, carry):
        halo_out[b] = ext_grad[blocks + b].T.astype(BF16)
        return carry

    lax.fori_loop(0, halo_out.shape[0], one_halo, 0, unroll=4)
    scale = 1.0 / total_nodes
    units = 2 * half
    packed[pl.ds(0, units), :] = sum_w[...] * scale
    packed[pl.ds(units, class_rows), :] = sum_c[...] * scale
    packed[pl.ds(units + class_rows, 8), :] = sum_b[:, :half] * scale
    packed[pl.ds(units + class_rows + 8, 8), :] = sum_b[:, half:] * scale
    rest = units + class_rows + 16
    packed[pl.ds(rest, packed.shape[0] - rest), :] = jnp.zeros((packed.shape[0] - rest, half), F32)
    for d, target in enumerate((share0, share1, share2, share3)):
        start = pl.multiple_of(lax.rem(ids[1] + d, NX) * LINE, LINE)
        target[...] = packed[pl.ds(start, LINE), :]
    own_copy.wait()


def backward(ids, cols, agg, other, weight_t, weight, cls, cls_t, bias, labels, adj, classes, total_nodes):
    blocks = cols.shape[0]
    tile = adj.shape[1]
    rows, half = agg.shape
    steps = rows // SPAN
    class_rows = cls_t.shape[0]
    ext_blocks = 2 * blocks

    def body(*refs):
        backward_kernel(classes, total_nodes, *refs)

    share = jax.ShapeDtypeStruct((LINE, half), F32)
    return pl.pallas_call(
        body,
        out_shape=(
            jax.ShapeDtypeStruct((blocks, tile, half), BF16),
            jax.ShapeDtypeStruct((blocks, half, tile), F32),
        ) + (share,) * NX,
        in_specs=[SMEM, SMEM] + [VMEM] * 8 + [ANY],
        out_specs=(VMEM, ANY) + (VMEM,) * NX,
        scratch_shapes=[
            pltpu.VMEM((ext_blocks, half, tile), F32),
            pltpu.VMEM(adj.shape, BF16),
            pltpu.VMEM((NX * LINE, half), F32),
            pltpu.VMEM((2 * half, half), F32),
            pltpu.VMEM((class_rows, half), F32),
            pltpu.VMEM((8, 2 * half), F32),
            pltpu.SemaphoreType.DMA((steps,)),
            pltpu.SemaphoreType.DMA,
        ],
        compiler_params=pltpu.CompilerParams(vmem_limit_bytes=36 * MIB),
        name="backward",
    )(ids, cols, agg, other, weight_t, weight, cls, cls_t, bias, labels, adj)


def scatter_kernel(rows, arrived, own, out, values, *sums):
    peers, cap = rows.shape
    count, width = out.shape
    values[...] = arrived[...].astype(F32)
    for total in sums:
        total[...] = jnp.zeros_like(total)

    def one_peer(p, carry):
        base = pl.multiple_of(p * cap, cap)
        for c in range(cap):
            total = sums[c % len(sums)]
            row = pl.ds(rows[p, c], 1)
            total[row, :] = total[row, :] + values[pl.ds(base + c, 1), :]
        return carry

    lax.fori_loop(0, peers, one_peer, 0)
    result = own[...]
    for total in sums:
        result = result + total[pl.ds(0, count), :]
    out[...] = result.astype(BF16)


def scatter_rows(send_rows, arrived, own):
    count, width = own.shape
    lanes = 8
    return pl.pallas_call(
        scatter_kernel,
        out_shape=jax.ShapeDtypeStruct((count, width), BF16),
        in_specs=[SMEM, VMEM, VMEM],
        out_specs=VMEM,
        scratch_shapes=[pltpu.VMEM(arrived.shape, F32)]
        + [pltpu.VMEM((count + 8, width), F32)] * lanes,
        compiler_params=pltpu.CompilerParams(vmem_limit_bytes=36 * MIB),
        name="scatter_rows",
    )(send_rows, arrived, own)


def small_call(body, outs, ids, arrays, scratch, name):
    return pl.pallas_call(
        body,
        out_shape=outs,
        in_specs=[SMEM] + [VMEM] * len(arrays),
        out_specs=jax.tree.map(lambda _: VMEM, outs),
        scratch_shapes=[pltpu.VMEM(scratch, F32)],
        compiler_params=pltpu.CompilerParams(vmem_limit_bytes=4 * MIB),
        name=name,
    )(ids, *arrays)


def shift(value, axis, step):
    sizes = {"x": NX, "y": NY, "z": NZ}
    pairs = []
    for y in range(NY):
        for z in range(NZ):
            for x in range(NX):
                place = {"x": x, "y": y, "z": z}
                source = (y * NZ + z) * NX + x
                place[axis] = (place[axis] + step) % sizes[axis]
                pairs.append((source, (place["y"] * NZ + place["z"]) * NX + place["x"]))
    return lax.ppermute(value, "dom", pairs)


def sum_nodes(ids, shares, classes, half):
    got = [shares[0]] + [shift(shares[d], "x", d) for d in range(1, NX)]
    part = LINE // NY

    def split_y(ids, a, b, c, d, o0, o1, o2, o3, total):
        total[...] = (a[...] + b[...]) + (c[...] + d[...])
        for k, target in enumerate((o0, o1, o2, o3)):
            start = pl.multiple_of(lax.rem(ids[2] + k, NY) * part, part)
            target[...] = total[pl.ds(start, part), :]

    piece = jax.ShapeDtypeStruct((part, half), F32)
    pieces = small_call(split_y, (piece,) * NY, ids, got, (LINE, half), "split_y")
    got = [pieces[0]] + [shift(pieces[d], "y", d) for d in range(1, NY)]
    mine = (got[0] + got[1]) + (got[2] + got[3])
    got = [mine] + [shift(mine, "z", d) for d in range(1, NZ)]

    def sum_z(ids, *refs):
        out, slots = refs[NZ], refs[NZ + 1]
        for d in range(NZ):
            start = pl.multiple_of(lax.rem(ids[3] + NZ - d, NZ) * part, part)
            slots[pl.ds(start, part), :] = refs[d][...]
        total = slots[pl.ds(0, part), :]
        for k in range(1, NZ):
            total = total + slots[pl.ds(k * part, part), :]
        out[...] = total

    mine = small_call(sum_z, piece, ids, got, (NZ * part, half), "sum_z")
    got = [mine] + [shift(mine, "y", d) for d in range(1, NY)]

    def join_y(ids, a, b, c, d, out, unused):
        for k, source in enumerate((a, b, c, d)):
            start = pl.multiple_of(lax.rem(ids[2] + NY - k, NY) * part, part)
            out[pl.ds(start, part), :] = source[...]

    line = jax.ShapeDtypeStruct((LINE, half), F32)
    mine = small_call(join_y, line, ids, got, (8, half), "join_y")
    got = [mine] + [shift(mine, "x", d) for d in range(1, NX)]
    units = 2 * half
    class_rows = -(-classes // 8) * 8

    def join_x(ids, a, b, c, d, out_w, out_c, out_b, packed):
        for k, source in enumerate((a, b, c, d)):
            start = pl.multiple_of(lax.rem(ids[1] + NX - k, NX) * LINE, LINE)
            packed[pl.ds(start, LINE), :] = source[...]
        for k in range(units // half):
            out_w[:, k * half : (k + 1) * half] = packed[pl.ds(k * half, half), :].T
        out_c[:, :half] = packed[pl.ds(units, half), :].T
        out_c[:, half:] = packed[pl.ds(units + half, half), :].T[:, : classes - half]
        for k in range(units // half):
            row = units + class_rows + 8 * k
            out_b[:, k * half : (k + 1) * half] = packed[pl.ds(row, 8), :]

    outs = (
        jax.ShapeDtypeStruct((half, units), F32),
        jax.ShapeDtypeStruct((half, classes), F32),
        jax.ShapeDtypeStruct((8, units), F32),
    )
    grad_weight, grad_cls, grad_bias = small_call(
        join_x, outs, ids, got, (NX * LINE, half), "join_x"
    )
    return grad_weight, grad_cls, grad_bias[0]


def on_device(feats, adj_tiles, adj_cols, send_rows, weight, bias, cls_w, labels):
    row_count, half = feats.shape
    tile = adj_tiles.shape[1]
    blocks = adj_cols.shape[0]
    peers, cap = send_rows.shape
    classes = cls_w.shape[1]
    units = weight.shape[1]
    total_nodes = row_count * lax.axis_size("dom")
    swap = [(0, 1), (1, 0)]

    outgoing = gather_rows(send_rows, feats).reshape(peers, cap, half)
    incoming = lax.all_to_all(outgoing, "dom", split_axis=0, concat_axis=0, tiled=True)

    weight_l, cls_l, bias_l, labels_l, _ = lax.optimization_barrier(
        (weight, cls_w, bias, labels, outgoing)
    )
    hid = lax.axis_index("hid")
    dom = lax.axis_index("dom")
    ids = jnp.stack([hid, dom % NX, dom // (NX * NZ), (dom // NX) % NZ]).astype(jnp.int32)
    weight_o = lax.ppermute(weight_l, "hid", swap)
    cls_o = lax.ppermute(cls_l, "hid", swap)
    first = hid == 0
    weight_full = jnp.concatenate(
        [jnp.where(first, weight_l, weight_o), jnp.where(first, weight_o, weight_l)], 0
    )
    cls_full = jnp.concatenate(
        [jnp.where(first, cls_l, cls_o), jnp.where(first, cls_o, cls_l)], 0
    )
    class_rows = -(-classes // 8) * 8
    cls_full = jnp.pad(cls_full, ((0, 0), (0, class_rows - classes)))
    bias_wide = jnp.broadcast_to(bias_l[:, None], (units, 128))
    label_rows = labels_l.reshape(row_count // SPAN, SPAN)

    halo = incoming.reshape(blocks, tile, half)
    agg = aggregate_blocks(adj_cols, feats.reshape(blocks, tile, half), halo, adj_tiles)
    agg = agg.reshape(row_count, half)
    other = lax.ppermute(agg, "hid", swap)
    halo_grad, own_grad, *shares = backward(
        ids, adj_cols, agg, other, weight_full.T, weight_l, cls_full, cls_full.T, bias_wide,
        label_rows, adj_tiles, classes, total_nodes,
    )
    returned = halo_grad.reshape(peers, cap, half)
    arrived = lax.all_to_all(returned, "dom", split_axis=0, concat_axis=0, tiled=True)
    own = jnp.swapaxes(own_grad, 1, 2).reshape(row_count, half)
    grad_weight, grad_cls, grad_bias = sum_nodes(ids, shares, classes, half)
    grad_feats = scatter_rows(send_rows, arrived.reshape(row_count, half), own)
    return (grad_feats, grad_weight, grad_bias, grad_cls)


def solution(mesh):
    return jax.shard_map(
        on_device,
        mesh=mesh,
        in_specs=(
            P("dom", "hid"),
            P("dom", None, None),
            P("dom", None),
            P("dom", None),
            P("hid", None),
            P(),
            P("hid", None),
            P("dom"),
        ),
        out_specs=(P("dom", "hid"), P("hid", None), P(), P("hid", None)),
        check_vma=False,
    )
```

time: 632 us -> 162 us (0.26)
  blocking collectives: 357 us -> 0 us
  other arithmetic: 88.6 us -> 0.15 us
  local copies, waits for them, and re-layouts: 56.2 us -> 15.2 us
  Pallas kernels: 0 us -> 39 us
  starting transfers between devices: 29.8 us -> 58.6 us
  matrix products: 23.9 us -> 0 us
  waiting for transfers between devices: 60.8 us -> 46.9 us
  between operations: 14.2 us -> 0.87 us
    psum x1 -> x0, blocking collectives: 355 us -> none  [on_device(): reduced = lax.psum((weight_term, class_term, bias_term), 'dom')]
    scatter-add x2 -> x0, other arithmetic: 76.2 us -> none  [the longest x1 51.7 us: on_device(): jax.ops.segment_sum(contrib.reshape(blocks * nonzero, tile_size, half_wid...]
    pallas_call x0 -> x8, Pallas kernels: none -> 39 us  [the longest x1 15.7 us: backward(): pl.pallas_call(body, out_shape=(jax.ShapeDtypeStruct((blocks, tile, half)...]
    ppermute x0 -> x22, starting transfers between devices: none -> 35.3 us  [the longest x19 34.5 us: shift(): return lax.ppermute(value, 'dom', pairs)]
    psum x2 -> x0, waiting for transfers between devices: 31.8 us -> none  [the longest x1 31.8 us: on_device(): preact = lax.psum(preact_part, 'hid') + bias]
    dot_general x8 -> x0, matrix products: 23.9 us -> none  [the longest x1 8.1 us: on_device(): jnp.einsum('rkij,rkjf->rif', tile_blocks, selected, preferred_element_typ...]
    gather x2 -> x0, local copies, waits for them, and re-layouts: 23.7 us -> none  [the longest x1 15 us: on_device(): outgoing = padded[send_rows]]
    ppermute x0 -> x22, waiting for transfers between devices: none -> 17.6 us  [the longest x19 15.8 us: shift(): return lax.ppermute(value, 'dom', pairs)]
  transfers between devices with their start and end apart: 4 -> 24, of which waited for: 2 -> 12; matrix products, arithmetic and copies ran while one was open for 2% -> 2% of each run, Pallas kernels for 0% -> 2%
where the time goes in v1:
time: 162 us; the launch traced here: 161 us
  starting transfers between devices  58.6 us (36%)
  waiting for transfers between devices  46.9 us (29%)
  Pallas kernels  39 us (24%)
  local copies, waits for them, and re-layouts  15.2 us (9%)
    ppermute x19, starting transfers between devices, shift(): return lax.ppermute(value, 'dom', pairs)  34.5 us
    all_to_all x1, waiting for transfers between devices, on_device(): lax.all_to_all(outgoing, 'dom', split_axis=0, concat_axis=0, tiled=True)  29.2 us
    ppermute x19, waiting for transfers between devices, shift(): return lax.ppermute(value, 'dom', pairs)  15.8 us
    pallas_call x1, Pallas kernels, backward(): pl.pallas_call(body, out_shape=(jax.ShapeDtypeStruct((blocks, tile, half)...  15.7 us
    all_to_all x1, starting transfers between devices, on_device(): lax.all_to_all(outgoing, 'dom', split_axis=0, concat_axis=0, tiled=True)  15.4 us
    unnamed x27, local copies, waits for them, and re-layouts  12.5 us
    pallas_call x1, Pallas kernels, scatter_rows(): pl.pallas_call(scatter_kernel, out_shape=jax.ShapeDtypeStruct((count, wid...  8.45 us
    all_to_all x1, starting transfers between devices, on_device(): lax.all_to_all(returned, 'dom', split_axis=0, concat_axis=0, tiled=True)  7.9 us
  transfers between devices with their start and end apart: 24, of which 12 were waited for; matrix products, arithmetic and copies ran while one was open for 2% of the time, Pallas kernels for 2%

profile of v1, /device:TPU:2, one launch (start us, length us, event | category | flops | bytes accessed | tf_op | source)
XLA Modules:
  0.0 160.7 jit_solution(11264296418394208261)
XLA Ops:
  2.7 6.7 %gather_rows.1 = bf16[4096,128]{1,0:T(8,128)(2,1)} custom-call(s32[128,32]{1,0:T(8,128)S(1)} %copy.20.rows, bf16[4096,128]{1,0:T(8,128)(2,1)S(1)} %copy-done.2), custom_call_target="tpu_custom_call" | custom-call | tf_op jit(solution)/shard_map/gather_rows/pallas_call | solution.py:42
  9.4 15.4 %all-to-all-start = ((bf16[128,32,128]{2,1,0:T(8,128)(2,1)}), bf16[128,32,128]{2,1,0:T(8,128)(2,1)S(1)}, u32[]{:S(2)}, u32[]{:S(2)}) async-start(bf16[128,32,128]{2,1,0:T(8,128)(2,1)} %bitcast.5), calls=%async_computation | async-start | bytes 2097152 | tf_op jit(solution)/shard_map/all_to_all | solution.py:354
  24.9 29.2 %all-to-all-done = bf16[128,32,128]{2,1,0:T(8,128)(2,1)S(1)} async-done(((bf16[128,32,128]{2,1,0:T(8,128)(2,1)}), bf16[128,32,128]{2,1,0:T(8,128)(2,1)S(1)}, u32[]{:S(2)}, u32[]{:S(2)}) %all-to-all-start) | async-done | bytes 1048608 | tf_op jit(solution)/shard_map/all_to_all | solution.py:354
  54.1 3.4 %copy-done = bf16[256,128,128]{2,1,0:T(8,128)(2,1)S(1)} copy-done((bf16[256,128,128]{2,1,0:T(8,128)(2,1)S(1)}, bf16[256,128,128]{2,1,0:T(8,128)(2,1)}, u32[]{:S(2)}) %copy-start) | copy-done | bytes 8388632
  57.5 5.0 %aggregate_blocks.1 = bf16[32,128,128]{2,1,0:T(8,128)(2,1)S(1)} custom-call(s32[32,8]{1,0:T(8,128)S(1)} %copy.17.cols.refs_1_, bf16[32,128,128]{2,1,0:T(8,128)(2,1)S(1)} %bitcast.21, bf16[32,128,128]{2,1,0:T(8,128)(2,1)S(1)} %bitcast.22, bf16[256,128,128]{2,1,0:T(8,128)(2,1)S(1)} %copy-done), custom_call_target="tpu_custom_call" | custom-call | tf_op jit(solution)/shard_map/aggregate_blocks/pallas_call | solution.py:86
  63.6 1.8 %collective-permute-done.2 = bf16[128,172]{0,1:T(8,128)(2,1)S(1)} collective-permute-done((bf16[128,172]{0,1:T(8,128)(2,1)S(1)}, bf16[128,172]{0,1:T(8,128)(2,1)S(1)}, u32[]{:S(2)}, u32[]{:S(2)}) %collective-permute-start.2) | collective-permute-done | bytes 44064 | tf_op jit(solution)/shard_map/ppermute | solution.py:363
  65.7 3.4 %copy-done.1 = bf16[256,128,128]{2,1,0:T(8,128)(2,1)S(1)} copy-done((bf16[256,128,128]{2,1,0:T(8,128)(2,1)S(1)}, bf16[256,128,128]{2,1,0:T(8,128)(2,1)}, u32[]{:S(2)}) %copy-start.1) | copy-done | bytes 8388632
  69.1 15.7 %backward.1 = (bf16[32,128,128]{2,1,0:T(8,128)(2,1)}, f32[32,128,128]{2,1,0:T(8,128)S(1)}, f32[128,128]{1,0:T(8,128)S(1)}, f32[128,128]{1,0:T(8,128)S(1)}, f32[1...) custom-call(s32[4]{0:T(128)S(1)} %pad_add_fusion.refs_0_.ids, s32[32,8]{1,0:T(8,128)S(1)} %copy.17.cols.refs_1_, ...), custom_call_target="tpu_custom_call" | custom-call | tf_op jit(solution)/shard_map/backward/pallas_call | solution.py:195
  86.2 7.9 %all-to-all-start.1 = ((bf16[128,32,128]{2,1,0:T(8,128)(2,1)}), bf16[128,32,128]{2,1,0:T(8,128)(2,1)S(1)}, u32[]{:S(2)}, u32[]{:S(2)}) async-start(bf16[128,32,128]{2,1,0:T(8,128)(2,1)} %bitcast.10), calls=%async_computation.1 | async-start | bytes 2097152 | tf_op jit(solution)/shard_map/all_to_all | solution.py:385
  97.1 1.7 %collective-permute-start.5 = (f32[128,128]{1,0:T(8,128)S(1)}, f32[128,128]{1,0:T(8,128)S(1)}, u32[]{:S(2)}, u32[]{:S(2)}) collective-permute-start(f32[128,128]{1,0:T(8,128)S(1)} %get-tuple-element.30), channel_id=1, source_target_pairs={{0,6},{2,0},{4,2},{6,4},{8,14},{10,8},{12,10},{14,12},{16,22},{18,... | collective-permute-start | bytes 196616 | tf_op jit(solution)/shard_map/ppermute | solution.py:277
  100.3 3.3 %collective-permute-done.4.c = f32[128,128]{1,0:T(8,128)S(1)} collective-permute-done((f32[128,128]{1,0:T(8,128)S(1)}, f32[128,128]{1,0:T(8,128)S(1)}, u32[]{:S(2)}, u32[]{:S(2)}) %collective-permute-start.4) | collective-permute-done | bytes 65568 | tf_op jit(solution)/shard_map/ppermute | solution.py:277
  105.9 3.1 %collective-permute-start.7 = (f32[32,128]{1,0:T(8,128)S(1)}, f32[32,128]{1,0:T(8,128)S(1)}, u32[]{:S(2)}, u32[]{:S(2)}) collective-permute-start(f32[32,128]{1,0:T(8,128)S(1)} %get-tuple-element.33), channel_id=1, source_target_pairs={{0,128},{2,130},{4,132},{6,134},{8,136},{10,138},{12,140},{14,142}... | collective-permute-start | bytes 49160 | tf_op jit(solution)/shard_map/ppermute | solution.py:277
  112.9 3.1 %collective-permute-start.15 = (f32[32,128]{1,0:T(8,128)S(1)}, f32[32,128]{1,0:T(8,128)S(1)}, u32[]{:S(2)}, u32[]{:S(2)}) collective-permute-start(f32[32,128]{1,0:T(8,128)S(1)} %add_add_fusion.refs_0_), channel_id=1, source_target_pairs={{0,56},{2,58},{4,60},{6,62},{8,0},{10,2},{12,4},{14,6},{16,8},{18,... | collective-permute-start | bytes 49160 | tf_op jit(solution)/shard_map/ppermute | solution.py:277
  116.0 1.6 collective-permute-start.14
  119.0 4.7 %collective-permute-start.12 = (f32[32,128]{1,0:T(8,128)S(1)}, f32[32,128]{1,0:T(8,128)S(1)}, u32[]{:S(2)}, u32[]{:S(2)}) collective-permute-start(f32[32,128]{1,0:T(8,128)S(1)} %add_add_fusion.refs_0_), channel_id=1, source_target_pairs={{0,32},{2,34},{4,36},{6,38},{8,40},{10,42},{12,44},{14,46},{16,48}... | collective-permute-start | bytes 49160 | tf_op jit(solution)/shard_map/ppermute | solution.py:277
  123.8 2.8 %collective-permute-start.10 = (f32[32,128]{1,0:T(8,128)S(1)}, f32[32,128]{1,0:T(8,128)S(1)}, u32[]{:S(2)}, u32[]{:S(2)}) collective-permute-start(f32[32,128]{1,0:T(8,128)S(1)} %add_add_fusion.refs_0_), channel_id=1, source_target_pairs={{0,16},{2,18},{4,20},{6,22},{8,24},{10,26},{12,28},{14,30},{16,32}... | collective-permute-start | bytes 49160 | tf_op jit(solution)/shard_map/ppermute | solution.py:277
  126.5 1.9 %collective-permute-start.9 = (f32[32,128]{1,0:T(8,128)S(1)}, f32[32,128]{1,0:T(8,128)S(1)}, u32[]{:S(2)}, u32[]{:S(2)}) collective-permute-start(f32[32,128]{1,0:T(8,128)S(1)} %add_add_fusion.refs_0_), channel_id=1, source_target_pairs={{0,8},{2,10},{4,12},{6,14},{8,16},{10,18},{12,20},{14,22},{16,24},... | collective-permute-start | bytes 49160 | tf_op jit(solution)/shard_map/ppermute | solution.py:277
  128.5 2.0 %collective-permute-done.11.refs_3_ = f32[32,128]{1,0:T(8,128)S(1)} collective-permute-done((f32[32,128]{1,0:T(8,128)S(1)}, f32[32,128]{1,0:T(8,128)S(1)}, u32[]{:S(2)}, u32[]{:S(2)}) %collective-permute-start.11) | collective-permute-done | bytes 16416 | tf_op jit(solution)/shard_map/ppermute | solution.py:277
  132.0 2.7 %collective-permute-start.18 = (f32[32,128]{1,0:T(8,128)S(1)}, f32[32,128]{1,0:T(8,128)S(1)}, u32[]{:S(2)}, u32[]{:S(2)}) collective-permute-start(f32[32,128]{1,0:T(8,128)S(1)} %sum_z.1.a), channel_id=1, source_target_pairs={{0,192},{2,194},{4,196},{6,198},{8,200},{10,202},{12,204},{14,206}... | collective-permute-start | bytes 49160 | tf_op jit(solution)/shard_map/ppermute | solution.py:277
  136.2 3.8 %collective-permute-done.17.c = f32[32,128]{1,0:T(8,128)S(1)} collective-permute-done((f32[32,128]{1,0:T(8,128)S(1)}, f32[32,128]{1,0:T(8,128)S(1)}, u32[]{:S(2)}, u32[]{:S(2)}) %collective-permute-start.17) | collective-permute-done | bytes 16416 | tf_op jit(solution)/shard_map/ppermute | solution.py:277
  140.5 1.7 %collective-permute-start.21 = (f32[128,128]{1,0:T(8,128)S(1)}, f32[128,128]{1,0:T(8,128)S(1)}, u32[]{:S(2)}, u32[]{:S(2)}) collective-permute-start(f32[128,128]{1,0:T(8,128)S(1)} %join_y.1.a), channel_id=1, source_target_pairs={{0,6},{2,0},{4,2},{6,4},{8,14},{10,8},{12,10},{14,12},{16,22},{18,... | collective-permute-start | bytes 196616 | tf_op jit(solution)/shard_map/ppermute | solution.py:277
  143.7 2.5 %collective-permute-start.19 = (f32[128,128]{1,0:T(8,128)S(1)}, f32[128,128]{1,0:T(8,128)S(1)}, u32[]{:S(2)}, u32[]{:S(2)}) collective-permute-start(f32[128,128]{1,0:T(8,128)S(1)} %join_y.1.a), channel_id=1, source_target_pairs={{0,2},{2,4},{4,6},{6,0},{8,10},{10,12},{12,14},{14,8},{16,18},{18,... | collective-permute-start | bytes 196616 | tf_op jit(solution)/shard_map/ppermute | solution.py:277
  146.2 1.9 %copy.19 = f32[32,128,128]{2,1,0:T(8,128)S(1)} copy(f32[32,128,128]{1,2,0:T(8,128)} %bitcast.23) | data formatting | bytes 4194304 | tf_op jit(solution)/shard_map/transpose | solution.py:386
  152.2 8.4 %scatter_rows.1 = bf16[4096,128]{1,0:T(8,128)(2,1)} custom-call(s32[128,32]{1,0:T(8,128)S(1)} %copy.20.rows, bf16[4096,128]{1,0:T(8,128)(2,1)S(1)} %bitcast.18, f32[4096,128]{1,0:T(8,128)S(1)} %bitcast.17), custom_call_target="tpu_custom_call" | custom-call | tf_op jit(solution)/shard_map/scatter_rows/pallas_call | solution.py:243
  (71 shorter events, 25.8 us)
Async XLA Ops:
  9.4 44.7 %all-to-all-start = ((bf16[128,32,128]{2,1,0:T(8,128)(2,1)}), bf16[128,32,128]{2,1,0:T(8,128)(2,1)S(1)}, u32[]{:S(2)}, u32[]{:S(2)}) async-start(bf16[128,32,128]{2,1,0:T(8,128)(2,1)} %bitcast.5), calls=%async_computation | async-start | bytes 2097152 | tf_op jit(solution)/shard_map/all_to_all | solution.py:354
  62.6 3.0 %collective-permute-start = (bf16[4096,128]{1,0:T(8,128)(2,1)S(1)}, bf16[4096,128]{1,0:T(8,128)(2,1)S(1)}, u32[]{:S(2)}, u32[]{:S(2)}) collective-permute-start(bf16[4096,128]{1,0:T(8,128)(2,1)S(1)} %bitcast.19), channel_id=1, source_target_pairs={{0,1},{1,0},{2,3},{3,2},{4,5},{5,4},{6,7},{7,6},{8,9},{9,8},{10,11... | collective-permute-start | bytes 3145736 | tf_op jit(solution)/shard_map/ppermute | solution.py:379
  62.7 2.7 %collective-permute-start.2 = (bf16[128,172]{0,1:T(8,128)(2,1)S(1)}, bf16[128,172]{0,1:T(8,128)(2,1)S(1)}, u32[]{:S(2)}, u32[]{:S(2)}) collective-permute-start(bf16[128,172]{0,1:T(8,128)(2,1)S(1)} %copy-done.8), channel_id=1, source_target_pairs={{0,1},{1,0},{2,3},{3,2},{4,5},{5,4},{6,7},{7,6},{8,9},{9,8},{10,11... | collective-permute-start | bytes 132104 | tf_op jit(solution)/shard_map/ppermute | solution.py:363
  63.3 2.2 %collective-permute-start.1 = (bf16[128,256]{0,1:T(8,128)(2,1)S(1)}, bf16[128,256]{0,1:T(8,128)(2,1)S(1)}, u32[]{:S(2)}, u32[]{:S(2)}) collective-permute-start(bf16[128,256]{0,1:T(8,128)(2,1)S(1)} %copy.15), channel_id=1, source_target_pairs={{0,1},{1,0},{2,3},{3,2},{4,5},{5,4},{6,7},{7,6},{8,9},{9,8},{10,11... | collective-permute-start | bytes 196616 | tf_op jit(solution)/shard_map/ppermute | solution.py:362
  86.2 66.0 %all-to-all-start.1 = ((bf16[128,32,128]{2,1,0:T(8,128)(2,1)}), bf16[128,32,128]{2,1,0:T(8,128)(2,1)S(1)}, u32[]{:S(2)}, u32[]{:S(2)}) async-start(bf16[128,32,128]{2,1,0:T(8,128)(2,1)} %bitcast.10), calls=%async_computation.1 | async-start | bytes 2097152 | tf_op jit(solution)/shard_map/all_to_all | solution.py:385
  94.1 6.2 %collective-permute-start.3 = (f32[128,128]{1,0:T(8,128)S(1)}, f32[128,128]{1,0:T(8,128)S(1)}, u32[]{:S(2)}, u32[]{:S(2)}) collective-permute-start(f32[128,128]{1,0:T(8,128)S(1)} %get-tuple-element.28), channel_id=1, source_target_pairs={{0,2},{2,4},{4,6},{6,0},{8,10},{10,12},{12,14},{14,8},{16,18},{18,... | collective-permute-start | bytes 196616 | tf_op jit(solution)/shard_map/ppermute | solution.py:277
  95.6 8.0 %collective-permute-start.4 = (f32[128,128]{1,0:T(8,128)S(1)}, f32[128,128]{1,0:T(8,128)S(1)}, u32[]{:S(2)}, u32[]{:S(2)}) collective-permute-start(f32[128,128]{1,0:T(8,128)S(1)} %get-tuple-element.29), channel_id=1, source_target_pairs={{0,4},{2,6},{4,0},{6,2},{8,12},{10,14},{12,8},{14,10},{16,20},{18,... | collective-permute-start | bytes 196616 | tf_op jit(solution)/shard_map/ppermute | solution.py:277
  97.1 7.7 %collective-permute-start.5 = (f32[128,128]{1,0:T(8,128)S(1)}, f32[128,128]{1,0:T(8,128)S(1)}, u32[]{:S(2)}, u32[]{:S(2)}) collective-permute-start(f32[128,128]{1,0:T(8,128)S(1)} %get-tuple-element.30), channel_id=1, source_target_pairs={{0,6},{2,0},{4,2},{6,4},{8,14},{10,8},{12,10},{14,12},{16,22},{18,... | collective-permute-start | bytes 196616 | tf_op jit(solution)/shard_map/ppermute | solution.py:277
  105.4 5.2 %collective-permute-start.6 = (f32[32,128]{1,0:T(8,128)S(1)}, f32[32,128]{1,0:T(8,128)S(1)}, u32[]{:S(2)}, u32[]{:S(2)}) collective-permute-start(f32[32,128]{1,0:T(8,128)S(1)} %get-tuple-element.32), channel_id=1, source_target_pairs={{0,64},{2,66},{4,68},{6,70},{8,72},{10,74},{12,76},{14,78},{16,80}... | collective-permute-start | bytes 49160 | tf_op jit(solution)/shard_map/ppermute | solution.py:277
  105.9 5.4 %collective-permute-start.7 = (f32[32,128]{1,0:T(8,128)S(1)}, f32[32,128]{1,0:T(8,128)S(1)}, u32[]{:S(2)}, u32[]{:S(2)}) collective-permute-start(f32[32,128]{1,0:T(8,128)S(1)} %get-tuple-element.33), channel_id=1, source_target_pairs={{0,128},{2,130},{4,132},{6,134},{8,136},{10,138},{12,140},{14,142}... | collective-permute-start | bytes 49160 | tf_op jit(solution)/shard_map/ppermute | solution.py:277
  109.0 3.8 %collective-permute-start.8 = (f32[32,128]{1,0:T(8,128)S(1)}, f32[32,128]{1,0:T(8,128)S(1)}, u32[]{:S(2)}, u32[]{:S(2)}) collective-permute-start(f32[32,128]{1,0:T(8,128)S(1)} %get-tuple-element.34), channel_id=1, source_target_pairs={{0,192},{2,194},{4,196},{6,198},{8,200},{10,202},{12,204},{14,206}... | collective-permute-start | bytes 49160 | tf_op jit(solution)/shard_map/ppermute | solution.py:277
  112.9 10.9 %collective-permute-start.15 = (f32[32,128]{1,0:T(8,128)S(1)}, f32[32,128]{1,0:T(8,128)S(1)}, u32[]{:S(2)}, u32[]{:S(2)}) collective-permute-start(f32[32,128]{1,0:T(8,128)S(1)} %add_add_fusion.refs_0_), channel_id=1, source_target_pairs={{0,56},{2,58},{4,60},{6,62},{8,0},{10,2},{12,4},{14,6},{16,8},{18,... | collective-permute-start | bytes 49160 | tf_op jit(solution)/shard_map/ppermute | solution.py:277
  116.0 10.5 %collective-permute-start.14 = (f32[32,128]{1,0:T(8,128)S(1)}, f32[32,128]{1,0:T(8,128)S(1)}, u32[]{:S(2)}, u32[]{:S(2)}) collective-permute-start(f32[32,128]{1,0:T(8,128)S(1)} %add_add_fusion.refs_0_), channel_id=1, source_target_pairs={{0,48},{2,50},{4,52},{6,54},{8,56},{10,58},{12,60},{14,62},{16,0},... | collective-permute-start | bytes 49160 | tf_op jit(solution)/shard_map/ppermute | solution.py:277
  117.6 10.9 %collective-permute-start.13 = (f32[32,128]{1,0:T(8,128)S(1)}, f32[32,128]{1,0:T(8,128)S(1)}, u32[]{:S(2)}, u32[]{:S(2)}) collective-permute-start(f32[32,128]{1,0:T(8,128)S(1)} %add_add_fusion.refs_0_), channel_id=1, source_target_pairs={{0,40},{2,42},{4,44},{6,46},{8,48},{10,50},{12,52},{14,54},{16,56}... | collective-permute-start | bytes 49160 | tf_op jit(solution)/shard_map/ppermute | solution.py:277
  119.0 9.4 %collective-permute-start.12 = (f32[32,128]{1,0:T(8,128)S(1)}, f32[32,128]{1,0:T(8,128)S(1)}, u32[]{:S(2)}, u32[]{:S(2)}) collective-permute-start(f32[32,128]{1,0:T(8,128)S(1)} %add_add_fusion.refs_0_), channel_id=1, source_target_pairs={{0,32},{2,34},{4,36},{6,38},{8,40},{10,42},{12,44},{14,46},{16,48}... | collective-permute-start | bytes 49160 | tf_op jit(solution)/shard_map/ppermute | solution.py:277
  123.8 6.7 %collective-permute-start.11 = (f32[32,128]{1,0:T(8,128)S(1)}, f32[32,128]{1,0:T(8,128)S(1)}, u32[]{:S(2)}, u32[]{:S(2)}) collective-permute-start(f32[32,128]{1,0:T(8,128)S(1)} %add_add_fusion.refs_0_), channel_id=1, source_target_pairs={{0,24},{2,26},{4,28},{6,30},{8,32},{10,34},{12,36},{14,38},{16,40}... | collective-permute-start | bytes 49160 | tf_op jit(solution)/shard_map/ppermute | solution.py:277
  123.8 6.7 %collective-permute-start.10 = (f32[32,128]{1,0:T(8,128)S(1)}, f32[32,128]{1,0:T(8,128)S(1)}, u32[]{:S(2)}, u32[]{:S(2)}) collective-permute-start(f32[32,128]{1,0:T(8,128)S(1)} %add_add_fusion.refs_0_), channel_id=1, source_target_pairs={{0,16},{2,18},{4,20},{6,22},{8,24},{10,26},{12,28},{14,30},{16,32}... | collective-permute-start | bytes 49160 | tf_op jit(solution)/shard_map/ppermute | solution.py:277
  126.5 5.0 %collective-permute-start.9 = (f32[32,128]{1,0:T(8,128)S(1)}, f32[32,128]{1,0:T(8,128)S(1)}, u32[]{:S(2)}, u32[]{:S(2)}) collective-permute-start(f32[32,128]{1,0:T(8,128)S(1)} %add_add_fusion.refs_0_), channel_id=1, source_target_pairs={{0,8},{2,10},{4,12},{6,14},{8,16},{10,18},{12,20},{14,22},{16,24},... | collective-permute-start | bytes 49160 | tf_op jit(solution)/shard_map/ppermute | solution.py:277
  132.0 4.1 %collective-permute-start.18 = (f32[32,128]{1,0:T(8,128)S(1)}, f32[32,128]{1,0:T(8,128)S(1)}, u32[]{:S(2)}, u32[]{:S(2)}) collective-permute-start(f32[32,128]{1,0:T(8,128)S(1)} %sum_z.1.a), channel_id=1, source_target_pairs={{0,192},{2,194},{4,196},{6,198},{8,200},{10,202},{12,204},{14,206}... | collective-permute-start | bytes 49160 | tf_op jit(solution)/shard_map/ppermute | solution.py:277
  134.7 5.2 %collective-permute-start.17 = (f32[32,128]{1,0:T(8,128)S(1)}, f32[32,128]{1,0:T(8,128)S(1)}, u32[]{:S(2)}, u32[]{:S(2)}) collective-permute-start(f32[32,128]{1,0:T(8,128)S(1)} %sum_z.1.a), channel_id=1, source_target_pairs={{0,128},{2,130},{4,132},{6,134},{8,136},{10,138},{12,140},{14,142}... | collective-permute-start | bytes 49160 | tf_op jit(solution)/shard_map/ppermute | solution.py:277
  134.7 5.2 %collective-permute-start.16 = (f32[32,128]{1,0:T(8,128)S(1)}, f32[32,128]{1,0:T(8,128)S(1)}, u32[]{:S(2)}, u32[]{:S(2)}) collective-permute-start(f32[32,128]{1,0:T(8,128)S(1)} %sum_z.1.a), channel_id=1, source_target_pairs={{0,64},{2,66},{4,68},{6,70},{8,72},{10,74},{12,76},{14,78},{16,80}... | collective-permute-start | bytes 49160 | tf_op jit(solution)/shard_map/ppermute | solution.py:277
  140.5 7.6 %collective-permute-start.21 = (f32[128,128]{1,0:T(8,128)S(1)}, f32[128,128]{1,0:T(8,128)S(1)}, u32[]{:S(2)}, u32[]{:S(2)}) collective-permute-start(f32[128,128]{1,0:T(8,128)S(1)} %join_y.1.a), channel_id=1, source_target_pairs={{0,6},{2,0},{4,2},{6,4},{8,14},{10,8},{12,10},{14,12},{16,22},{18,... | collective-permute-start | bytes 196616 | tf_op jit(solution)/shard_map/ppermute | solution.py:277
  142.2 5.9 %collective-permute-start.20 = (f32[128,128]{1,0:T(8,128)S(1)}, f32[128,128]{1,0:T(8,128)S(1)}, u32[]{:S(2)}, u32[]{:S(2)}) collective-permute-start(f32[128,128]{1,0:T(8,128)S(1)} %join_y.1.a), channel_id=1, source_target_pairs={{0,4},{2,6},{4,0},{6,2},{8,12},{10,14},{12,8},{14,10},{16,20},{18,... | collective-permute-start | bytes 196616 | tf_op jit(solution)/shard_map/ppermute | solution.py:277
  143.7 4.5 %collective-permute-start.19 = (f32[128,128]{1,0:T(8,128)S(1)}, f32[128,128]{1,0:T(8,128)S(1)}, u32[]{:S(2)}, u32[]{:S(2)}) collective-permute-start(f32[128,128]{1,0:T(8,128)S(1)} %join_y.1.a), channel_id=1, source_target_pairs={{0,2},{2,4},{4,6},{6,0},{8,10},{10,12},{12,14},{14,8},{16,18},{18,... | collective-permute-start | bytes 196616 | tf_op jit(solution)/shard_map/ppermute | solution.py:277
  (12 other events, 109.4 us)

commit v2 on v1

--- a/solution.py
+++ b/solution.py
@@ -12,7 +12,7 @@
 SMEM = pl.BlockSpec(memory_space=pltpu.SMEM)
 ANY = pl.BlockSpec(memory_space=pl.ANY)
 NX, NY, NZ = 4, 4, 8
-LINE = 128
+PACKED = 512
 SPAN = 512
 
 
@@ -100,8 +100,8 @@
 
 def backward_kernel(
     classes, total_nodes, ids, cols, agg, other, weight_t, weight, cls, cls_t, bias, labels, adj,
-    halo_out, own_out, share0, share1, share2, share3,
-    ext_grad, tiles, packed, sum_w, sum_c, sum_b, sems, own_sem,
+    halo_out, own_out, packed,
+    ext_grad, tiles, sum_w, sum_c, sum_b, sems, own_sem,
 ):
     blocks, nonzero = cols.shape
     tile = adj.shape[1]
@@ -174,9 +174,6 @@
     packed[pl.ds(units + class_rows + 8, 8), :] = sum_b[:, half:] * scale
     rest = units + class_rows + 16
     packed[pl.ds(rest, packed.shape[0] - rest), :] = jnp.zeros((packed.shape[0] - rest, half), F32)
-    for d, target in enumerate((share0, share1, share2, share3)):
-        start = pl.multiple_of(lax.rem(ids[1] + d, NX) * LINE, LINE)
-        target[...] = packed[pl.ds(start, LINE), :]
     own_copy.wait()
 
 
@@ -191,19 +188,18 @@
     def body(*refs):
         backward_kernel(classes, total_nodes, *refs)
 
-    share = jax.ShapeDtypeStruct((LINE, half), F32)
     return pl.pallas_call(
         body,
         out_shape=(
             jax.ShapeDtypeStruct((blocks, tile, half), BF16),
             jax.ShapeDtypeStruct((blocks, half, tile), F32),
-        ) + (share,) * NX,
+            jax.ShapeDtypeStruct((PACKED, half), F32),
+        ),
         in_specs=[SMEM, SMEM] + [VMEM] * 8 + [ANY],
-        out_specs=(VMEM, ANY) + (VMEM,) * NX,
+        out_specs=(VMEM, ANY, VMEM),
         scratch_shapes=[
             pltpu.VMEM((ext_blocks, half, tile), F32),
             pltpu.VMEM(adj.shape, BF16),
-            pltpu.VMEM((NX * LINE, half), F32),
             pltpu.VMEM((2 * half, half), F32),
             pltpu.VMEM((class_rows, half), F32),
             pltpu.VMEM((8, 2 * half), F32),
@@ -252,92 +248,81 @@
     )(send_rows, arrived, own)
 
 
-def small_call(body, outs, ids, arrays, scratch, name):
-    return pl.pallas_call(
-        body,
-        out_shape=outs,
-        in_specs=[SMEM] + [VMEM] * len(arrays),
-        out_specs=jax.tree.map(lambda _: VMEM, outs),
-        scratch_shapes=[pltpu.VMEM(scratch, F32)],
-        compiler_params=pltpu.CompilerParams(vmem_limit_bytes=4 * MIB),
-        name=name,
-    )(ids, *arrays)
-
-
-def shift(value, axis, step):
-    sizes = {"x": NX, "y": NY, "z": NZ}
+def move(value, axis, target):
     pairs = []
     for y in range(NY):
         for z in range(NZ):
             for x in range(NX):
                 place = {"x": x, "y": y, "z": z}
-                source = (y * NZ + z) * NX + x
-                place[axis] = (place[axis] + step) % sizes[axis]
-                pairs.append((source, (place["y"] * NZ + place["z"]) * NX + place["x"]))
+                place[axis] = target(place[axis])
+                pairs.append(
+                    ((y * NZ + z) * NX + x, (place["y"] * NZ + place["z"]) * NX + place["x"])
+                )
     return lax.ppermute(value, "dom", pairs)
 
 
-def sum_nodes(ids, shares, classes, half):
-    got = [shares[0]] + [shift(shares[d], "x", d) for d in range(1, NX)]
-    part = LINE // NY
-
-    def split_y(ids, a, b, c, d, o0, o1, o2, o3, total):
-        total[...] = (a[...] + b[...]) + (c[...] + d[...])
-        for k, target in enumerate((o0, o1, o2, o3)):
-            start = pl.multiple_of(lax.rem(ids[2] + k, NY) * part, part)
-            target[...] = total[pl.ds(start, part), :]
-
-    piece = jax.ShapeDtypeStruct((part, half), F32)
-    pieces = small_call(split_y, (piece,) * NY, ids, got, (LINE, half), "split_y")
-    got = [pieces[0]] + [shift(pieces[d], "y", d) for d in range(1, NY)]
-    mine = (got[0] + got[1]) + (got[2] + got[3])
-    got = [mine] + [shift(mine, "z", d) for d in range(1, NZ)]
-
-    def sum_z(ids, *refs):
-        out, slots = refs[NZ], refs[NZ + 1]
-        for d in range(NZ):
-            start = pl.multiple_of(lax.rem(ids[3] + NZ - d, NZ) * part, part)
-            slots[pl.ds(start, part), :] = refs[d][...]
-        total = slots[pl.ds(0, part), :]
-        for k in range(1, NZ):
-            total = total + slots[pl.ds(k * part, part), :]
-        out[...] = total
-
-    mine = small_call(sum_z, piece, ids, got, (NZ * part, half), "sum_z")
-    got = [mine] + [shift(mine, "y", d) for d in range(1, NY)]
-
-    def join_y(ids, a, b, c, d, out, unused):
-        for k, source in enumerate((a, b, c, d)):
-            start = pl.multiple_of(lax.rem(ids[2] + NY - k, NY) * part, part)
-            out[pl.ds(start, part), :] = source[...]
-
-    line = jax.ShapeDtypeStruct((LINE, half), F32)
-    mine = small_call(join_y, line, ids, got, (8, half), "join_y")
-    got = [mine] + [shift(mine, "x", d) for d in range(1, NX)]
-    units = 2 * half
-    class_rows = -(-classes // 8) * 8
-
-    def join_x(ids, a, b, c, d, out_w, out_c, out_b, packed):
-        for k, source in enumerate((a, b, c, d)):
-            start = pl.multiple_of(lax.rem(ids[1] + NX - k, NX) * LINE, LINE)
-            packed[pl.ds(start, LINE), :] = source[...]
+def ahead(value, axis, step, size):
+    return move(value, axis, lambda place: (place + step) % size)
+
+
+def across(value, axis, flip):
+    return move(value, axis, lambda place: place ^ flip)
+
+
+def add_pairs(values):
+    while len(values) > 1:
+        values = [a + b for a, b in zip(values[::2], values[1::2])]
+    return values[0]
+
+
+def swap_shares(packed):
+    groups = [
+        [(y * NZ + z) * NX + x for z in range(NZ)] for y in range(NY) for x in range(NX)
+    ]
+    shares = packed.reshape(NZ, -1, packed.shape[1])
+    return lax.all_to_all(
+        shares, "dom", split_axis=0, concat_axis=0, tiled=True, axis_index_groups=groups
+    )
+
+
+def sum_xy(mine):
+    for axis in ("x", "y"):
+        mine = add_pairs([mine] + [across(mine, axis, flip) for flip in (1, 2, 3)])
+    return mine
+
+
+def finish(ids, mine, grad_feats, classes, units):
+    part, half = mine.shape
+    got = [mine] + [ahead(mine, "z", d, NZ) for d in range(1, NZ)]
+    got, grad_feats = lax.optimization_barrier((got, grad_feats))
+    class_rows = -(-classes // 16) * 16
+
+    def body(ids, *refs):
+        shares, (out_w, out_c, out_b, packed) = refs[:NZ], refs[NZ:]
+        for d, share in enumerate(shares):
+            start = pl.multiple_of(lax.rem(ids[1] + NZ - d, NZ) * part, part)
+            packed[pl.ds(start, part), :] = share[...]
         for k in range(units // half):
             out_w[:, k * half : (k + 1) * half] = packed[pl.ds(k * half, half), :].T
-        out_c[:, :half] = packed[pl.ds(units, half), :].T
-        out_c[:, half:] = packed[pl.ds(units + half, half), :].T[:, : classes - half]
+        out_c[...] = packed[pl.ds(units, classes), :]
         for k in range(units // half):
             row = units + class_rows + 8 * k
-            out_b[:, k * half : (k + 1) * half] = packed[pl.ds(row, 8), :]
-
-    outs = (
-        jax.ShapeDtypeStruct((half, units), F32),
-        jax.ShapeDtypeStruct((half, classes), F32),
-        jax.ShapeDtypeStruct((8, units), F32),
-    )
-    grad_weight, grad_cls, grad_bias = small_call(
-        join_x, outs, ids, got, (NX * LINE, half), "join_x"
-    )
-    return grad_weight, grad_cls, grad_bias[0]
+            out_b[:, k * half : (k + 1) * half] = packed[pl.ds(row, 1), :]
+
+    grad_weight, grad_cls, grad_bias = pl.pallas_call(
+        body,
+        out_shape=(
+            jax.ShapeDtypeStruct((half, units), F32),
+            jax.ShapeDtypeStruct((classes, half), F32),
+            jax.ShapeDtypeStruct((1, units), F32),
+        ),
+        in_specs=[SMEM] + [VMEM] * NZ,
+        out_specs=(VMEM,) * 3,
+        scratch_shapes=[pltpu.VMEM((PACKED, half), F32)],
+        compiler_params=pltpu.CompilerParams(vmem_limit_bytes=4 * MIB),
+        name="finish",
+    )(ids, *got)
+    return grad_feats, grad_weight, grad_bias[0], grad_cls.T
 
 
 def on_device(feats, adj_tiles, adj_cols, send_rows, weight, bias, cls_w, labels):
@@ -358,7 +343,7 @@
     )
     hid = lax.axis_index("hid")
     dom = lax.axis_index("dom")
-    ids = jnp.stack([hid, dom % NX, dom // (NX * NZ), (dom // NX) % NZ]).astype(jnp.int32)
+    ids = jnp.stack([hid, (dom // NX) % NZ]).astype(jnp.int32)
     weight_o = lax.ppermute(weight_l, "hid", swap)
     cls_o = lax.ppermute(cls_l, "hid", swap)
     first = hid == 0
@@ -377,16 +362,17 @@
     agg = aggregate_blocks(adj_cols, feats.reshape(blocks, tile, half), halo, adj_tiles)
     agg = agg.reshape(row_count, half)
     other = lax.ppermute(agg, "hid", swap)
-    halo_grad, own_grad, *shares = backward(
+    halo_grad, own_grad, packed = backward(
         ids, adj_cols, agg, other, weight_full.T, weight_l, cls_full, cls_full.T, bias_wide,
         label_rows, adj_tiles, classes, total_nodes,
     )
+    shares = swap_shares(packed)
+    halo_grad, own_grad, shares = lax.optimization_barrier((halo_grad, own_grad, shares))
     returned = halo_grad.reshape(peers, cap, half)
     arrived = lax.all_to_all(returned, "dom", split_axis=0, concat_axis=0, tiled=True)
     own = jnp.swapaxes(own_grad, 1, 2).reshape(row_count, half)
-    grad_weight, grad_cls, grad_bias = sum_nodes(ids, shares, classes, half)
     grad_feats = scatter_rows(send_rows, arrived.reshape(row_count, half), own)
-    return (grad_feats, grad_weight, grad_bias, grad_cls)
+    return finish(ids, sum_xy(shares.sum(0)), grad_feats, classes, units)
 
 
 def solution(mesh):

time: 162 us -> 154 us (0.951)
  blocking collectives: 0 us -> 16 us
  starting transfers between devices: 58.6 us -> 47.1 us
  waiting for transfers between devices: 46.9 us -> 38.7 us
  local copies, waits for them, and re-layouts: 15.2 us -> 12.5 us
  Pallas kernels: 39 us -> 37.2 us
    all_to_all x0 -> x1, blocking collectives: none -> 16 us  [swap_shares(): lax.all_to_all(shares, 'dom', split_axis=0, concat_axis=0, tiled=True, ax...]
    ppermute x19 -> x13, starting transfers between devices: 34.5 us -> 24.3 us  [move(): return lax.ppermute(value, 'dom', pairs)]
    ppermute x19 -> x13, waiting for transfers between devices: 15.8 us -> 7.69 us  [move(): return lax.ppermute(value, 'dom', pairs)]
    unnamed x27 -> x22, local copies, waits for them, and re-layouts: 12.5 us -> 10.2 us
    pallas_call x4 -> x1, Pallas kernels: 3.02 us -> 1.33 us  [finish(): pl.pallas_call(body, out_shape=(jax.ShapeDtypeStruct((half, units), F32),...]
  transfers between devices with their start and end apart: 24 -> 18, of which waited for: 12 -> 6; matrix products, arithmetic and copies ran while one was open for 2% -> 2% of each run, Pallas kernels for 2% -> 6%
where the time goes in v2:
time: 154 us; the launch traced here: 153 us
  starting transfers between devices  47.1 us (31%)
  waiting for transfers between devices  38.7 us (25%)
  Pallas kernels  37.2 us (24%)
  blocking collectives  16 us (10%)
  local copies, waits for them, and re-layouts  12.5 us (8%)
    all_to_all x1, waiting for transfers between devices, on_device(): lax.all_to_all(outgoing, 'dom', split_axis=0, concat_axis=0, tiled=True)  29.2 us
    ppermute x13, starting transfers between devices, move(): return lax.ppermute(value, 'dom', pairs)  24.3 us
    all_to_all x1, blocking collectives, swap_shares(): lax.all_to_all(shares, 'dom', split_axis=0, concat_axis=0, tiled=True, ax...  16 us
    pallas_call x1, Pallas kernels, backward(): pl.pallas_call(body, out_shape=(jax.ShapeDtypeStruct((blocks, tile, half)...  15.7 us
    all_to_all x1, starting transfers between devices, on_device(): lax.all_to_all(outgoing, 'dom', split_axis=0, concat_axis=0, tiled=True)  15.4 us
    unnamed x22, local copies, waits for them, and re-layouts  10.2 us
    pallas_call x1, Pallas kernels, scatter_rows(): pl.pallas_call(scatter_kernel, out_shape=jax.ShapeDtypeStruct((count, wid...  8.45 us
    ppermute x13, waiting for transfers between devices, move(): return lax.ppermute(value, 'dom', pairs)  7.69 us
  transfers between devices with their start and end apart: 18, of which 6 were waited for; matrix products, arithmetic and copies ran while one was open for 2% of the time, Pallas kernels for 6%

profile of v2, /device:TPU:2, one launch (start us, length us, event | category | flops | bytes accessed | tf_op | source)
XLA Modules:
  0.0 152.6 jit_solution(17395143180612865738)
XLA Ops:
  2.7 6.7 %gather_rows.1 = bf16[4096,128]{1,0:T(8,128)(2,1)} custom-call(s32[128,32]{1,0:T(8,128)S(1)} %copy.12.rows, bf16[4096,128]{1,0:T(8,128)(2,1)S(1)} %copy-done.2), custom_call_target="tpu_custom_call" | custom-call | tf_op jit(solution)/shard_map/gather_rows/pallas_call | solution.py:42
  9.4 15.4 %all-to-all-start = ((bf16[128,32,128]{2,1,0:T(8,128)(2,1)}), bf16[128,32,128]{2,1,0:T(8,128)(2,1)S(1)}, u32[]{:S(2)}, u32[]{:S(2)}) async-start(bf16[128,32,128]{2,1,0:T(8,128)(2,1)} %bitcast.3), calls=%async_computation | async-start | bytes 2097152 | tf_op jit(solution)/shard_map/all_to_all | solution.py:339
  24.9 29.2 %all-to-all-done = bf16[128,32,128]{2,1,0:T(8,128)(2,1)S(1)} async-done(((bf16[128,32,128]{2,1,0:T(8,128)(2,1)}), bf16[128,32,128]{2,1,0:T(8,128)(2,1)S(1)}, u32[]{:S(2)}, u32[]{:S(2)}) %all-to-all-start) | async-done | bytes 1048608 | tf_op jit(solution)/shard_map/all_to_all | solution.py:339
  54.1 3.4 %copy-done = bf16[256,128,128]{2,1,0:T(8,128)(2,1)S(1)} copy-done((bf16[256,128,128]{2,1,0:T(8,128)(2,1)S(1)}, bf16[256,128,128]{2,1,0:T(8,128)(2,1)}, u32[]{:S(2)}) %copy-start) | copy-done | bytes 8388632
  57.5 5.0 %aggregate_blocks.1 = bf16[32,128,128]{2,1,0:T(8,128)(2,1)S(1)} custom-call(s32[32,8]{1,0:T(8,128)S(1)} %copy.17.cols.refs_1_, bf16[32,128,128]{2,1,0:T(8,128)(2,1)S(1)} %bitcast.21, bf16[32,128,128]{2,1,0:T(8,128)(2,1)S(1)} %bitcast.22, bf16[256,128,128]{2,1,0:T(8,128)(2,1)S(1)} %copy-done), custom_call_target="tpu_custom_call" | custom-call | tf_op jit(solution)/shard_map/aggregate_blocks/pallas_call | solution.py:86
  63.6 1.8 %collective-permute-done.2 = bf16[128,172]{0,1:T(8,128)(2,1)S(1)} collective-permute-done((bf16[128,172]{0,1:T(8,128)(2,1)S(1)}, bf16[128,172]{0,1:T(8,128)(2,1)S(1)}, u32[]{:S(2)}, u32[]{:S(2)}) %collective-permute-start.2) | collective-permute-done | bytes 44064 | tf_op jit(solution)/shard_map/ppermute | solution.py:348
  65.7 3.4 %copy-done.1 = bf16[256,128,128]{2,1,0:T(8,128)(2,1)S(1)} copy-done((bf16[256,128,128]{2,1,0:T(8,128)(2,1)S(1)}, bf16[256,128,128]{2,1,0:T(8,128)(2,1)}, u32[]{:S(2)}) %copy-start.1) | copy-done | bytes 8388632
  69.1 15.7 %backward.1 = (bf16[32,128,128]{2,1,0:T(8,128)(2,1)}, f32[32,128,128]{2,1,0:T(8,128)S(1)}, f32[512,128]{1,0:T(8,128)S(1)}) custom-call(s32[2]{0:T(128)S(1)} %pad_add_fusion.refs_0_.ids, s32[32,8]{1,0:T(8,128)S(1)} %copy.17.cols.refs_1_, bf16[4096,128]{1,0:T(8,128)(2,1)S(1)} %bitcast.20, bf16[4096,128]{1,0:T(8,128)(2,1)S(1)} %collective-permute-done.refs_3_, ...), custom_call_target="tpu_custom_call" | custom-call | tf_op jit(solution)/shard_map/backward/pallas_call | solution.py:191
  86.2 16.0 %all_to_all.15 = f32[8,64,128]{2,1,0:T(8,128)S(1)} all-to-all(f32[8,64,128]{2,1,0:T(8,128)S(1)} %bitcast.24), channel_id=1, replica_groups={{0,8,16,24,32,40,48,56},{2,10,18,26,34,42,50,58},{4,12,20,28,36,44,52,6..., dimensions={0} | all-to-all | bytes 524288 | tf_op jit(solution)/shard_map/all_to_all | solution.py:283
  102.2 6.6 %all-to-all-start.2 = ((bf16[128,32,128]{2,1,0:T(8,128)(2,1)}), bf16[128,32,128]{2,1,0:T(8,128)(2,1)S(1)}, u32[]{:S(2)}, u32[]{:S(2)}) async-start(bf16[128,32,128]{2,1,0:T(8,128)(2,1)} %bitcast.9), calls=%async_computation.2 | async-start | bytes 2097152 | tf_op jit(solution)/shard_map/all_to_all | solution.py:372
  108.8 1.6 %collective-permute-start.5 = (f32[64,128]{1,0:T(8,128)S(1)}, f32[64,128]{1,0:T(8,128)S(1)}, u32[]{:S(2)}, u32[]{:S(2)}) collective-permute-start(f32[64,128]{1,0:T(8,128)S(1)} %reduce_sum.9), channel_id=1, source_target_pairs={{0,6},{2,4},{4,2},{6,0},{8,14},{10,12},{12,10},{14,8},{16,22},{18,... | collective-permute-start | bytes 98312 | tf_op jit(solution)/shard_map/ppermute | solution.py:261
  110.4 1.6 %collective-permute-start.4 = (f32[64,128]{1,0:T(8,128)S(1)}, f32[64,128]{1,0:T(8,128)S(1)}, u32[]{:S(2)}, u32[]{:S(2)}) collective-permute-start(f32[64,128]{1,0:T(8,128)S(1)} %reduce_sum.9), channel_id=1, source_target_pairs={{0,4},{2,6},{4,0},{6,2},{8,12},{10,14},{12,8},{14,10},{16,20},{18,... | collective-permute-start | bytes 98312 | tf_op jit(solution)/shard_map/ppermute | solution.py:261
  113.0 2.9 %collective-permute-done.4 = f32[64,128]{1,0:T(8,128)S(1)} collective-permute-done((f32[64,128]{1,0:T(8,128)S(1)}, f32[64,128]{1,0:T(8,128)S(1)}, u32[]{:S(2)}, u32[]{:S(2)}) %collective-permute-start.4) | collective-permute-done | bytes 32800 | tf_op jit(solution)/shard_map/ppermute | solution.py:261
  116.1 3.2 %collective-permute-start.8 = (f32[64,128]{1,0:T(8,128)S(1)}, f32[64,128]{1,0:T(8,128)S(1)}, u32[]{:S(2)}, u32[]{:S(2)}) collective-permute-start(f32[64,128]{1,0:T(8,128)S(1)} %add_add_fusion.1), channel_id=1, source_target_pairs={{0,192},{2,194},{4,196},{6,198},{8,200},{10,202},{12,204},{14,206}... | collective-permute-start | bytes 98312 | tf_op jit(solution)/shard_map/ppermute | solution.py:261
  120.3 1.7 %collective-permute-done.8 = f32[64,128]{1,0:T(8,128)S(1)} collective-permute-done((f32[64,128]{1,0:T(8,128)S(1)}, f32[64,128]{1,0:T(8,128)S(1)}, u32[]{:S(2)}, u32[]{:S(2)}) %collective-permute-start.8) | collective-permute-done | bytes 32800 | tf_op jit(solution)/shard_map/ppermute | solution.py:261
  122.0 2.9 %collective-permute-done.7 = f32[64,128]{1,0:T(8,128)S(1)} collective-permute-done((f32[64,128]{1,0:T(8,128)S(1)}, f32[64,128]{1,0:T(8,128)S(1)}, u32[]{:S(2)}, u32[]{:S(2)}) %collective-permute-start.7) | collective-permute-done | bytes 32800 | tf_op jit(solution)/shard_map/ppermute | solution.py:261
  124.9 3.7 %collective-permute-start.15 = (f32[64,128]{1,0:T(8,128)S(1)}, f32[64,128]{1,0:T(8,128)S(1)}, u32[]{:S(2)}, u32[]{:S(2)}) collective-permute-start(f32[64,128]{1,0:T(8,128)S(1)} %add_add_fusion.refs_0_), channel_id=1, source_target_pairs={{0,56},{2,58},{4,60},{6,62},{8,0},{10,2},{12,4},{14,6},{16,8},{18,... | collective-permute-start | bytes 98312 | tf_op jit(solution)/shard_map/ppermute | solution.py:261
  128.6 2.0 %collective-permute-start.14 = (f32[64,128]{1,0:T(8,128)S(1)}, f32[64,128]{1,0:T(8,128)S(1)}, u32[]{:S(2)}, u32[]{:S(2)}) collective-permute-start(f32[64,128]{1,0:T(8,128)S(1)} %add_add_fusion.refs_0_), channel_id=1, source_target_pairs={{0,48},{2,50},{4,52},{6,54},{8,56},{10,58},{12,60},{14,62},{16,0},... | collective-permute-start | bytes 98312 | tf_op jit(solution)/shard_map/ppermute | solution.py:261
  130.7 1.7 %collective-permute-start.13 = (f32[64,128]{1,0:T(8,128)S(1)}, f32[64,128]{1,0:T(8,128)S(1)}, u32[]{:S(2)}, u32[]{:S(2)}) collective-permute-start(f32[64,128]{1,0:T(8,128)S(1)} %add_add_fusion.refs_0_), channel_id=1, source_target_pairs={{0,40},{2,42},{4,44},{6,46},{8,48},{10,50},{12,52},{14,54},{16,56}... | collective-permute-start | bytes 98312 | tf_op jit(solution)/shard_map/ppermute | solution.py:261
  132.4 3.5 %collective-permute-start.12 = (f32[64,128]{1,0:T(8,128)S(1)}, f32[64,128]{1,0:T(8,128)S(1)}, u32[]{:S(2)}, u32[]{:S(2)}) collective-permute-start(f32[64,128]{1,0:T(8,128)S(1)} %add_add_fusion.refs_0_), channel_id=1, source_target_pairs={{0,32},{2,34},{4,36},{6,38},{8,40},{10,42},{12,44},{14,46},{16,48}... | collective-permute-start | bytes 98312 | tf_op jit(solution)/shard_map/ppermute | solution.py:261
  135.9 3.5 %collective-permute-start.10 = (f32[64,128]{1,0:T(8,128)S(1)}, f32[64,128]{1,0:T(8,128)S(1)}, u32[]{:S(2)}, u32[]{:S(2)}) collective-permute-start(f32[64,128]{1,0:T(8,128)S(1)} %add_add_fusion.refs_0_), channel_id=1, source_target_pairs={{0,16},{2,18},{4,20},{6,22},{8,24},{10,26},{12,28},{14,30},{16,32}... | collective-permute-start | bytes 98312 | tf_op jit(solution)/shard_map/ppermute | solution.py:261
  139.5 1.4 collective-permute-start.9
  140.8 1.9 %copy.19 = f32[32,128,128]{2,1,0:T(8,128)S(1)} copy(f32[32,128,128]{1,2,0:T(8,128)} %bitcast.23) | data formatting | bytes 4194304 | tf_op jit(solution)/shard_map/transpose | solution.py:373
  142.8 8.5 %scatter_rows.1 = bf16[4096,128]{1,0:T(8,128)(2,1)} custom-call(s32[128,32]{1,0:T(8,128)S(1)} %copy.12.rows, bf16[4096,128]{1,0:T(8,128)(2,1)S(1)} %bitcast.18, f32[4096,128]{1,0:T(8,128)S(1)} %bitcast.17), custom_call_target="tpu_custom_call" | custom-call | tf_op jit(solution)/shard_map/scatter_rows/pallas_call | solution.py:239
  (53 shorter events, 8.4 us)
Async XLA Ops:
  2.7 22.2 %copy-start.8 = (s32[32,8]{0,1:T(8,128)S(1)}, s32[32,8]{0,1:T(8,128)}, u32[]{:S(2)}) copy-start(s32[32,8]{0,1:T(8,128)} %param.10) | copy-start | bytes 3076
  2.7 51.5 %copy-start.3 = (bf16[4096,128]{1,0:T(8,128)(2,1)S(1)}, bf16[4096,128]{1,0:T(8,128)(2,1)}, u32[]{:S(2)}) copy-start(bf16[4096,128]{1,0:T(8,128)(2,1)} %feats.1) | copy-start | bytes 3145732
  9.4 44.7 %all-to-all-start = ((bf16[128,32,128]{2,1,0:T(8,128)(2,1)}), bf16[128,32,128]{2,1,0:T(8,128)(2,1)S(1)}, u32[]{:S(2)}, u32[]{:S(2)}) async-start(bf16[128,32,128]{2,1,0:T(8,128)(2,1)} %bitcast.3), calls=%async_computation | async-start | bytes 2097152 | tf_op jit(solution)/shard_map/all_to_all | solution.py:339
  57.5 5.2 %copy-start.6 = (bf16[128,172]{0,1:T(8,128)(2,1)S(1)}, bf16[128,172]{0,1:T(8,128)(2,1)}, u32[]{:S(2)}) copy-start(bf16[128,172]{0,1:T(8,128)(2,1)} %param.14) | copy-start | bytes 132100
  57.5 5.7 %copy-start.5 = (bf16[128,256]{1,0:T(8,128)(2,1)S(1)}, bf16[128,256]{1,0:T(8,128)(2,1)}, u32[]{:S(2)}) copy-start(bf16[128,256]{1,0:T(8,128)(2,1)} %refs_5_) | copy-start | bytes 196612
  57.5 6.0 %copy-start.7 = (s32[4096]{0:T(1024)S(1)}, s32[4096]{0:T(1024)}, u32[]{:S(2)}) copy-start(s32[4096]{0:T(1024)} %param.15) | copy-start | bytes 49156
  57.5 8.1 %copy-start.9 = (f32[256]{0:T(256)S(1)}, f32[256]{0:T(256)}, u32[]{:S(2)}) copy-start(f32[256]{0:T(256)} %param.13) | copy-start | bytes 3076
  62.6 3.0 %collective-permute-start = (bf16[4096,128]{1,0:T(8,128)(2,1)S(1)}, bf16[4096,128]{1,0:T(8,128)(2,1)S(1)}, u32[]{:S(2)}, u32[]{:S(2)}) collective-permute-start(bf16[4096,128]{1,0:T(8,128)(2,1)S(1)} %bitcast.19), channel_id=1, source_target_pairs={{0,1},{1,0},{2,3},{3,2},{4,5},{5,4},{6,7},{7,6},{8,9},{9,8},{10,11... | collective-permute-start | bytes 3145736 | tf_op jit(solution)/shard_map/ppermute | solution.py:364
  62.7 2.7 %collective-permute-start.2 = (bf16[128,172]{0,1:T(8,128)(2,1)S(1)}, bf16[128,172]{0,1:T(8,128)(2,1)S(1)}, u32[]{:S(2)}, u32[]{:S(2)}) collective-permute-start(bf16[128,172]{0,1:T(8,128)(2,1)S(1)} %copy-done.6), channel_id=1, source_target_pairs={{0,1},{1,0},{2,3},{3,2},{4,5},{5,4},{6,7},{7,6},{8,9},{9,8},{10,11... | collective-permute-start | bytes 132104 | tf_op jit(solution)/shard_map/ppermute | solution.py:348
  63.3 2.2 %collective-permute-start.1 = (bf16[128,256]{0,1:T(8,128)(2,1)S(1)}, bf16[128,256]{0,1:T(8,128)(2,1)S(1)}, u32[]{:S(2)}, u32[]{:S(2)}) collective-permute-start(bf16[128,256]{0,1:T(8,128)(2,1)S(1)} %copy.15), channel_id=1, source_target_pairs={{0,1},{1,0},{2,3},{3,2},{4,5},{5,4},{6,7},{7,6},{8,9},{9,8},{10,11... | collective-permute-start | bytes 196616 | tf_op jit(solution)/shard_map/ppermute | solution.py:347
  102.2 40.6 %all-to-all-start.2 = ((bf16[128,32,128]{2,1,0:T(8,128)(2,1)}), bf16[128,32,128]{2,1,0:T(8,128)(2,1)S(1)}, u32[]{:S(2)}, u32[]{:S(2)}) async-start(bf16[128,32,128]{2,1,0:T(8,128)(2,1)} %bitcast.9), calls=%async_computation.2 | async-start | bytes 2097152 | tf_op jit(solution)/shard_map/all_to_all | solution.py:372
  108.8 4.2 %collective-permute-start.5 = (f32[64,128]{1,0:T(8,128)S(1)}, f32[64,128]{1,0:T(8,128)S(1)}, u32[]{:S(2)}, u32[]{:S(2)}) collective-permute-start(f32[64,128]{1,0:T(8,128)S(1)} %reduce_sum.9), channel_id=1, source_target_pairs={{0,6},{2,4},{4,2},{6,0},{8,14},{10,12},{12,10},{14,8},{16,22},{18,... | collective-permute-start | bytes 98312 | tf_op jit(solution)/shard_map/ppermute | solution.py:261
  110.4 5.5 %collective-permute-start.4 = (f32[64,128]{1,0:T(8,128)S(1)}, f32[64,128]{1,0:T(8,128)S(1)}, u32[]{:S(2)}, u32[]{:S(2)}) collective-permute-start(f32[64,128]{1,0:T(8,128)S(1)} %reduce_sum.9), channel_id=1, source_target_pairs={{0,4},{2,6},{4,0},{6,2},{8,12},{10,14},{12,8},{14,10},{16,20},{18,... | collective-permute-start | bytes 98312 | tf_op jit(solution)/shard_map/ppermute | solution.py:261
  112.0 4.1 %collective-permute-start.3 = (f32[64,128]{1,0:T(8,128)S(1)}, f32[64,128]{1,0:T(8,128)S(1)}, u32[]{:S(2)}, u32[]{:S(2)}) collective-permute-start(f32[64,128]{1,0:T(8,128)S(1)} %reduce_sum.9), channel_id=1, source_target_pairs={{0,2},{2,0},{4,6},{6,4},{8,10},{10,8},{12,14},{14,12},{16,18},{18,... | collective-permute-start | bytes 98312 | tf_op jit(solution)/shard_map/ppermute | solution.py:261
  116.1 5.9 %collective-permute-start.8 = (f32[64,128]{1,0:T(8,128)S(1)}, f32[64,128]{1,0:T(8,128)S(1)}, u32[]{:S(2)}, u32[]{:S(2)}) collective-permute-start(f32[64,128]{1,0:T(8,128)S(1)} %add_add_fusion.1), channel_id=1, source_target_pairs={{0,192},{2,194},{4,196},{6,198},{8,200},{10,202},{12,204},{14,206}... | collective-permute-start | bytes 98312 | tf_op jit(solution)/shard_map/ppermute | solution.py:261
  119.3 5.6 %collective-permute-start.7 = (f32[64,128]{1,0:T(8,128)S(1)}, f32[64,128]{1,0:T(8,128)S(1)}, u32[]{:S(2)}, u32[]{:S(2)}) collective-permute-start(f32[64,128]{1,0:T(8,128)S(1)} %add_add_fusion.1), channel_id=1, source_target_pairs={{0,128},{2,130},{4,132},{6,134},{8,136},{10,138},{12,140},{14,142}... | collective-permute-start | bytes 98312 | tf_op jit(solution)/shard_map/ppermute | solution.py:261
  119.7 5.2 %collective-permute-start.6 = (f32[64,128]{1,0:T(8,128)S(1)}, f32[64,128]{1,0:T(8,128)S(1)}, u32[]{:S(2)}, u32[]{:S(2)}) collective-permute-start(f32[64,128]{1,0:T(8,128)S(1)} %add_add_fusion.1), channel_id=1, source_target_pairs={{0,64},{2,66},{4,68},{6,70},{8,72},{10,74},{12,76},{14,78},{16,80}... | collective-permute-start | bytes 98312 | tf_op jit(solution)/shard_map/ppermute | solution.py:261
  124.9 11.0 %collective-permute-start.15 = (f32[64,128]{1,0:T(8,128)S(1)}, f32[64,128]{1,0:T(8,128)S(1)}, u32[]{:S(2)}, u32[]{:S(2)}) collective-permute-start(f32[64,128]{1,0:T(8,128)S(1)} %add_add_fusion.refs_0_), channel_id=1, source_target_pairs={{0,56},{2,58},{4,60},{6,62},{8,0},{10,2},{12,4},{14,6},{16,8},{18,... | collective-permute-start | bytes 98312 | tf_op jit(solution)/shard_map/ppermute | solution.py:261
  128.6 10.8 %collective-permute-start.14 = (f32[64,128]{1,0:T(8,128)S(1)}, f32[64,128]{1,0:T(8,128)S(1)}, u32[]{:S(2)}, u32[]{:S(2)}) collective-permute-start(f32[64,128]{1,0:T(8,128)S(1)} %add_add_fusion.refs_0_), channel_id=1, source_target_pairs={{0,48},{2,50},{4,52},{6,54},{8,56},{10,58},{12,60},{14,62},{16,0},... | collective-permute-start | bytes 98312 | tf_op jit(solution)/shard_map/ppermute | solution.py:261
  130.7 20.5 %collective-permute-start.13 = (f32[64,128]{1,0:T(8,128)S(1)}, f32[64,128]{1,0:T(8,128)S(1)}, u32[]{:S(2)}, u32[]{:S(2)}) collective-permute-start(f32[64,128]{1,0:T(8,128)S(1)} %add_add_fusion.refs_0_), channel_id=1, source_target_pairs={{0,40},{2,42},{4,44},{6,46},{8,48},{10,50},{12,52},{14,54},{16,56}... | collective-permute-start | bytes 98312 | tf_op jit(solution)/shard_map/ppermute | solution.py:261
  132.4 18.9 %collective-permute-start.12 = (f32[64,128]{1,0:T(8,128)S(1)}, f32[64,128]{1,0:T(8,128)S(1)}, u32[]{:S(2)}, u32[]{:S(2)}) collective-permute-start(f32[64,128]{1,0:T(8,128)S(1)} %add_add_fusion.refs_0_), channel_id=1, source_target_pairs={{0,32},{2,34},{4,36},{6,38},{8,40},{10,42},{12,44},{14,46},{16,48}... | collective-permute-start | bytes 98312 | tf_op jit(solution)/shard_map/ppermute | solution.py:261
  135.8 15.4 %collective-permute-start.11 = (f32[64,128]{1,0:T(8,128)S(1)}, f32[64,128]{1,0:T(8,128)S(1)}, u32[]{:S(2)}, u32[]{:S(2)}) collective-permute-start(f32[64,128]{1,0:T(8,128)S(1)} %add_add_fusion.refs_0_), channel_id=1, source_target_pairs={{0,24},{2,26},{4,28},{6,30},{8,32},{10,34},{12,36},{14,38},{16,40}... | collective-permute-start | bytes 98312 | tf_op jit(solution)/shard_map/ppermute | solution.py:261
  135.9 15.3 %collective-permute-start.10 = (f32[64,128]{1,0:T(8,128)S(1)}, f32[64,128]{1,0:T(8,128)S(1)}, u32[]{:S(2)}, u32[]{:S(2)}) collective-permute-start(f32[64,128]{1,0:T(8,128)S(1)} %add_add_fusion.refs_0_), channel_id=1, source_target_pairs={{0,16},{2,18},{4,20},{6,22},{8,24},{10,26},{12,28},{14,30},{16,32}... | collective-permute-start | bytes 98312 | tf_op jit(solution)/shard_map/ppermute | solution.py:261
  139.5 11.8 %collective-permute-start.9 = (f32[64,128]{1,0:T(8,128)S(1)}, f32[64,128]{1,0:T(8,128)S(1)}, u32[]{:S(2)}, u32[]{:S(2)}) collective-permute-start(f32[64,128]{1,0:T(8,128)S(1)} %add_add_fusion.refs_0_), channel_id=1, source_target_pairs={{0,8},{2,10},{4,12},{6,14},{8,16},{10,18},{12,20},{14,22},{16,24},... | collective-permute-start | bytes 98312 | tf_op jit(solution)/shard_map/ppermute | solution.py:261
  (4 other events, 9.4 us)

commit v3 on v2

--- a/solution.py
+++ b/solution.py
@@ -10,9 +10,10 @@
 MIB = 1 << 20
 VMEM = pl.BlockSpec(memory_space=pltpu.VMEM)
 SMEM = pl.BlockSpec(memory_space=pltpu.SMEM)
-ANY = pl.BlockSpec(memory_space=pl.ANY)
+HBM = pl.BlockSpec(memory_space=pltpu.HBM)
 NX, NY, NZ = 4, 4, 8
 PACKED = 512
+TILE_STEPS = 8
 SPAN = 512
 
 
@@ -20,61 +21,82 @@
     return lax.dot_general(a, b, (((da,), (db,)), ((), ())), preferred_element_type=F32)
 
 
-def gather_kernel(rows, feats, out, table, picked):
-    peers, cap = rows.shape
+def in_hbm(value):
+    return pltpu.with_memory_space_constraint(value, pltpu.HBM)
+
+
+def gather_kernel(rows_hbm, feats_hbm, out, rows, feats, table, picked, row_sem, sems):
+    cap, peers = rows.shape
     count = feats.shape[0]
-    table[pl.ds(0, count), :] = feats[...].astype(F32)
+    part = count // sems.shape[0]
+
+    def part_copy(i):
+        span = pl.ds(i * part, part)
+        return pltpu.make_async_copy(feats_hbm.at[span], feats.at[span], sems.at[i])
+
+    row_copy = pltpu.make_async_copy(rows_hbm, rows, row_sem)
+    row_copy.start()
+    for i in range(sems.shape[0]):
+        part_copy(i).start()
     table[pl.ds(count, 8), :] = jnp.zeros((8, table.shape[1]), F32)
+    for i in range(sems.shape[0]):
+        span = pl.ds(i * part, part)
+        part_copy(i).wait()
+        table[span, :] = feats[span, :].astype(F32)
+    row_copy.wait()
 
     def one_peer(p, carry):
         base = pl.multiple_of(p * cap, cap)
         for c in range(cap):
-            picked[pl.ds(base + c, 1), :] = table[pl.ds(rows[p, c], 1), :]
+            picked[pl.ds(base + c, 1), :] = table[pl.ds(rows[c, p], 1), :]
         return carry
 
     lax.fori_loop(0, peers, one_peer, 0)
     out[...] = picked[...].astype(BF16)
 
 
-def gather_rows(send_rows, feats):
+def gather_rows(rows, feats):
     count, width = feats.shape
-    slots = send_rows.size
+    slots = rows.size
     return pl.pallas_call(
         gather_kernel,
         out_shape=jax.ShapeDtypeStruct((slots, width), BF16),
-        in_specs=[SMEM, VMEM],
+        in_specs=[HBM, HBM],
         out_specs=VMEM,
-        scratch_shapes=[pltpu.VMEM((count + 8, width), F32), pltpu.VMEM((slots, width), F32)],
-        compiler_params=pltpu.CompilerParams(vmem_limit_bytes=24 * MIB),
+        scratch_shapes=[
+            pltpu.SMEM(rows.shape, rows.dtype),
+            pltpu.VMEM(feats.shape, BF16),
+            pltpu.VMEM((count + 8, width), F32),
+            pltpu.VMEM((slots, width), F32),
+            pltpu.SemaphoreType.DMA,
+            pltpu.SemaphoreType.DMA((4,)),
+        ],
+        compiler_params=pltpu.CompilerParams(vmem_limit_bytes=12 * MIB),
+        cost_estimate=pl.CostEstimate(flops=0, bytes_accessed=8 * MIB, transcendentals=0),
         name="gather_rows",
-    )(send_rows, feats)
+    )(in_hbm(rows), in_hbm(feats))
+
+
+def tile_copy(adj, tiles, sems, i):
+    span = pl.ds(i * (adj.shape[0] // sems.shape[0]), adj.shape[0] // sems.shape[0])
+    return pltpu.make_async_copy(adj.at[span], tiles.at[span], sems.at[i])
 
 
 def aggregate_kernel(cols, feats, halo, adj, agg, ext, tiles, sems):
-    blocks, nonzero = cols.shape
-    steps = sems.shape[0] - 2
-    span = adj.shape[0] // steps
-    own_copy = pltpu.make_async_copy(feats, ext.at[pl.ds(0, blocks)], sems.at[0])
-    halo_copy = pltpu.make_async_copy(halo, ext.at[pl.ds(blocks, halo.shape[0])], sems.at[1])
-
-    def tile_copy(i):
-        return pltpu.make_async_copy(
-            adj.at[pl.ds(i * span, span)], tiles.at[pl.ds(i * span, span)], sems.at[2 + i]
-        )
-
-    own_copy.start()
-    halo_copy.start()
+    nonzero, blocks = cols.shape
+    steps = sems.shape[0]
+    per_step = blocks // steps
     for i in range(steps):
-        tile_copy(i).start()
-    own_copy.wait()
-    halo_copy.wait()
+        tile_copy(adj, tiles, sems, i).start()
+    ext[pl.ds(0, blocks)] = feats[...]
+    ext[pl.ds(blocks, halo.shape[0])] = halo[...]
 
     def one_step(i, carry):
-        tile_copy(i).wait()
-        for j in range(span // nonzero):
-            r = i * (span // nonzero) + j
+        tile_copy(adj, tiles, sems, i).wait()
+        for j in range(per_step):
+            r = i * per_step + j
             left = jnp.concatenate([tiles[r * nonzero + k] for k in range(nonzero)], 1)
-            right = jnp.concatenate([ext[cols[r, k]] for k in range(nonzero)], 0)
+            right = jnp.concatenate([ext[cols[k, r]] for k in range(nonzero)], 0)
             agg[r] = contract(left, right, 1, 0).astype(BF16)
         return carry
 
@@ -82,20 +104,20 @@
 
 
 def aggregate_blocks(cols, feats, halo, adj):
-    steps = 8
     return pl.pallas_call(
         aggregate_kernel,
         out_shape=jax.ShapeDtypeStruct(feats.shape, BF16),
-        in_specs=[SMEM, ANY, ANY, ANY],
+        in_specs=[SMEM, VMEM, VMEM, HBM],
         out_specs=VMEM,
         scratch_shapes=[
             pltpu.VMEM((feats.shape[0] + halo.shape[0],) + feats.shape[1:], BF16),
             pltpu.VMEM(adj.shape, BF16),
-            pltpu.SemaphoreType.DMA((2 + steps,)),
+            pltpu.SemaphoreType.DMA((TILE_STEPS,)),
         ],
         compiler_params=pltpu.CompilerParams(vmem_limit_bytes=24 * MIB),
+        cost_estimate=pl.CostEstimate(flops=1 << 30, bytes_accessed=12 * MIB, transcendentals=0),
         name="aggregate_blocks",
-    )(cols, feats, halo, adj)
+    )(cols, feats, halo, in_hbm(adj))
 
 
 def backward_kernel(
@@ -103,7 +125,7 @@
     halo_out, own_out, packed,
     ext_grad, tiles, sum_w, sum_c, sum_b, sems, own_sem,
 ):
-    blocks, nonzero = cols.shape
+    nonzero, blocks = cols.shape
     tile = adj.shape[1]
     steps = sems.shape[0]
     span = adj.shape[0] // steps
@@ -154,7 +176,7 @@
             right = jnp.concatenate([tiles[r * nonzero + k] for k in range(nonzero)], 1)
             term = contract(agg_grad[:, j * tile : (j + 1) * tile], right, 1, 0)
             for k in range(nonzero):
-                ext_grad[cols[r, k]] += term[:, k * tile : (k + 1) * tile]
+                ext_grad[cols[k, r]] += term[:, k * tile : (k + 1) * tile]
         return carry
 
     lax.fori_loop(0, steps, one_step, 0)
@@ -178,7 +200,7 @@
 
 
 def backward(ids, cols, agg, other, weight_t, weight, cls, cls_t, bias, labels, adj, classes, total_nodes):
-    blocks = cols.shape[0]
+    blocks = cols.shape[1]
     tile = adj.shape[1]
     rows, half = agg.shape
     steps = rows // SPAN
@@ -192,11 +214,11 @@
         body,
         out_shape=(
             jax.ShapeDtypeStruct((blocks, tile, half), BF16),
-            jax.ShapeDtypeStruct((blocks, half, tile), F32),
+            pltpu.HBM((blocks, half, tile), F32),
             jax.ShapeDtypeStruct((PACKED, half), F32),
         ),
-        in_specs=[SMEM, SMEM] + [VMEM] * 8 + [ANY],
-        out_specs=(VMEM, ANY, VMEM),
+        in_specs=[SMEM, SMEM] + [VMEM] * 8 + [HBM],
+        out_specs=(VMEM, HBM, VMEM),
         scratch_shapes=[
             pltpu.VMEM((ext_blocks, half, tile), F32),
             pltpu.VMEM(adj.shape, BF16),
@@ -208,44 +230,53 @@
         ],
         compiler_params=pltpu.CompilerParams(vmem_limit_bytes=36 * MIB),
         name="backward",
-    )(ids, cols, agg, other, weight_t, weight, cls, cls_t, bias, labels, adj)
-
-
-def scatter_kernel(rows, arrived, own, out, values, *sums):
-    peers, cap = rows.shape
+    )(ids, cols, agg, other, weight_t, weight, cls, cls_t, bias, labels, in_hbm(adj))
+
+
+def scatter_kernel(rows_hbm, arrived, own, out, rows, values, row_sem, *sums):
+    cap, peers = rows.shape
     count, width = out.shape
+    row_copy = pltpu.make_async_copy(rows_hbm, rows, row_sem)
+    row_copy.start()
     values[...] = arrived[...].astype(F32)
-    for total in sums:
+    sums[0][pl.ds(0, count), :] = own[...]
+    for total in sums[1:]:
         total[...] = jnp.zeros_like(total)
+    row_copy.wait()
 
     def one_peer(p, carry):
         base = pl.multiple_of(p * cap, cap)
         for c in range(cap):
             total = sums[c % len(sums)]
-            row = pl.ds(rows[p, c], 1)
+            row = pl.ds(rows[c, p], 1)
             total[row, :] = total[row, :] + values[pl.ds(base + c, 1), :]
         return carry
 
     lax.fori_loop(0, peers, one_peer, 0)
-    result = own[...]
-    for total in sums:
+    result = sums[0][pl.ds(0, count), :]
+    for total in sums[1:]:
         result = result + total[pl.ds(0, count), :]
     out[...] = result.astype(BF16)
 
 
-def scatter_rows(send_rows, arrived, own):
+def scatter_rows(rows, arrived, own):
     count, width = own.shape
     lanes = 8
     return pl.pallas_call(
         scatter_kernel,
         out_shape=jax.ShapeDtypeStruct((count, width), BF16),
-        in_specs=[SMEM, VMEM, VMEM],
+        in_specs=[HBM, VMEM, VMEM],
         out_specs=VMEM,
-        scratch_shapes=[pltpu.VMEM(arrived.shape, F32)]
+        scratch_shapes=[
+            pltpu.SMEM(rows.shape, rows.dtype),
+            pltpu.VMEM(arrived.shape, F32),
+            pltpu.SemaphoreType.DMA,
+        ]
         + [pltpu.VMEM((count + 8, width), F32)] * lanes,
-        compiler_params=pltpu.CompilerParams(vmem_limit_bytes=36 * MIB),
+        compiler_params=pltpu.CompilerParams(vmem_limit_bytes=32 * MIB),
+        cost_estimate=pl.CostEstimate(flops=0, bytes_accessed=8 * MIB, transcendentals=0),
         name="scatter_rows",
-    )(send_rows, arrived, own)
+    )(in_hbm(rows), arrived, own)
 
 
 def move(value, axis, target):
@@ -335,12 +366,14 @@
     total_nodes = row_count * lax.axis_size("dom")
     swap = [(0, 1), (1, 0)]
 
-    outgoing = gather_rows(send_rows, feats).reshape(peers, cap, half)
+    rows = send_rows.T
+    outgoing = gather_rows(rows, feats).reshape(peers, cap, half)
     incoming = lax.all_to_all(outgoing, "dom", split_axis=0, concat_axis=0, tiled=True)
 
-    weight_l, cls_l, bias_l, labels_l, _ = lax.optimization_barrier(
-        (weight, cls_w, bias, labels, outgoing)
-    )
+    weight_l, cls_l, bias_l, labels_l, adj_cols, _ = lax.optimization_barrier(
+        (weight, cls_w, bias, labels, adj_cols, outgoing)
+    )
+    cols = adj_cols.T
     hid = lax.axis_index("hid")
     dom = lax.axis_index("dom")
     ids = jnp.stack([hid, (dom // NX) % NZ]).astype(jnp.int32)
@@ -358,12 +391,20 @@
     bias_wide = jnp.broadcast_to(bias_l[:, None], (units, 128))
     label_rows = labels_l.reshape(row_count // SPAN, SPAN)
 
+    weight_t = weight_full.T
+    cls_t = cls_full.T
+    incoming, cols, ids, weight_t, weight_l, cls_full, cls_t, bias_wide, label_rows = (
+        lax.optimization_barrier(
+            (incoming, cols, ids, weight_t, weight_l, cls_full, cls_t, bias_wide, label_rows)
+        )
+    )
+
     halo = incoming.reshape(blocks, tile, half)
-    agg = aggregate_blocks(adj_cols, feats.reshape(blocks, tile, half), halo, adj_tiles)
+    agg = aggregate_blocks(cols, feats.reshape(blocks, tile, half), halo, adj_tiles)
     agg = agg.reshape(row_count, half)
     other = lax.ppermute(agg, "hid", swap)
     halo_grad, own_grad, packed = backward(
-        ids, adj_cols, agg, other, weight_full.T, weight_l, cls_full, cls_full.T, bias_wide,
+        ids, cols, agg, other, weight_t, weight_l, cls_full, cls_t, bias_wide,
         label_rows, adj_tiles, classes, total_nodes,
     )
     shares = swap_shares(packed)
@@ -371,7 +412,7 @@
     returned = halo_grad.reshape(peers, cap, half)
     arrived = lax.all_to_all(returned, "dom", split_axis=0, concat_axis=0, tiled=True)
     own = jnp.swapaxes(own_grad, 1, 2).reshape(row_count, half)
-    grad_feats = scatter_rows(send_rows, arrived.reshape(row_count, half), own)
+    grad_feats = scatter_rows(rows, arrived.reshape(row_count, half), own)
     return finish(ids, sum_xy(shares.sum(0)), grad_feats, classes, units)
 
 

time: 154 us -> 147 us (0.955)
  local copies, waits for them, and re-layouts: 12.5 us -> 5.33 us
    unnamed x22, local copies, waits for them, and re-layouts: 10.2 us -> 3.11 us
    ppermute x1, waiting for transfers between devices: 0.01 us -> 2.54 us  [on_device(): other = lax.ppermute(agg, 'hid', swap)]
    all_to_all x1, waiting for transfers between devices: 29.2 us -> 27.2 us  [on_device(): lax.all_to_all(outgoing, 'dom', split_axis=0, concat_axis=0, tiled=True)]
    ppermute x1, waiting for transfers between devices: 1.82 us -> 0.01 us  [on_device(): cls_o = lax.ppermute(cls_l, 'hid', swap)]
  transfers between devices with their start and end apart: 18 -> 18, of which waited for: 6 -> 6; matrix products, arithmetic and copies ran while one was open for 2% -> 2% of each run, Pallas kernels for 6% -> 5%
where the time goes in v3:
time: 147 us; the launch traced here: 146 us
  starting transfers between devices  47.2 us (32%)
  waiting for transfers between devices  37.4 us (25%)
  Pallas kernels  37.3 us (25%)
  blocking collectives  16 us (11%)
  local copies, waits for them, and re-layouts  5.33 us (4%)
    all_to_all x1, waiting for transfers between devices, on_device(): lax.all_to_all(outgoing, 'dom', split_axis=0, concat_axis=0, tiled=True)  27.2 us
    ppermute x13, starting transfers between devices, move(): return lax.ppermute(value, 'dom', pairs)  24.3 us
    all_to_all x1, blocking collectives, swap_shares(): lax.all_to_all(shares, 'dom', split_axis=0, concat_axis=0, tiled=True, ax...  16 us
    all_to_all x1, starting transfers between devices, on_device(): lax.all_to_all(outgoing, 'dom', split_axis=0, concat_axis=0, tiled=True)  15.6 us
    pallas_call x1, Pallas kernels, backward(): pl.pallas_call(body, out_shape=(jax.ShapeDtypeStruct((blocks, tile, half)...  15.3 us
    pallas_call x1, Pallas kernels, scatter_rows(): pl.pallas_call(scatter_kernel, out_shape=jax.ShapeDtypeStruct((count, wid...  7.98 us
    ppermute x13, waiting for transfers between devices, move(): return lax.ppermute(value, 'dom', pairs)  7.69 us
    pallas_call x1, Pallas kernels, gather_rows(): pl.pallas_call(gather_kernel, out_shape=jax.ShapeDtypeStruct((slots, widt...  7.37 us
  transfers between devices with their start and end apart: 18, of which 6 were waited for; matrix products, arithmetic and copies ran while one was open for 2% of the time, Pallas kernels for 5%

profile of v3, /device:TPU:2, one launch (start us, length us, event | category | flops | bytes accessed | tf_op | source)
XLA Modules:
  0.0 145.5 jit_solution(3165666089580407640)
XLA Ops:
  0.7 7.4 %gather_rows.1 = bf16[4096,128]{1,0:T(8,128)(2,1)} custom-call(s32[32,128]{1,0:T(8,128)} %bitcast.29, bf16[4096,128]{1,0:T(8,128)(2,1)} %feats_hbm.1), custom_call_target="tpu_custom_call" | custom-call | bytes 8388608 | tf_op jit(solution)/shard_map/gather_rows/pallas_call | solution.py:61
  8.1 15.6 %all-to-all-start = ((bf16[128,32,128]{2,1,0:T(8,128)(2,1)}), bf16[128,32,128]{2,1,0:T(8,128)(2,1)S(1)}, u32[]{:S(2)}, u32[]{:S(2)}) async-start(bf16[128,32,128]{2,1,0:T(8,128)(2,1)} %bitcast.1), calls=%async_computation | async-start | bytes 2097152 | tf_op jit(solution)/shard_map/all_to_all | solution.py:371
  25.8 27.2 %all-to-all-done = bf16[128,32,128]{2,1,0:T(8,128)(2,1)S(1)} async-done(((bf16[128,32,128]{2,1,0:T(8,128)(2,1)}), bf16[128,32,128]{2,1,0:T(8,128)(2,1)S(1)}, u32[]{:S(2)}, u32[]{:S(2)}) %all-to-all-start) | async-done | bytes 1048608 | tf_op jit(solution)/shard_map/all_to_all | solution.py:371
  53.1 5.3 %aggregate_blocks.1 = bf16[32,128,128]{2,1,0:T(8,128)(2,1)S(1)} custom-call(s32[8,32]{1,0:T(8,128)S(1)} %bitcast.26, bf16[32,128,128]{2,1,0:T(8,128)(2,1)S(1)} %bitcast.23, bf16[32,128,128]{2,1,0:T(8,128)(2,1)S(1)} %bitcast.24, bf16[256,128,128]{2,1,0:T(8,128)(2,1)} %refs_10_.1), custom_call_target="tpu_custom_call" | custom-call | flops 1073741824 | bytes 12582912 | tf_op jit(solution)/shard_map/aggregate_blocks/pallas_call | solution.py:107
  58.6 2.5 %collective-permute-done.2.refs_3_ = bf16[4096,128]{1,0:T(8,128)(2,1)S(1)} collective-permute-done((bf16[4096,128]{1,0:T(8,128)(2,1)S(1)}, bf16[4096,128]{1,0:T(8,128)(2,1)S(1)}, u32[]{:S(2)}, u32[]{:S(2)}) %collective-permute-start.2) | collective-permute-done | bytes 1048608 | tf_op jit(solution)/shard_map/ppermute | solution.py:405
  64.2 15.3 %backward.1 = (bf16[32,128,128]{2,1,0:T(8,128)(2,1)}, f32[32,128,128]{2,1,0:T(8,128)}, f32[512,128]{1,0:T(8,128)S(1)}) custom-call(s32[2]{0:T(128)S(1)} %copy-done.6, s32[8,32]{1,0:T(8,128)S(1)} %bitcast.27, bf16[4096,128]{1,0:T(8,128)(2,1)S(1)} %bitcast.22, bf16[4096,128]{1,0:T(8,128)(2,1)S(1)} %collective-permute-done.2.refs_3_, ...), custom_call_target="tpu_custom_call" | custom-call | tf_op jit(solution)/shard_map/backward/pallas_call | solution.py:213
  79.5 16.0 %all_to_all.15 = f32[8,64,128]{2,1,0:T(8,128)S(1)} all-to-all(f32[8,64,128]{2,1,0:T(8,128)S(1)} %bitcast.25), channel_id=1, replica_groups={{0,8,16,24,32,40,48,56},{2,10,18,26,34,42,50,58},{4,12,20,28,36,44,52,6..., dimensions={0} | all-to-all | bytes 524288 | tf_op jit(solution)/shard_map/all_to_all | solution.py:314
  95.5 6.6 %all-to-all-start.2 = ((bf16[128,32,128]{2,1,0:T(8,128)(2,1)}), bf16[128,32,128]{2,1,0:T(8,128)(2,1)S(1)}, u32[]{:S(2)}, u32[]{:S(2)}) async-start(bf16[128,32,128]{2,1,0:T(8,128)(2,1)} %bitcast.11), calls=%async_computation.2 | async-start | bytes 2097152 | tf_op jit(solution)/shard_map/all_to_all | solution.py:413
  102.2 1.6 %collective-permute-start.5 = (f32[64,128]{1,0:T(8,128)S(1)}, f32[64,128]{1,0:T(8,128)S(1)}, u32[]{:S(2)}, u32[]{:S(2)}) collective-permute-start(f32[64,128]{1,0:T(8,128)S(1)} %reduce_sum.9), channel_id=1, source_target_pairs={{0,6},{2,4},{4,2},{6,0},{8,14},{10,12},{12,10},{14,8},{16,22},{18,... | collective-permute-start | bytes 98312 | tf_op jit(solution)/shard_map/ppermute | solution.py:292
  103.8 1.6 %collective-permute-start.4 = (f32[64,128]{1,0:T(8,128)S(1)}, f32[64,128]{1,0:T(8,128)S(1)}, u32[]{:S(2)}, u32[]{:S(2)}) collective-permute-start(f32[64,128]{1,0:T(8,128)S(1)} %reduce_sum.9), channel_id=1, source_target_pairs={{0,4},{2,6},{4,0},{6,2},{8,12},{10,14},{12,8},{14,10},{16,20},{18,... | collective-permute-start | bytes 98312 | tf_op jit(solution)/shard_map/ppermute | solution.py:292
  105.4 1.0 collective-permute-start.3
  106.4 2.9 %collective-permute-done.4 = f32[64,128]{1,0:T(8,128)S(1)} collective-permute-done((f32[64,128]{1,0:T(8,128)S(1)}, f32[64,128]{1,0:T(8,128)S(1)}, u32[]{:S(2)}, u32[]{:S(2)}) %collective-permute-start.4) | collective-permute-done | bytes 32800 | tf_op jit(solution)/shard_map/ppermute | solution.py:292
  109.5 3.2 %collective-permute-start.8 = (f32[64,128]{1,0:T(8,128)S(1)}, f32[64,128]{1,0:T(8,128)S(1)}, u32[]{:S(2)}, u32[]{:S(2)}) collective-permute-start(f32[64,128]{1,0:T(8,128)S(1)} %add_add_fusion.1), channel_id=1, source_target_pairs={{0,192},{2,194},{4,196},{6,198},{8,200},{10,202},{12,204},{14,206}... | collective-permute-start | bytes 98312 | tf_op jit(solution)/shard_map/ppermute | solution.py:292
  113.7 1.8 %collective-permute-done.8 = f32[64,128]{1,0:T(8,128)S(1)} collective-permute-done((f32[64,128]{1,0:T(8,128)S(1)}, f32[64,128]{1,0:T(8,128)S(1)}, u32[]{:S(2)}, u32[]{:S(2)}) %collective-permute-start.8) | collective-permute-done | bytes 32800 | tf_op jit(solution)/shard_map/ppermute | solution.py:292
  115.5 2.8 %collective-permute-done.7 = f32[64,128]{1,0:T(8,128)S(1)} collective-permute-done((f32[64,128]{1,0:T(8,128)S(1)}, f32[64,128]{1,0:T(8,128)S(1)}, u32[]{:S(2)}, u32[]{:S(2)}) %collective-permute-start.7) | collective-permute-done | bytes 32800 | tf_op jit(solution)/shard_map/ppermute | solution.py:292
  118.3 3.7 %collective-permute-start.15 = (f32[64,128]{1,0:T(8,128)S(1)}, f32[64,128]{1,0:T(8,128)S(1)}, u32[]{:S(2)}, u32[]{:S(2)}) collective-permute-start(f32[64,128]{1,0:T(8,128)S(1)} %add_add_fusion.refs_0_), channel_id=1, source_target_pairs={{0,56},{2,58},{4,60},{6,62},{8,0},{10,2},{12,4},{14,6},{16,8},{18,... | collective-permute-start | bytes 98312 | tf_op jit(solution)/shard_map/ppermute | solution.py:292
  122.0 2.0 %collective-permute-start.14 = (f32[64,128]{1,0:T(8,128)S(1)}, f32[64,128]{1,0:T(8,128)S(1)}, u32[]{:S(2)}, u32[]{:S(2)}) collective-permute-start(f32[64,128]{1,0:T(8,128)S(1)} %add_add_fusion.refs_0_), channel_id=1, source_target_pairs={{0,48},{2,50},{4,52},{6,54},{8,56},{10,58},{12,60},{14,62},{16,0},... | collective-permute-start | bytes 98312 | tf_op jit(solution)/shard_map/ppermute | solution.py:292
  124.0 1.6 %collective-permute-start.13 = (f32[64,128]{1,0:T(8,128)S(1)}, f32[64,128]{1,0:T(8,128)S(1)}, u32[]{:S(2)}, u32[]{:S(2)}) collective-permute-start(f32[64,128]{1,0:T(8,128)S(1)} %add_add_fusion.refs_0_), channel_id=1, source_target_pairs={{0,40},{2,42},{4,44},{6,46},{8,48},{10,50},{12,52},{14,54},{16,56}... | collective-permute-start | bytes 98312 | tf_op jit(solution)/shard_map/ppermute | solution.py:292
  125.7 3.5 %collective-permute-start.12 = (f32[64,128]{1,0:T(8,128)S(1)}, f32[64,128]{1,0:T(8,128)S(1)}, u32[]{:S(2)}, u32[]{:S(2)}) collective-permute-start(f32[64,128]{1,0:T(8,128)S(1)} %add_add_fusion.refs_0_), channel_id=1, source_target_pairs={{0,32},{2,34},{4,36},{6,38},{8,40},{10,42},{12,44},{14,46},{16,48}... | collective-permute-start | bytes 98312 | tf_op jit(solution)/shard_map/ppermute | solution.py:292
  129.3 3.5 %collective-permute-start.10 = (f32[64,128]{1,0:T(8,128)S(1)}, f32[64,128]{1,0:T(8,128)S(1)}, u32[]{:S(2)}, u32[]{:S(2)}) collective-permute-start(f32[64,128]{1,0:T(8,128)S(1)} %add_add_fusion.refs_0_), channel_id=1, source_target_pairs={{0,16},{2,18},{4,20},{6,22},{8,24},{10,26},{12,28},{14,30},{16,32}... | collective-permute-start | bytes 98312 | tf_op jit(solution)/shard_map/ppermute | solution.py:292
  132.8 1.4 collective-permute-start.9
  134.2 1.9 %copy.16 = f32[32,128,128]{2,1,0:T(8,128)S(1)} copy(f32[32,128,128]{1,2,0:T(8,128)} %bitcast.28) | data formatting | bytes 4194304 | tf_op jit(solution)/shard_map/transpose | solution.py:414
  136.1 8.0 %scatter_rows.1 = bf16[4096,128]{1,0:T(8,128)(2,1)} custom-call(s32[32,128]{1,0:T(8,128)} %bitcast.30, bf16[4096,128]{1,0:T(8,128)(2,1)S(1)} %bitcast.20, f32[4096,128]{1,0:T(8,128)S(1)} %bitcast.19), custom_call_target="tpu_custom_call" | custom-call | bytes 8388608 | tf_op jit(solution)/shard_map/scatter_rows/pallas_call | solution.py:265
  144.2 1.3 finish.1
  (53 shorter events, 6.8 us)
Async XLA Ops:
  0.6 23.0 %copy-start.8 = (bf16[128,172]{0,1:T(8,128)(2,1)S(1)}, bf16[128,172]{0,1:T(8,128)(2,1)}, u32[]{:S(2)}) copy-start(bf16[128,172]{0,1:T(8,128)(2,1)} %param.14) | copy-start | bytes 132100
  0.6 23.1 %copy-start.2 = (bf16[128,256]{1,0:T(8,128)(2,1)S(1)}, bf16[128,256]{1,0:T(8,128)(2,1)}, u32[]{:S(2)}) copy-start(bf16[128,256]{1,0:T(8,128)(2,1)} %refs_5_) | copy-start | bytes 196612
  0.7 24.4 %copy-start.9 = (s32[4096]{0:T(1024)S(1)}, s32[4096]{0:T(1024)}, u32[]{:S(2)}) copy-start(s32[4096]{0:T(1024)} %param.15) | copy-start | bytes 49156
  8.0 44.9 %copy-start.10 = (f32[256]{0:T(256)S(1)}, f32[256]{0:T(256)}, u32[]{:S(2)}) copy-start(f32[256]{0:T(256)} %param.13) | copy-start | bytes 3076
  8.0 45.0 %copy-start = (bf16[4096,128]{1,0:T(8,128)(2,1)S(1)}, bf16[4096,128]{1,0:T(8,128)(2,1)}, u32[]{:S(2)}) copy-start(bf16[4096,128]{1,0:T(8,128)(2,1)} %feats_hbm.1) | copy-start | bytes 3145732
  8.1 45.0 %copy-start.4 = (s32[32,8]{0,1:T(8,128)S(1)}, s32[32,8]{0,1:T(8,128)}, u32[]{:S(2)}) copy-start(s32[32,8]{0,1:T(8,128)} %param.10) | copy-start | bytes 3076
  8.1 44.9 %all-to-all-start = ((bf16[128,32,128]{2,1,0:T(8,128)(2,1)}), bf16[128,32,128]{2,1,0:T(8,128)(2,1)S(1)}, u32[]{:S(2)}, u32[]{:S(2)}) async-start(bf16[128,32,128]{2,1,0:T(8,128)(2,1)} %bitcast.1), calls=%async_computation | async-start | bytes 2097152 | tf_op jit(solution)/shard_map/all_to_all | solution.py:371
  23.7 1.4 collective-permute-start.1
  23.9 1.9 %collective-permute-start = (bf16[128,256]{0,1:T(8,128)(2,1)S(1)}, bf16[128,256]{0,1:T(8,128)(2,1)S(1)}, u32[]{:S(2)}, u32[]{:S(2)}) collective-permute-start(bf16[128,256]{0,1:T(8,128)(2,1)S(1)} %copy.13), channel_id=1, source_target_pairs={{0,1},{1,0},{2,3},{3,2},{4,5},{5,4},{6,7},{7,6},{8,9},{9,8},{10,11... | collective-permute-start | bytes 196616 | tf_op jit(solution)/shard_map/ppermute | solution.py:380
  58.4 2.7 %collective-permute-start.2 = (bf16[4096,128]{1,0:T(8,128)(2,1)S(1)}, bf16[4096,128]{1,0:T(8,128)(2,1)S(1)}, u32[]{:S(2)}, u32[]{:S(2)}) collective-permute-start(bf16[4096,128]{1,0:T(8,128)(2,1)S(1)} %bitcast.21), channel_id=1, source_target_pairs={{0,1},{1,0},{2,3},{3,2},{4,5},{5,4},{6,7},{7,6},{8,9},{9,8},{10,11... | collective-permute-start | bytes 3145736 | tf_op jit(solution)/shard_map/ppermute | solution.py:405
  95.5 40.6 %all-to-all-start.2 = ((bf16[128,32,128]{2,1,0:T(8,128)(2,1)}), bf16[128,32,128]{2,1,0:T(8,128)(2,1)S(1)}, u32[]{:S(2)}, u32[]{:S(2)}) async-start(bf16[128,32,128]{2,1,0:T(8,128)(2,1)} %bitcast.11), calls=%async_computation.2 | async-start | bytes 2097152 | tf_op jit(solution)/shard_map/all_to_all | solution.py:413
  102.2 4.2 %collective-permute-start.5 = (f32[64,128]{1,0:T(8,128)S(1)}, f32[64,128]{1,0:T(8,128)S(1)}, u32[]{:S(2)}, u32[]{:S(2)}) collective-permute-start(f32[64,128]{1,0:T(8,128)S(1)} %reduce_sum.9), channel_id=1, source_target_pairs={{0,6},{2,4},{4,2},{6,0},{8,14},{10,12},{12,10},{14,8},{16,22},{18,... | collective-permute-start | bytes 98312 | tf_op jit(solution)/shard_map/ppermute | solution.py:292
  103.8 5.5 %collective-permute-start.4 = (f32[64,128]{1,0:T(8,128)S(1)}, f32[64,128]{1,0:T(8,128)S(1)}, u32[]{:S(2)}, u32[]{:S(2)}) collective-permute-start(f32[64,128]{1,0:T(8,128)S(1)} %reduce_sum.9), channel_id=1, source_target_pairs={{0,4},{2,6},{4,0},{6,2},{8,12},{10,14},{12,8},{14,10},{16,20},{18,... | collective-permute-start | bytes 98312 | tf_op jit(solution)/shard_map/ppermute | solution.py:292
  105.4 4.1 %collective-permute-start.3 = (f32[64,128]{1,0:T(8,128)S(1)}, f32[64,128]{1,0:T(8,128)S(1)}, u32[]{:S(2)}, u32[]{:S(2)}) collective-permute-start(f32[64,128]{1,0:T(8,128)S(1)} %reduce_sum.9), channel_id=1, source_target_pairs={{0,2},{2,0},{4,6},{6,4},{8,10},{10,8},{12,14},{14,12},{16,18},{18,... | collective-permute-start | bytes 98312 | tf_op jit(solution)/shard_map/ppermute | solution.py:292
  109.5 6.0 %collective-permute-start.8 = (f32[64,128]{1,0:T(8,128)S(1)}, f32[64,128]{1,0:T(8,128)S(1)}, u32[]{:S(2)}, u32[]{:S(2)}) collective-permute-start(f32[64,128]{1,0:T(8,128)S(1)} %add_add_fusion.1), channel_id=1, source_target_pairs={{0,192},{2,194},{4,196},{6,198},{8,200},{10,202},{12,204},{14,206}... | collective-permute-start | bytes 98312 | tf_op jit(solution)/shard_map/ppermute | solution.py:292
  112.6 5.6 %collective-permute-start.7 = (f32[64,128]{1,0:T(8,128)S(1)}, f32[64,128]{1,0:T(8,128)S(1)}, u32[]{:S(2)}, u32[]{:S(2)}) collective-permute-start(f32[64,128]{1,0:T(8,128)S(1)} %add_add_fusion.1), channel_id=1, source_target_pairs={{0,128},{2,130},{4,132},{6,134},{8,136},{10,138},{12,140},{14,142}... | collective-permute-start | bytes 98312 | tf_op jit(solution)/shard_map/ppermute | solution.py:292
  113.1 5.2 %collective-permute-start.6 = (f32[64,128]{1,0:T(8,128)S(1)}, f32[64,128]{1,0:T(8,128)S(1)}, u32[]{:S(2)}, u32[]{:S(2)}) collective-permute-start(f32[64,128]{1,0:T(8,128)S(1)} %add_add_fusion.1), channel_id=1, source_target_pairs={{0,64},{2,66},{4,68},{6,70},{8,72},{10,74},{12,76},{14,78},{16,80}... | collective-permute-start | bytes 98312 | tf_op jit(solution)/shard_map/ppermute | solution.py:292
  118.3 11.0 %collective-permute-start.15 = (f32[64,128]{1,0:T(8,128)S(1)}, f32[64,128]{1,0:T(8,128)S(1)}, u32[]{:S(2)}, u32[]{:S(2)}) collective-permute-start(f32[64,128]{1,0:T(8,128)S(1)} %add_add_fusion.refs_0_), channel_id=1, source_target_pairs={{0,56},{2,58},{4,60},{6,62},{8,0},{10,2},{12,4},{14,6},{16,8},{18,... | collective-permute-start | bytes 98312 | tf_op jit(solution)/shard_map/ppermute | solution.py:292
  122.0 10.8 %collective-permute-start.14 = (f32[64,128]{1,0:T(8,128)S(1)}, f32[64,128]{1,0:T(8,128)S(1)}, u32[]{:S(2)}, u32[]{:S(2)}) collective-permute-start(f32[64,128]{1,0:T(8,128)S(1)} %add_add_fusion.refs_0_), channel_id=1, source_target_pairs={{0,48},{2,50},{4,52},{6,54},{8,56},{10,58},{12,60},{14,62},{16,0},... | collective-permute-start | bytes 98312 | tf_op jit(solution)/shard_map/ppermute | solution.py:292
  124.0 20.1 %collective-permute-start.13 = (f32[64,128]{1,0:T(8,128)S(1)}, f32[64,128]{1,0:T(8,128)S(1)}, u32[]{:S(2)}, u32[]{:S(2)}) collective-permute-start(f32[64,128]{1,0:T(8,128)S(1)} %add_add_fusion.refs_0_), channel_id=1, source_target_pairs={{0,40},{2,42},{4,44},{6,46},{8,48},{10,50},{12,52},{14,54},{16,56}... | collective-permute-start | bytes 98312 | tf_op jit(solution)/shard_map/ppermute | solution.py:292
  125.7 18.4 %collective-permute-start.12 = (f32[64,128]{1,0:T(8,128)S(1)}, f32[64,128]{1,0:T(8,128)S(1)}, u32[]{:S(2)}, u32[]{:S(2)}) collective-permute-start(f32[64,128]{1,0:T(8,128)S(1)} %add_add_fusion.refs_0_), channel_id=1, source_target_pairs={{0,32},{2,34},{4,36},{6,38},{8,40},{10,42},{12,44},{14,46},{16,48}... | collective-permute-start | bytes 98312 | tf_op jit(solution)/shard_map/ppermute | solution.py:292
  129.2 14.9 %collective-permute-start.11 = (f32[64,128]{1,0:T(8,128)S(1)}, f32[64,128]{1,0:T(8,128)S(1)}, u32[]{:S(2)}, u32[]{:S(2)}) collective-permute-start(f32[64,128]{1,0:T(8,128)S(1)} %add_add_fusion.refs_0_), channel_id=1, source_target_pairs={{0,24},{2,26},{4,28},{6,30},{8,32},{10,34},{12,36},{14,38},{16,40}... | collective-permute-start | bytes 98312 | tf_op jit(solution)/shard_map/ppermute | solution.py:292
  129.3 14.9 %collective-permute-start.10 = (f32[64,128]{1,0:T(8,128)S(1)}, f32[64,128]{1,0:T(8,128)S(1)}, u32[]{:S(2)}, u32[]{:S(2)}) collective-permute-start(f32[64,128]{1,0:T(8,128)S(1)} %add_add_fusion.refs_0_), channel_id=1, source_target_pairs={{0,16},{2,18},{4,20},{6,22},{8,24},{10,26},{12,28},{14,30},{16,32}... | collective-permute-start | bytes 98312 | tf_op jit(solution)/shard_map/ppermute | solution.py:292
  132.8 11.3 %collective-permute-start.9 = (f32[64,128]{1,0:T(8,128)S(1)}, f32[64,128]{1,0:T(8,128)S(1)}, u32[]{:S(2)}, u32[]{:S(2)}) collective-permute-start(f32[64,128]{1,0:T(8,128)S(1)} %add_add_fusion.refs_0_), channel_id=1, source_target_pairs={{0,8},{2,10},{4,12},{6,14},{8,16},{10,18},{12,20},{14,22},{16,24},... | collective-permute-start | bytes 98312 | tf_op jit(solution)/shard_map/ppermute | solution.py:292
  (5 other events, 11.1 us)

commit v4 on v3

--- a/solution.py
+++ b/solution.py
@@ -12,7 +12,7 @@
 SMEM = pl.BlockSpec(memory_space=pltpu.SMEM)
 HBM = pl.BlockSpec(memory_space=pltpu.HBM)
 NX, NY, NZ = 4, 4, 8
-PACKED = 512
+PACKED = 448
 TILE_STEPS = 8
 SPAN = 512
 
@@ -120,42 +120,30 @@
     )(cols, feats, halo, in_hbm(adj))
 
 
-def backward_kernel(
-    classes, total_nodes, ids, cols, agg, other, weight_t, weight, cls, cls_t, bias, labels, adj,
-    halo_out, own_out, packed,
-    ext_grad, tiles, sum_w, sum_c, sum_b, sems, own_sem,
+def dense_kernel(
+    classes, total_nodes, ids, agg, other, weight_t, weight, cls, cls_t, bias, labels,
+    grad_out, packed, sum_w, sum_c, sum_b,
 ):
-    nonzero, blocks = cols.shape
-    tile = adj.shape[1]
-    steps = sems.shape[0]
-    span = adj.shape[0] // steps
-    per_step = SPAN // tile
-    hid = ids[0]
-
-    def tile_copy(i):
-        return pltpu.make_async_copy(
-            adj.at[pl.ds(i * span, span)], tiles.at[pl.ds(i * span, span)], sems.at[i]
+    steps = labels.shape[0]
+    class_rows = cls_t.shape[0]
+    first = ids[0] == 0
+    half = agg.shape[1]
+
+    def both(mine, theirs, dim):
+        return jnp.concatenate(
+            [jnp.where(first, mine, theirs), jnp.where(first, theirs, mine)], dim
         )
 
-    for i in range(steps):
-        tile_copy(i).start()
-    ext_grad[...] = jnp.zeros_like(ext_grad)
     sum_w[...] = jnp.zeros_like(sum_w)
     sum_c[...] = jnp.zeros_like(sum_c)
     sum_b[...] = jnp.zeros_like(sum_b)
-    class_rows = cls_t.shape[0]
     class_id = lax.broadcasted_iota(jnp.int32, (class_rows, SPAN), 0)
-    first = hid == 0
-    half = agg.shape[1]
 
     def one_step(i, carry):
         nodes = pl.ds(pl.multiple_of(i * SPAN, SPAN), SPAN)
         mine = agg[nodes, :]
-        theirs = other[nodes, :]
-        both = jnp.concatenate(
-            [jnp.where(first, mine, theirs), jnp.where(first, theirs, mine)], 1
-        )
-        preact = contract(weight_t[...], both, 1, 1) + jnp.tile(bias[...], (1, SPAN // bias.shape[1]))
+        preact = contract(weight_t[...], both(mine, other[nodes, :], 1), 1, 1)
+        preact = preact + jnp.tile(bias[...], (1, SPAN // bias.shape[1]))
         hidden = jnp.maximum(preact, 0.0).astype(BF16)
         logits = contract(cls_t[...], hidden, 1, 0)
         logits = jnp.where(class_id < classes, logits, -jnp.inf)
@@ -170,67 +158,100 @@
         sum_c[...] += contract(logit_grad, own_hidden, 1, 1)
         sum_b[...] += contract(jnp.ones((8, SPAN), BF16), preact_grad, 1, 1)
         agg_grad = contract(weight[...], preact_grad, 1, 0).astype(BF16)
-        tile_copy(i).wait()
-        for j in range(per_step):
-            r = i * per_step + j
-            right = jnp.concatenate([tiles[r * nonzero + k] for k in range(nonzero)], 1)
-            term = contract(agg_grad[:, j * tile : (j + 1) * tile], right, 1, 0)
-            for k in range(nonzero):
-                ext_grad[cols[k, r]] += term[:, k * tile : (k + 1) * tile]
+        for j in range(SPAN // half):
+            grad_out[i * (SPAN // half) + j] = agg_grad[:, j * half : (j + 1) * half]
         return carry
 
     lax.fori_loop(0, steps, one_step, 0)
-    own_copy = pltpu.make_async_copy(ext_grad.at[pl.ds(0, blocks)], own_out, own_sem)
-    own_copy.start()
-
-    def one_halo(b, carry):
-        halo_out[b] = ext_grad[blocks + b].T.astype(BF16)
-        return carry
-
-    lax.fori_loop(0, halo_out.shape[0], one_halo, 0, unroll=4)
     scale = 1.0 / total_nodes
     units = 2 * half
     packed[pl.ds(0, units), :] = sum_w[...] * scale
     packed[pl.ds(units, class_rows), :] = sum_c[...] * scale
     packed[pl.ds(units + class_rows, 8), :] = sum_b[:, :half] * scale
     packed[pl.ds(units + class_rows + 8, 8), :] = sum_b[:, half:] * scale
-    rest = units + class_rows + 16
-    packed[pl.ds(rest, packed.shape[0] - rest), :] = jnp.zeros((packed.shape[0] - rest, half), F32)
-    own_copy.wait()
-
-
-def backward(ids, cols, agg, other, weight_t, weight, cls, cls_t, bias, labels, adj, classes, total_nodes):
-    blocks = cols.shape[1]
-    tile = adj.shape[1]
+
+
+def dense(ids, agg, other, weight_t, weight, cls, cls_t, bias, labels, classes, total_nodes):
     rows, half = agg.shape
+    units = weight.shape[1]
     steps = rows // SPAN
     class_rows = cls_t.shape[0]
-    ext_blocks = 2 * blocks
 
     def body(*refs):
-        backward_kernel(classes, total_nodes, *refs)
+        dense_kernel(classes, total_nodes, *refs)
 
     return pl.pallas_call(
         body,
         out_shape=(
+            jax.ShapeDtypeStruct((rows // half, half, half), BF16),
+            jax.ShapeDtypeStruct((PACKED, half), F32),
+        ),
+        in_specs=[SMEM] + [VMEM] * 8,
+        out_specs=(VMEM,) * 2,
+        scratch_shapes=[
+            pltpu.VMEM((units, half), F32),
+            pltpu.VMEM((class_rows, half), F32),
+            pltpu.VMEM((8, units), F32),
+        ],
+        compiler_params=pltpu.CompilerParams(vmem_limit_bytes=16 * MIB),
+        cost_estimate=pl.CostEstimate(flops=5 << 30, bytes_accessed=4 * MIB, transcendentals=1 << 20),
+        name="dense",
+    )(ids, agg, other, weight_t, weight, cls, cls_t, bias, labels)
+
+
+def spread_kernel(cols, grads, adj, halo_out, own_out, ext_grad, tiles, sems, own_sem):
+    nonzero, blocks = cols.shape
+    tile = adj.shape[1]
+    steps = sems.shape[0]
+    per_step = blocks // steps
+    for i in range(steps):
+        tile_copy(adj, tiles, sems, i).start()
+    ext_grad[...] = jnp.zeros_like(ext_grad)
+
+    def one_step(i, carry):
+        tile_copy(adj, tiles, sems, i).wait()
+        for j in range(per_step):
+            r = i * per_step + j
+            right = jnp.concatenate([tiles[r * nonzero + k] for k in range(nonzero)], 1)
+            term = contract(grads[r], right, 1, 0)
+            for k in range(nonzero):
+                ext_grad[cols[k, r]] += term[:, k * tile : (k + 1) * tile]
+        return carry
+
+    lax.fori_loop(0, steps, one_step, 0)
+    own_copy = pltpu.make_async_copy(ext_grad.at[pl.ds(0, blocks)], own_out, own_sem)
+    own_copy.start()
+
+    def one_halo(b, carry):
+        halo_out[b] = ext_grad[blocks + b].T.astype(BF16)
+        return carry
+
+    lax.fori_loop(0, halo_out.shape[0], one_halo, 0, unroll=4)
+    own_copy.wait()
+
+
+def spread_blocks(cols, grads, adj):
+    blocks = cols.shape[1]
+    tile = adj.shape[1]
+    half = grads.shape[1]
+    return pl.pallas_call(
+        spread_kernel,
+        out_shape=(
             jax.ShapeDtypeStruct((blocks, tile, half), BF16),
             pltpu.HBM((blocks, half, tile), F32),
-            jax.ShapeDtypeStruct((PACKED, half), F32),
         ),
-        in_specs=[SMEM, SMEM] + [VMEM] * 8 + [HBM],
-        out_specs=(VMEM, HBM, VMEM),
+        in_specs=[SMEM, VMEM, HBM],
+        out_specs=(VMEM, HBM),
         scratch_shapes=[
-            pltpu.VMEM((ext_blocks, half, tile), F32),
+            pltpu.VMEM((2 * blocks, half, tile), F32),
             pltpu.VMEM(adj.shape, BF16),
-            pltpu.VMEM((2 * half, half), F32),
-            pltpu.VMEM((class_rows, half), F32),
-            pltpu.VMEM((8, 2 * half), F32),
-            pltpu.SemaphoreType.DMA((steps,)),
+            pltpu.SemaphoreType.DMA((TILE_STEPS,)),
             pltpu.SemaphoreType.DMA,
         ],
-        compiler_params=pltpu.CompilerParams(vmem_limit_bytes=36 * MIB),
-        name="backward",
-    )(ids, cols, agg, other, weight_t, weight, cls, cls_t, bias, labels, in_hbm(adj))
+        compiler_params=pltpu.CompilerParams(vmem_limit_bytes=24 * MIB),
+        cost_estimate=pl.CostEstimate(flops=1 << 30, bytes_accessed=12 * MIB, transcendentals=0),
+        name="spread_blocks",
+    )(cols, grads, in_hbm(adj))
 
 
 def scatter_kernel(rows_hbm, arrived, own, out, rows, values, row_sem, *sums):
@@ -403,10 +424,11 @@
     agg = aggregate_blocks(cols, feats.reshape(blocks, tile, half), halo, adj_tiles)
     agg = agg.reshape(row_count, half)
     other = lax.ppermute(agg, "hid", swap)
-    halo_grad, own_grad, packed = backward(
-        ids, cols, agg, other, weight_t, weight_l, cls_full, cls_t, bias_wide,
-        label_rows, adj_tiles, classes, total_nodes,
-    )
+    grads, packed = dense(
+        ids, agg, other, weight_t, weight_l, cls_full, cls_t, bias_wide, label_rows,
+        classes, total_nodes,
+    )
+    halo_grad, own_grad = spread_blocks(cols, grads, adj_tiles)
     shares = swap_shares(packed)
     halo_grad, own_grad, shares = lax.optimization_barrier((halo_grad, own_grad, shares))
     returned = halo_grad.reshape(peers, cap, half)

time: 147 us -> 142 us (0.966)
  blocking collectives: 16 us -> 0 us
  starting transfers between devices: 47.2 us -> 52.9 us
  waiting for transfers between devices: 37.4 us -> 40.8 us
  Pallas kernels: 37.3 us -> 39.6 us
    all_to_all x1 -> x0, blocking collectives: 16 us -> none  [swap_shares(): lax.all_to_all(shares, 'dom', split_axis=0, concat_axis=0, tiled=True, ax...]
    all_to_all x0 -> x1, starting transfers between devices: none -> 4.03 us  [swap_shares(): lax.all_to_all(shares, 'dom', split_axis=0, concat_axis=0, tiled=True, ax...]
    all_to_all x0 -> x1, waiting for transfers between devices: none -> 3.59 us  [swap_shares(): lax.all_to_all(shares, 'dom', split_axis=0, concat_axis=0, tiled=True, ax...]
    pallas_call x1 -> x2, Pallas kernels: 15.3 us -> 17.6 us  [the longest x1 9.68 us: dense(): pl.pallas_call(body, out_shape=(jax.ShapeDtypeStruct((rows // half, half,...]
    all_to_all x1, starting transfers between devices: 6.63 us -> 8.6 us  [on_device(): lax.all_to_all(returned, 'dom', split_axis=0, concat_axis=0, tiled=True)]
    unnamed x22 -> x18, local copies, waits for them, and re-layouts: 3.11 us -> 3.07 us
  transfers between devices with their start and end apart: 18 -> 19, of which waited for: 6 -> 7; matrix products, arithmetic and copies ran while one was open for 2% -> 3% of each run, Pallas kernels for 5% -> 11%
where the time goes in v4:
time: 142 us; the launch traced here: 141 us
  starting transfers between devices  52.9 us (37%)
  waiting for transfers between devices  40.8 us (29%)
  Pallas kernels  39.6 us (28%)
  local copies, waits for them, and re-layouts  6.18 us (4%)
    all_to_all x1, waiting for transfers between devices, on_device(): lax.all_to_all(outgoing, 'dom', split_axis=0, concat_axis=0, tiled=True)  27.3 us
    ppermute x13, starting transfers between devices, move(): return lax.ppermute(value, 'dom', pairs)  23.9 us
    all_to_all x1, starting transfers between devices, on_device(): lax.all_to_all(outgoing, 'dom', split_axis=0, concat_axis=0, tiled=True)  15.6 us
    pallas_call x1, Pallas kernels, dense(): pl.pallas_call(body, out_shape=(jax.ShapeDtypeStruct((rows // half, half,...  9.68 us
    all_to_all x1, starting transfers between devices, on_device(): lax.all_to_all(returned, 'dom', split_axis=0, concat_axis=0, tiled=True)  8.6 us
    pallas_call x1, Pallas kernels, scatter_rows(): pl.pallas_call(scatter_kernel, out_shape=jax.ShapeDtypeStruct((count, wid...  7.98 us
    pallas_call x1, Pallas kernels, spread_blocks(): pl.pallas_call(spread_kernel, out_shape=(jax.ShapeDtypeStruct((blocks, ti...  7.87 us
    ppermute x13, waiting for transfers between devices, move(): return lax.ppermute(value, 'dom', pairs)  7.85 us
  transfers between devices with their start and end apart: 19, of which 7 were waited for; matrix products, arithmetic and copies ran while one was open for 3% of the time, Pallas kernels for 11%

profile of v4, /device:TPU:2, one launch (start us, length us, event | category | flops | bytes accessed | tf_op | source)
XLA Modules:
  0.0 141.1 jit_solution(3871793505292141027)
XLA Ops:
  0.7 7.4 %gather_rows.1 = bf16[4096,128]{1,0:T(8,128)(2,1)} custom-call(s32[32,128]{1,0:T(8,128)} %bitcast.28, bf16[4096,128]{1,0:T(8,128)(2,1)} %feats_hbm.1), custom_call_target="tpu_custom_call" | custom-call | bytes 8388608 | tf_op jit(solution)/shard_map/gather_rows/pallas_call | solution.py:61
  8.1 15.6 %all-to-all-start = ((bf16[128,32,128]{2,1,0:T(8,128)(2,1)}), bf16[128,32,128]{2,1,0:T(8,128)(2,1)S(1)}, u32[]{:S(2)}, u32[]{:S(2)}) async-start(bf16[128,32,128]{2,1,0:T(8,128)(2,1)} %bitcast.1), calls=%async_computation | async-start | bytes 2097152 | tf_op jit(solution)/shard_map/all_to_all | solution.py:392
  25.7 27.3 %all-to-all-done = bf16[128,32,128]{2,1,0:T(8,128)(2,1)S(1)} async-done(((bf16[128,32,128]{2,1,0:T(8,128)(2,1)}), bf16[128,32,128]{2,1,0:T(8,128)(2,1)S(1)}, u32[]{:S(2)}, u32[]{:S(2)}) %all-to-all-start) | async-done | bytes 1048608 | tf_op jit(solution)/shard_map/all_to_all | solution.py:392
  53.1 5.3 %aggregate_blocks.1 = bf16[32,128,128]{2,1,0:T(8,128)(2,1)S(1)} custom-call(s32[8,32]{1,0:T(8,128)S(1)} %bitcast.25, bf16[32,128,128]{2,1,0:T(8,128)(2,1)S(1)} %bitcast.21, bf16[32,128,128]{2,1,0:T(8,128)(2,1)S(1)} %bitcast.22, bf16[256,128,128]{2,1,0:T(8,128)(2,1)} %adj.3), custom_call_target="tpu_custom_call" | custom-call | flops 1073741824 | bytes 12582912 | tf_op jit(solution)/shard_map/aggregate_blocks/pallas_call | solution.py:107
  59.5 1.6 %collective-permute-done.2.refs_2_ = bf16[4096,128]{1,0:T(8,128)(2,1)S(1)} collective-permute-done((bf16[4096,128]{1,0:T(8,128)(2,1)S(1)}, bf16[4096,128]{1,0:T(8,128)(2,1)S(1)}, u32[]{:S(2)}, u32[]{:S(2)}) %collective-permute-start.2) | collective-permute-done | bytes 1048608 | tf_op jit(solution)/shard_map/ppermute | solution.py:426
  63.0 1.2 copy-done.5
  64.2 9.7 %dense.1 = (bf16[32,128,128]{2,1,0:T(8,128)(2,1)S(1)}, f32[448,128]{1,0:T(8,128)}) custom-call(s32[2]{0:T(128)S(1)} %pad_add_fusion.refs_0_.ids, bf16[4096,128]{1,0:T(8,128)(2,1)S(1)} %bitcast.24, bf16[4096,128]{1,0:T(8,128)(2,1)S(1)} %copy-done.5, bf16[256,256]{1,0:T(8,128)(2,1)S(1)} %maximum_bitcast_fusion.refs_3_, bf16[128,256]{1,0:T(8,128)(2,1)S(1)} %copy-done.2, ...), custom_call_target="tpu_custom_call" | custom-call | flops 5368709120 | bytes 4194304 | tf_op jit(solution)/shard_map/dense/pallas_call | solution.py:183
  73.9 4.0 %all-to-all-start.1 = ((f32[8,56,128]{2,1,0:T(8,128)}), f32[8,56,128]{2,1,0:T(8,128)S(1)}, u32[]{:S(2)}, u32[]{:S(2)}) async-start(f32[8,56,128]{2,1,0:T(8,128)} %bitcast.10), calls=%async_computation.1 | async-start | bytes 458752 | tf_op jit(solution)/shard_map/all_to_all | solution.py:335
  77.9 7.9 %spread_blocks.1 = (bf16[32,128,128]{2,1,0:T(8,128)(2,1)}, f32[32,128,128]{2,1,0:T(8,128)}) custom-call(s32[8,32]{1,0:T(8,128)S(1)} %bitcast.26, bf16[32,128,128]{2,1,0:T(8,128)(2,1)S(1)} %get-tuple-element.51.grads, bf16[256,128,128]{2,1,0:T(8,128)(2,1)} %adj.3), custom_call_target="tpu_custom_call" | custom-call | flops 1073741824 | bytes 12582912 | tf_op jit(solution)/shard_map/spread_blocks/pallas_call | solution.py:237
  85.8 3.6 %all-to-all-done.1 = f32[8,56,128]{2,1,0:T(8,128)S(1)} async-done(((f32[8,56,128]{2,1,0:T(8,128)}), f32[8,56,128]{2,1,0:T(8,128)S(1)}, u32[]{:S(2)}, u32[]{:S(2)}) %all-to-all-start.1) | async-done | bytes 229408 | tf_op jit(solution)/shard_map/all_to_all | solution.py:335
  89.4 8.6 %all-to-all-start.2 = ((bf16[128,32,128]{2,1,0:T(8,128)(2,1)}), bf16[128,32,128]{2,1,0:T(8,128)(2,1)S(1)}, u32[]{:S(2)}, u32[]{:S(2)}) async-start(bf16[128,32,128]{2,1,0:T(8,128)(2,1)} %bitcast.11), calls=%async_computation.2 | async-start | bytes 2097152 | tf_op jit(solution)/shard_map/all_to_all | solution.py:435
  98.0 1.6 %collective-permute-start.5 = (f32[56,128]{1,0:T(8,128)S(1)}, f32[56,128]{1,0:T(8,128)S(1)}, u32[]{:S(2)}, u32[]{:S(2)}) collective-permute-start(f32[56,128]{1,0:T(8,128)S(1)} %reduce_sum.9), channel_id=1, source_target_pairs={{0,6},{2,4},{4,2},{6,0},{8,14},{10,12},{12,10},{14,8},{16,22},{18,... | collective-permute-start | bytes 86024 | tf_op jit(solution)/shard_map/ppermute | solution.py:313
  99.6 1.5 %collective-permute-start.4 = (f32[56,128]{1,0:T(8,128)S(1)}, f32[56,128]{1,0:T(8,128)S(1)}, u32[]{:S(2)}, u32[]{:S(2)}) collective-permute-start(f32[56,128]{1,0:T(8,128)S(1)} %reduce_sum.9), channel_id=1, source_target_pairs={{0,4},{2,6},{4,0},{6,2},{8,12},{10,14},{12,8},{14,10},{16,20},{18,... | collective-permute-start | bytes 86024 | tf_op jit(solution)/shard_map/ppermute | solution.py:313
  102.2 3.0 %collective-permute-done.4 = f32[56,128]{1,0:T(8,128)S(1)} collective-permute-done((f32[56,128]{1,0:T(8,128)S(1)}, f32[56,128]{1,0:T(8,128)S(1)}, u32[]{:S(2)}, u32[]{:S(2)}) %collective-permute-start.4) | collective-permute-done | bytes 28704 | tf_op jit(solution)/shard_map/ppermute | solution.py:313
  105.2 3.3 %collective-permute-start.8 = (f32[56,128]{1,0:T(8,128)S(1)}, f32[56,128]{1,0:T(8,128)S(1)}, u32[]{:S(2)}, u32[]{:S(2)}) collective-permute-start(f32[56,128]{1,0:T(8,128)S(1)} %add_add_fusion.1), channel_id=1, source_target_pairs={{0,192},{2,194},{4,196},{6,198},{8,200},{10,202},{12,204},{14,206}... | collective-permute-start | bytes 86024 | tf_op jit(solution)/shard_map/ppermute | solution.py:313
  110.7 3.7 %collective-permute-done.7 = f32[56,128]{1,0:T(8,128)S(1)} collective-permute-done((f32[56,128]{1,0:T(8,128)S(1)}, f32[56,128]{1,0:T(8,128)S(1)}, u32[]{:S(2)}, u32[]{:S(2)}) %collective-permute-start.7) | collective-permute-done | bytes 28704 | tf_op jit(solution)/shard_map/ppermute | solution.py:313
  114.3 2.9 %collective-permute-start.15 = (f32[56,128]{1,0:T(8,128)S(1)}, f32[56,128]{1,0:T(8,128)S(1)}, u32[]{:S(2)}, u32[]{:S(2)}) collective-permute-start(f32[56,128]{1,0:T(8,128)S(1)} %add_add_fusion.refs_0_), channel_id=1, source_target_pairs={{0,56},{2,58},{4,60},{6,62},{8,0},{10,2},{12,4},{14,6},{16,8},{18,... | collective-permute-start | bytes 86024 | tf_op jit(solution)/shard_map/ppermute | solution.py:313
  117.3 2.4 %collective-permute-start.14 = (f32[56,128]{1,0:T(8,128)S(1)}, f32[56,128]{1,0:T(8,128)S(1)}, u32[]{:S(2)}, u32[]{:S(2)}) collective-permute-start(f32[56,128]{1,0:T(8,128)S(1)} %add_add_fusion.refs_0_), channel_id=1, source_target_pairs={{0,48},{2,50},{4,52},{6,54},{8,56},{10,58},{12,60},{14,62},{16,0},... | collective-permute-start | bytes 86024 | tf_op jit(solution)/shard_map/ppermute | solution.py:313
  119.6 1.2 collective-permute-start.13
  120.8 4.1 %collective-permute-start.12 = (f32[56,128]{1,0:T(8,128)S(1)}, f32[56,128]{1,0:T(8,128)S(1)}, u32[]{:S(2)}, u32[]{:S(2)}) collective-permute-start(f32[56,128]{1,0:T(8,128)S(1)} %add_add_fusion.refs_0_), channel_id=1, source_target_pairs={{0,32},{2,34},{4,36},{6,38},{8,40},{10,42},{12,44},{14,46},{16,48}... | collective-permute-start | bytes 86024 | tf_op jit(solution)/shard_map/ppermute | solution.py:313
  125.0 3.7 %collective-permute-start.10 = (f32[56,128]{1,0:T(8,128)S(1)}, f32[56,128]{1,0:T(8,128)S(1)}, u32[]{:S(2)}, u32[]{:S(2)}) collective-permute-start(f32[56,128]{1,0:T(8,128)S(1)} %add_add_fusion.refs_0_), channel_id=1, source_target_pairs={{0,16},{2,18},{4,20},{6,22},{8,24},{10,26},{12,28},{14,30},{16,32}... | collective-permute-start | bytes 86024 | tf_op jit(solution)/shard_map/ppermute | solution.py:313
  129.8 1.9 %copy.16 = f32[32,128,128]{2,1,0:T(8,128)S(1)} copy(f32[32,128,128]{1,2,0:T(8,128)} %bitcast.27) | data formatting | bytes 4194304 | tf_op jit(solution)/shard_map/transpose | solution.py:436
  131.7 8.0 %scatter_rows.1 = bf16[4096,128]{1,0:T(8,128)(2,1)} custom-call(s32[32,128]{1,0:T(8,128)} %bitcast.29, bf16[4096,128]{1,0:T(8,128)(2,1)S(1)} %bitcast.20, f32[4096,128]{1,0:T(8,128)S(1)} %bitcast.19), custom_call_target="tpu_custom_call" | custom-call | bytes 8388608 | tf_op jit(solution)/shard_map/scatter_rows/pallas_call | solution.py:286
  139.8 1.3 finish.1
  (51 shorter events, 9.4 us)
Async XLA Ops:
  0.6 23.1 %copy-start.1 = (bf16[128,256]{1,0:T(8,128)(2,1)S(1)}, bf16[128,256]{1,0:T(8,128)(2,1)}, u32[]{:S(2)}) copy-start(bf16[128,256]{1,0:T(8,128)(2,1)} %refs_4_) | copy-start | bytes 196612
  0.7 23.9 %copy-start.7 = (s32[4096]{0:T(1024)S(1)}, s32[4096]{0:T(1024)}, u32[]{:S(2)}) copy-start(s32[4096]{0:T(1024)} %param.15) | copy-start | bytes 49156
  8.0 44.9 %copy-start.8 = (f32[256]{0:T(256)S(1)}, f32[256]{0:T(256)}, u32[]{:S(2)}) copy-start(f32[256]{0:T(256)} %param.13) | copy-start | bytes 3076
  8.0 45.0 %copy-start = (bf16[4096,128]{1,0:T(8,128)(2,1)S(1)}, bf16[4096,128]{1,0:T(8,128)(2,1)}, u32[]{:S(2)}) copy-start(bf16[4096,128]{1,0:T(8,128)(2,1)} %feats_hbm.1) | copy-start | bytes 3145732
  8.1 45.0 %copy-start.3 = (s32[32,8]{0,1:T(8,128)S(1)}, s32[32,8]{0,1:T(8,128)}, u32[]{:S(2)}) copy-start(s32[32,8]{0,1:T(8,128)} %param.10) | copy-start | bytes 3076
  8.1 44.9 %all-to-all-start = ((bf16[128,32,128]{2,1,0:T(8,128)(2,1)}), bf16[128,32,128]{2,1,0:T(8,128)(2,1)S(1)}, u32[]{:S(2)}, u32[]{:S(2)}) async-start(bf16[128,32,128]{2,1,0:T(8,128)(2,1)} %bitcast.1), calls=%async_computation | async-start | bytes 2097152 | tf_op jit(solution)/shard_map/all_to_all | solution.py:392
  23.7 1.3 collective-permute-start.1
  23.9 1.8 %collective-permute-start = (bf16[128,256]{0,1:T(8,128)(2,1)S(1)}, bf16[128,256]{0,1:T(8,128)(2,1)S(1)}, u32[]{:S(2)}, u32[]{:S(2)}) collective-permute-start(bf16[128,256]{0,1:T(8,128)(2,1)S(1)} %copy.13), channel_id=1, source_target_pairs={{0,1},{1,0},{2,3},{3,2},{4,5},{5,4},{6,7},{7,6},{8,9},{9,8},{10,11... | collective-permute-start | bytes 196616 | tf_op jit(solution)/shard_map/ppermute | solution.py:401
  58.4 2.7 %collective-permute-start.2 = (bf16[4096,128]{1,0:T(8,128)(2,1)S(1)}, bf16[4096,128]{1,0:T(8,128)(2,1)S(1)}, u32[]{:S(2)}, u32[]{:S(2)}) collective-permute-start(bf16[4096,128]{1,0:T(8,128)(2,1)S(1)} %bitcast.23), channel_id=1, source_target_pairs={{0,1},{1,0},{2,3},{3,2},{4,5},{5,4},{6,7},{7,6},{8,9},{9,8},{10,11... | collective-permute-start | bytes 3145736 | tf_op jit(solution)/shard_map/ppermute | solution.py:426
  73.9 15.5 %all-to-all-start.1 = ((f32[8,56,128]{2,1,0:T(8,128)}), f32[8,56,128]{2,1,0:T(8,128)S(1)}, u32[]{:S(2)}, u32[]{:S(2)}) async-start(f32[8,56,128]{2,1,0:T(8,128)} %bitcast.10), calls=%async_computation.1 | async-start | bytes 458752 | tf_op jit(solution)/shard_map/all_to_all | solution.py:335
  89.4 42.3 %all-to-all-start.2 = ((bf16[128,32,128]{2,1,0:T(8,128)(2,1)}), bf16[128,32,128]{2,1,0:T(8,128)(2,1)S(1)}, u32[]{:S(2)}, u32[]{:S(2)}) async-start(bf16[128,32,128]{2,1,0:T(8,128)(2,1)} %bitcast.11), calls=%async_computation.2 | async-start | bytes 2097152 | tf_op jit(solution)/shard_map/all_to_all | solution.py:435
  98.0 4.2 %collective-permute-start.5 = (f32[56,128]{1,0:T(8,128)S(1)}, f32[56,128]{1,0:T(8,128)S(1)}, u32[]{:S(2)}, u32[]{:S(2)}) collective-permute-start(f32[56,128]{1,0:T(8,128)S(1)} %reduce_sum.9), channel_id=1, source_target_pairs={{0,6},{2,4},{4,2},{6,0},{8,14},{10,12},{12,10},{14,8},{16,22},{18,... | collective-permute-start | bytes 86024 | tf_op jit(solution)/shard_map/ppermute | solution.py:313
  99.6 5.7 %collective-permute-start.4 = (f32[56,128]{1,0:T(8,128)S(1)}, f32[56,128]{1,0:T(8,128)S(1)}, u32[]{:S(2)}, u32[]{:S(2)}) collective-permute-start(f32[56,128]{1,0:T(8,128)S(1)} %reduce_sum.9), channel_id=1, source_target_pairs={{0,4},{2,6},{4,0},{6,2},{8,12},{10,14},{12,8},{14,10},{16,20},{18,... | collective-permute-start | bytes 86024 | tf_op jit(solution)/shard_map/ppermute | solution.py:313
  101.1 4.2 %collective-permute-start.3 = (f32[56,128]{1,0:T(8,128)S(1)}, f32[56,128]{1,0:T(8,128)S(1)}, u32[]{:S(2)}, u32[]{:S(2)}) collective-permute-start(f32[56,128]{1,0:T(8,128)S(1)} %reduce_sum.9), channel_id=1, source_target_pairs={{0,2},{2,0},{4,6},{6,4},{8,10},{10,8},{12,14},{14,12},{16,18},{18,... | collective-permute-start | bytes 86024 | tf_op jit(solution)/shard_map/ppermute | solution.py:313
  105.2 5.4 %collective-permute-start.8 = (f32[56,128]{1,0:T(8,128)S(1)}, f32[56,128]{1,0:T(8,128)S(1)}, u32[]{:S(2)}, u32[]{:S(2)}) collective-permute-start(f32[56,128]{1,0:T(8,128)S(1)} %add_add_fusion.1), channel_id=1, source_target_pairs={{0,192},{2,194},{4,196},{6,198},{8,200},{10,202},{12,204},{14,206}... | collective-permute-start | bytes 86024 | tf_op jit(solution)/shard_map/ppermute | solution.py:313
  108.6 5.8 %collective-permute-start.7 = (f32[56,128]{1,0:T(8,128)S(1)}, f32[56,128]{1,0:T(8,128)S(1)}, u32[]{:S(2)}, u32[]{:S(2)}) collective-permute-start(f32[56,128]{1,0:T(8,128)S(1)} %add_add_fusion.1), channel_id=1, source_target_pairs={{0,128},{2,130},{4,132},{6,134},{8,136},{10,138},{12,140},{14,142}... | collective-permute-start | bytes 86024 | tf_op jit(solution)/shard_map/ppermute | solution.py:313
  109.0 5.3 %collective-permute-start.6 = (f32[56,128]{1,0:T(8,128)S(1)}, f32[56,128]{1,0:T(8,128)S(1)}, u32[]{:S(2)}, u32[]{:S(2)}) collective-permute-start(f32[56,128]{1,0:T(8,128)S(1)} %add_add_fusion.1), channel_id=1, source_target_pairs={{0,64},{2,66},{4,68},{6,70},{8,72},{10,74},{12,76},{14,78},{16,80}... | collective-permute-start | bytes 86024 | tf_op jit(solution)/shard_map/ppermute | solution.py:313
  114.3 10.6 %collective-permute-start.15 = (f32[56,128]{1,0:T(8,128)S(1)}, f32[56,128]{1,0:T(8,128)S(1)}, u32[]{:S(2)}, u32[]{:S(2)}) collective-permute-start(f32[56,128]{1,0:T(8,128)S(1)} %add_add_fusion.refs_0_), channel_id=1, source_target_pairs={{0,56},{2,58},{4,60},{6,62},{8,0},{10,2},{12,4},{14,6},{16,8},{18,... | collective-permute-start | bytes 86024 | tf_op jit(solution)/shard_map/ppermute | solution.py:313
  117.3 11.4 %collective-permute-start.14 = (f32[56,128]{1,0:T(8,128)S(1)}, f32[56,128]{1,0:T(8,128)S(1)}, u32[]{:S(2)}, u32[]{:S(2)}) collective-permute-start(f32[56,128]{1,0:T(8,128)S(1)} %add_add_fusion.refs_0_), channel_id=1, source_target_pairs={{0,48},{2,50},{4,52},{6,54},{8,56},{10,58},{12,60},{14,62},{16,0},... | collective-permute-start | bytes 86024 | tf_op jit(solution)/shard_map/ppermute | solution.py:313
  119.6 20.1 %collective-permute-start.13 = (f32[56,128]{1,0:T(8,128)S(1)}, f32[56,128]{1,0:T(8,128)S(1)}, u32[]{:S(2)}, u32[]{:S(2)}) collective-permute-start(f32[56,128]{1,0:T(8,128)S(1)} %add_add_fusion.refs_0_), channel_id=1, source_target_pairs={{0,40},{2,42},{4,44},{6,46},{8,48},{10,50},{12,52},{14,54},{16,56}... | collective-permute-start | bytes 86024 | tf_op jit(solution)/shard_map/ppermute | solution.py:313
  120.8 18.9 %collective-permute-start.12 = (f32[56,128]{1,0:T(8,128)S(1)}, f32[56,128]{1,0:T(8,128)S(1)}, u32[]{:S(2)}, u32[]{:S(2)}) collective-permute-start(f32[56,128]{1,0:T(8,128)S(1)} %add_add_fusion.refs_0_), channel_id=1, source_target_pairs={{0,32},{2,34},{4,36},{6,38},{8,40},{10,42},{12,44},{14,46},{16,48}... | collective-permute-start | bytes 86024 | tf_op jit(solution)/shard_map/ppermute | solution.py:313
  125.0 14.8 %collective-permute-start.11 = (f32[56,128]{1,0:T(8,128)S(1)}, f32[56,128]{1,0:T(8,128)S(1)}, u32[]{:S(2)}, u32[]{:S(2)}) collective-permute-start(f32[56,128]{1,0:T(8,128)S(1)} %add_add_fusion.refs_0_), channel_id=1, source_target_pairs={{0,24},{2,26},{4,28},{6,30},{8,32},{10,34},{12,36},{14,38},{16,40}... | collective-permute-start | bytes 86024 | tf_op jit(solution)/shard_map/ppermute | solution.py:313
  125.0 14.8 %collective-permute-start.10 = (f32[56,128]{1,0:T(8,128)S(1)}, f32[56,128]{1,0:T(8,128)S(1)}, u32[]{:S(2)}, u32[]{:S(2)}) collective-permute-start(f32[56,128]{1,0:T(8,128)S(1)} %add_add_fusion.refs_0_), channel_id=1, source_target_pairs={{0,16},{2,18},{4,20},{6,22},{8,24},{10,26},{12,28},{14,30},{16,32}... | collective-permute-start | bytes 86024 | tf_op jit(solution)/shard_map/ppermute | solution.py:313
  128.6 11.1 %collective-permute-start.9 = (f32[56,128]{1,0:T(8,128)S(1)}, f32[56,128]{1,0:T(8,128)S(1)}, u32[]{:S(2)}, u32[]{:S(2)}) collective-permute-start(f32[56,128]{1,0:T(8,128)S(1)} %add_add_fusion.refs_0_), channel_id=1, source_target_pairs={{0,8},{2,10},{4,12},{6,14},{8,16},{10,18},{12,20},{14,22},{16,24},... | collective-permute-start | bytes 86024 | tf_op jit(solution)/shard_map/ppermute | solution.py:313
  (4 other events, 26.1 us)

commit v5 on v4

--- a/solution.py
+++ b/solution.py
@@ -14,7 +14,7 @@
 NX, NY, NZ = 4, 4, 8
 PACKED = 448
 TILE_STEPS = 8
-SPAN = 512
+SPAN = 2048
 
 
 def contract(a, b, da, db):
@@ -25,14 +25,19 @@
     return pltpu.with_memory_space_constraint(value, pltpu.HBM)
 
 
-def gather_kernel(rows_hbm, feats_hbm, out, rows, feats, table, picked, row_sem, sems):
+def gather_kernel(rows_hbm, feats_hbm, out, rows, feats, table, picked, ready, row_sem, sems, out_sems):
     cap, peers = rows.shape
     count = feats.shape[0]
     part = count // sems.shape[0]
+    some = peers // out_sems.shape[0]
 
     def part_copy(i):
         span = pl.ds(i * part, part)
         return pltpu.make_async_copy(feats_hbm.at[span], feats.at[span], sems.at[i])
+
+    def out_copy(i):
+        span = pl.ds(i * some * cap, some * cap)
+        return pltpu.make_async_copy(ready.at[span], out.at[span], out_sems.at[i])
 
     row_copy = pltpu.make_async_copy(rows_hbm, rows, row_sem)
     row_copy.start()
@@ -51,8 +56,13 @@
             picked[pl.ds(base + c, 1), :] = table[pl.ds(rows[c, p], 1), :]
         return carry
 
-    lax.fori_loop(0, peers, one_peer, 0)
-    out[...] = picked[...].astype(BF16)
+    for i in range(out_sems.shape[0]):
+        lax.fori_loop(i * some, (i + 1) * some, one_peer, 0)
+        span = pl.ds(i * some * cap, some * cap)
+        ready[span, :] = picked[span, :].astype(BF16)
+        out_copy(i).start()
+    for i in range(out_sems.shape[0]):
+        out_copy(i).wait()
 
 
 def gather_rows(rows, feats):
@@ -60,15 +70,17 @@
     slots = rows.size
     return pl.pallas_call(
         gather_kernel,
-        out_shape=jax.ShapeDtypeStruct((slots, width), BF16),
+        out_shape=pltpu.HBM((slots, width), BF16),
         in_specs=[HBM, HBM],
-        out_specs=VMEM,
+        out_specs=HBM,
         scratch_shapes=[
             pltpu.SMEM(rows.shape, rows.dtype),
             pltpu.VMEM(feats.shape, BF16),
             pltpu.VMEM((count + 8, width), F32),
             pltpu.VMEM((slots, width), F32),
+            pltpu.VMEM((slots, width), BF16),
             pltpu.SemaphoreType.DMA,
+            pltpu.SemaphoreType.DMA((4,)),
             pltpu.SemaphoreType.DMA((4,)),
         ],
         compiler_params=pltpu.CompilerParams(vmem_limit_bytes=12 * MIB),
@@ -121,8 +133,9 @@
 
 
 def dense_kernel(
-    classes, total_nodes, ids, agg, other, weight_t, weight, cls, cls_t, bias, labels,
-    grad_out, packed, sum_w, sum_c, sum_b,
+    classes, total_nodes, ids, agg, other, weight, weight_o, class_t, class_o, bias_row, labels,
+    grad_out, packed,
+    sum_w, sum_c, sum_b, weight_t, cls_t, cls, bias,
 ):
     steps = labels.shape[0]
     class_rows = cls_t.shape[0]
@@ -134,6 +147,10 @@
             [jnp.where(first, mine, theirs), jnp.where(first, theirs, mine)], dim
         )
 
+    weight_t[...] = both(weight[...], weight_o[...], 0).T
+    cls_t[...] = both(class_t[...], class_o[...], 1)
+    cls[...] = cls_t[...].T
+    bias[...] = jnp.broadcast_to(bias_row[...], (128, 2 * half)).T
     sum_w[...] = jnp.zeros_like(sum_w)
     sum_c[...] = jnp.zeros_like(sum_c)
     sum_b[...] = jnp.zeros_like(sum_b)
@@ -148,7 +165,7 @@
         logits = contract(cls_t[...], hidden, 1, 0)
         logits = jnp.where(class_id < classes, logits, -jnp.inf)
         powers = jnp.exp(logits - jnp.max(logits, 0, keepdims=True))
-        share = powers / jnp.sum(powers, 0, keepdims=True)
+        share = powers * (1.0 / jnp.sum(powers, 0, keepdims=True))
         label = labels[pl.ds(i, 1), :]
         logit_grad = (share - jnp.where(class_id == label, 1.0, 0.0)).astype(BF16)
         hidden_grad = contract(cls[...], logit_grad, 1, 0)
@@ -171,11 +188,11 @@
     packed[pl.ds(units + class_rows + 8, 8), :] = sum_b[:, half:] * scale
 
 
-def dense(ids, agg, other, weight_t, weight, cls, cls_t, bias, labels, classes, total_nodes):
+def dense(ids, agg, other, weight, weight_o, class_t, class_o, bias_row, labels, classes, total_nodes):
     rows, half = agg.shape
     units = weight.shape[1]
     steps = rows // SPAN
-    class_rows = cls_t.shape[0]
+    class_rows = class_t.shape[0]
 
     def body(*refs):
         dense_kernel(classes, total_nodes, *refs)
@@ -192,11 +209,15 @@
             pltpu.VMEM((units, half), F32),
             pltpu.VMEM((class_rows, half), F32),
             pltpu.VMEM((8, units), F32),
+            pltpu.VMEM((units, 2 * half), BF16),
+            pltpu.VMEM((class_rows, units), BF16),
+            pltpu.VMEM((units, class_rows), BF16),
+            pltpu.VMEM((units, 128), F32),
         ],
-        compiler_params=pltpu.CompilerParams(vmem_limit_bytes=16 * MIB),
+        compiler_params=pltpu.CompilerParams(vmem_limit_bytes=32 * MIB),
         cost_estimate=pl.CostEstimate(flops=5 << 30, bytes_accessed=4 * MIB, transcendentals=1 << 20),
         name="dense",
-    )(ids, agg, other, weight_t, weight, cls, cls_t, bias, labels)
+    )(ids, agg, other, weight, weight_o, class_t, class_o, bias_row, labels)
 
 
 def spread_kernel(cols, grads, adj, halo_out, own_out, ext_grad, tiles, sems, own_sem):
@@ -254,7 +275,7 @@
     )(cols, grads, in_hbm(adj))
 
 
-def scatter_kernel(rows_hbm, arrived, own, out, rows, values, row_sem, *sums):
+def scatter_kernel(rows_hbm, arrived, own, out, rows, values, ready, row_sem, out_sems, *sums):
     cap, peers = rows.shape
     count, width = out.shape
     row_copy = pltpu.make_async_copy(rows_hbm, rows, row_sem)
@@ -274,10 +295,21 @@
         return carry
 
     lax.fori_loop(0, peers, one_peer, 0)
-    result = sums[0][pl.ds(0, count), :]
-    for total in sums[1:]:
-        result = result + total[pl.ds(0, count), :]
-    out[...] = result.astype(BF16)
+    part = count // out_sems.shape[0]
+
+    def out_copy(i):
+        span = pl.ds(i * part, part)
+        return pltpu.make_async_copy(ready.at[span], out.at[span], out_sems.at[i])
+
+    for i in range(out_sems.shape[0]):
+        span = pl.ds(i * part, part)
+        result = sums[0][span, :]
+        for total in sums[1:]:
+            result = result + total[span, :]
+        ready[span, :] = result.astype(BF16)
+        out_copy(i).start()
+    for i in range(out_sems.shape[0]):
+        out_copy(i).wait()
 
 
 def scatter_rows(rows, arrived, own):
@@ -285,13 +317,15 @@
     lanes = 8
     return pl.pallas_call(
         scatter_kernel,
-        out_shape=jax.ShapeDtypeStruct((count, width), BF16),
+        out_shape=pltpu.HBM((count, width), BF16),
         in_specs=[HBM, VMEM, VMEM],
-        out_specs=VMEM,
+        out_specs=HBM,
         scratch_shapes=[
             pltpu.SMEM(rows.shape, rows.dtype),
             pltpu.VMEM(arrived.shape, F32),
+            pltpu.VMEM((count, width), BF16),
             pltpu.SemaphoreType.DMA,
+            pltpu.SemaphoreType.DMA((4,)),
         ]
         + [pltpu.VMEM((count + 8, width), F32)] * lanes,
         compiler_params=pltpu.CompilerParams(vmem_limit_bytes=32 * MIB),
@@ -337,10 +371,8 @@
     )
 
 
-def sum_xy(mine):
-    for axis in ("x", "y"):
-        mine = add_pairs([mine] + [across(mine, axis, flip) for flip in (1, 2, 3)])
-    return mine
+def sum_along(mine, axis):
+    return add_pairs([mine] + [across(mine, axis, flip) for flip in (1, 2, 3)])
 
 
 def finish(ids, mine, grad_feats, classes, units):
@@ -391,32 +423,20 @@
     outgoing = gather_rows(rows, feats).reshape(peers, cap, half)
     incoming = lax.all_to_all(outgoing, "dom", split_axis=0, concat_axis=0, tiled=True)
 
-    weight_l, cls_l, bias_l, labels_l, adj_cols, _ = lax.optimization_barrier(
+    weight, cls_w, bias, labels, adj_cols, _ = lax.optimization_barrier(
         (weight, cls_w, bias, labels, adj_cols, outgoing)
     )
     cols = adj_cols.T
-    hid = lax.axis_index("hid")
     dom = lax.axis_index("dom")
-    ids = jnp.stack([hid, (dom // NX) % NZ]).astype(jnp.int32)
-    weight_o = lax.ppermute(weight_l, "hid", swap)
-    cls_o = lax.ppermute(cls_l, "hid", swap)
-    first = hid == 0
-    weight_full = jnp.concatenate(
-        [jnp.where(first, weight_l, weight_o), jnp.where(first, weight_o, weight_l)], 0
-    )
-    cls_full = jnp.concatenate(
-        [jnp.where(first, cls_l, cls_o), jnp.where(first, cls_o, cls_l)], 0
-    )
-    class_rows = -(-classes // 8) * 8
-    cls_full = jnp.pad(cls_full, ((0, 0), (0, class_rows - classes)))
-    bias_wide = jnp.broadcast_to(bias_l[:, None], (units, 128))
-    label_rows = labels_l.reshape(row_count // SPAN, SPAN)
-
-    weight_t = weight_full.T
-    cls_t = cls_full.T
-    incoming, cols, ids, weight_t, weight_l, cls_full, cls_t, bias_wide, label_rows = (
+    ids = jnp.stack([lax.axis_index("hid"), dom // NX % NZ]).astype(jnp.int32)
+    class_t = jnp.pad(cls_w.T, ((0, -classes % 16), (0, 0)))
+    weight_o = lax.ppermute(weight, "hid", swap)
+    class_o = lax.ppermute(class_t, "hid", swap)
+    bias_row = bias[None, :]
+    label_rows = labels.reshape(row_count // SPAN, SPAN)
+    incoming, cols, ids, weight, weight_o, class_t, class_o, bias_row, label_rows = (
         lax.optimization_barrier(
-            (incoming, cols, ids, weight_t, weight_l, cls_full, cls_t, bias_wide, label_rows)
+            (incoming, cols, ids, weight, weight_o, class_t, class_o, bias_row, label_rows)
         )
     )
 
@@ -425,7 +445,7 @@
     agg = agg.reshape(row_count, half)
     other = lax.ppermute(agg, "hid", swap)
     grads, packed = dense(
-        ids, agg, other, weight_t, weight_l, cls_full, cls_t, bias_wide, label_rows,
+        ids, agg, other, weight, weight_o, class_t, class_o, bias_row, label_rows,
         classes, total_nodes,
     )
     halo_grad, own_grad = spread_blocks(cols, grads, adj_tiles)
@@ -433,9 +453,12 @@
     halo_grad, own_grad, shares = lax.optimization_barrier((halo_grad, own_grad, shares))
     returned = halo_grad.reshape(peers, cap, half)
     arrived = lax.all_to_all(returned, "dom", split_axis=0, concat_axis=0, tiled=True)
+    share = sum_along(shares.sum(0), "x")
     own = jnp.swapaxes(own_grad, 1, 2).reshape(row_count, half)
+    share, own = lax.optimization_barrier((share, own))
+    share = sum_along(share, "y")
     grad_feats = scatter_rows(rows, arrived.reshape(row_count, half), own)
-    return finish(ids, sum_xy(shares.sum(0)), grad_feats, classes, units)
+    return finish(ids, share, grad_feats, classes, units)
 
 
 def solution(mesh):

time: 142 us -> 133 us (0.937)
  local copies, waits for them, and re-layouts: 6.18 us -> 1.96 us
  Pallas kernels: 39.6 us -> 35.4 us
    pallas_call x1, Pallas kernels: 9.68 us -> 5.95 us  [dense(): pl.pallas_call(body, out_shape=(jax.ShapeDtypeStruct((rows // half, half,...]
    unnamed x18 -> x12, local copies, waits for them, and re-layouts: 3.07 us -> 0.02 us
    ppermute x13, waiting for transfers between devices: 7.85 us -> 5.86 us  [move(): return lax.ppermute(value, 'dom', pairs)]
  transfers between devices with their start and end apart: 19 -> 19, of which waited for: 7 -> 8; matrix products, arithmetic and copies ran while one was open for 3% -> 2% of each run, Pallas kernels for 11% -> 12%
where the time goes in v5:
time: 133 us; the launch traced here: 132 us
  starting transfers between devices  52.6 us (40%)
  waiting for transfers between devices  40.7 us (31%)
  Pallas kernels  35.4 us (27%)
  local copies, waits for them, and re-layouts  1.96 us (1%)
    all_to_all x1, waiting for transfers between devices, on_device(): lax.all_to_all(outgoing, 'dom', split_axis=0, concat_axis=0, tiled=True)  27.8 us
    ppermute x13, starting transfers between devices, move(): return lax.ppermute(value, 'dom', pairs)  23.9 us
    all_to_all x1, starting transfers between devices, on_device(): lax.all_to_all(outgoing, 'dom', split_axis=0, concat_axis=0, tiled=True)  15.4 us
    all_to_all x1, starting transfers between devices, on_device(): lax.all_to_all(returned, 'dom', split_axis=0, concat_axis=0, tiled=True)  8.58 us
    pallas_call x1, Pallas kernels, spread_blocks(): pl.pallas_call(spread_kernel, out_shape=(jax.ShapeDtypeStruct((blocks, ti...  7.86 us
    pallas_call x1, Pallas kernels, scatter_rows(): pl.pallas_call(scatter_kernel, out_shape=pltpu.HBM((count, width), BF16),...  7.75 us
    pallas_call x1, Pallas kernels, gather_rows(): pl.pallas_call(gather_kernel, out_shape=pltpu.HBM((slots, width), BF16),...  7.2 us
    pallas_call x1, Pallas kernels, dense(): pl.pallas_call(body, out_shape=(jax.ShapeDtypeStruct((rows // half, half,...  5.95 us
  transfers between devices with their start and end apart: 19, of which 8 were waited for; matrix products, arithmetic and copies ran while one was open for 2% of the time, Pallas kernels for 12%

profile of v5, /device:TPU:2, one launch (start us, length us, event | category | flops | bytes accessed | tf_op | source)
XLA Modules:
  0.0 131.6 jit_solution(10953274982388874522)
XLA Ops:
  0.7 7.2 %gather_rows.1 = bf16[4096,128]{1,0:T(8,128)(2,1)} custom-call(s32[32,128]{1,0:T(8,128)} %bitcast.28, bf16[4096,128]{1,0:T(8,128)(2,1)} %feats_hbm.1), custom_call_target="tpu_custom_call" | custom-call | bytes 8388608 | tf_op jit(solution)/shard_map/gather_rows/pallas_call | solution.py:71
  7.9 15.4 %all-to-all-start = ((bf16[128,32,128]{2,1,0:T(8,128)(2,1)}), bf16[128,32,128]{2,1,0:T(8,128)(2,1)S(1)}, u32[]{:S(2)}, u32[]{:S(2)}) async-start(bf16[128,32,128]{2,1,0:T(8,128)(2,1)} %bitcast.26), calls=%async_computation | async-start | bytes 2097152 | tf_op jit(solution)/shard_map/all_to_all | solution.py:424
  24.9 27.8 %all-to-all-done = bf16[128,32,128]{2,1,0:T(8,128)(2,1)S(1)} async-done(((bf16[128,32,128]{2,1,0:T(8,128)(2,1)}), bf16[128,32,128]{2,1,0:T(8,128)(2,1)S(1)}, u32[]{:S(2)}, u32[]{:S(2)}) %all-to-all-start) | async-done | bytes 1048608 | tf_op jit(solution)/shard_map/all_to_all | solution.py:424
  52.6 5.3 %aggregate_blocks.1 = bf16[32,128,128]{2,1,0:T(8,128)(2,1)S(1)} custom-call(s32[8,32]{1,0:T(8,128)S(1)} %bitcast.23, bf16[32,128,128]{2,1,0:T(8,128)(2,1)S(1)} %bitcast.19, bf16[32,128,128]{2,1,0:T(8,128)(2,1)S(1)} %bitcast.20, bf16[256,128,128]{2,1,0:T(8,128)(2,1)} %adj.3), custom_call_target="tpu_custom_call" | custom-call | flops 1073741824 | bytes 12582912 | tf_op jit(solution)/shard_map/aggregate_blocks/pallas_call | solution.py:119
  58.1 2.6 %collective-permute-done.2.refs_2_ = bf16[4096,128]{1,0:T(8,128)(2,1)S(1)} collective-permute-done((bf16[4096,128]{1,0:T(8,128)(2,1)S(1)}, bf16[4096,128]{1,0:T(8,128)(2,1)S(1)}, u32[]{:S(2)}, u32[]{:S(2)}) %collective-permute-start.2) | collective-permute-done | bytes 1048608 | tf_op jit(solution)/shard_map/ppermute | solution.py:446
  60.7 6.0 %dense.1 = (bf16[32,128,128]{2,1,0:T(8,128)(2,1)S(1)}, f32[448,128]{1,0:T(8,128)}) custom-call(s32[2]{0:T(128)S(1)} %pad_add_fusion.refs_0_.ids, bf16[4096,128]{1,0:T(8,128)(2,1)S(1)} %bitcast.22, bf16[4096,128]{1,0:T(8,128)(2,1)S(1)} %collective-permute-done.2.refs_2_, bf16[128,256]{1,0:T(8,128)(2,1)S(1)} %copy-done.2, ...), custom_call_target="tpu_custom_call" | custom-call | flops 5368709120 | bytes 4194304 | tf_op jit(solution)/shard_map/dense/pallas_call | solution.py:200
  66.7 4.0 %all-to-all-start.1 = ((f32[8,56,128]{2,1,0:T(8,128)}), f32[8,56,128]{2,1,0:T(8,128)S(1)}, u32[]{:S(2)}, u32[]{:S(2)}) async-start(f32[8,56,128]{2,1,0:T(8,128)} %bitcast.10), calls=%async_computation.1 | async-start | bytes 458752 | tf_op jit(solution)/shard_map/all_to_all | solution.py:369
  70.7 7.9 %spread_blocks.1 = (bf16[32,128,128]{2,1,0:T(8,128)(2,1)}, f32[32,128,128]{2,1,0:T(8,128)}) custom-call(s32[8,32]{1,0:T(8,128)S(1)} %bitcast.24, bf16[32,128,128]{2,1,0:T(8,128)(2,1)S(1)} %get-tuple-element.53.grads, bf16[256,128,128]{2,1,0:T(8,128)(2,1)} %adj.3), custom_call_target="tpu_custom_call" | custom-call | flops 1073741824 | bytes 12582912 | tf_op jit(solution)/shard_map/spread_blocks/pallas_call | solution.py:258
  78.6 3.6 %all-to-all-done.1 = f32[8,56,128]{2,1,0:T(8,128)S(1)} async-done(((f32[8,56,128]{2,1,0:T(8,128)}), f32[8,56,128]{2,1,0:T(8,128)S(1)}, u32[]{:S(2)}, u32[]{:S(2)}) %all-to-all-start.1) | async-done | bytes 229408 | tf_op jit(solution)/shard_map/all_to_all | solution.py:369
  82.2 8.6 %all-to-all-start.2 = ((bf16[128,32,128]{2,1,0:T(8,128)(2,1)}), bf16[128,32,128]{2,1,0:T(8,128)(2,1)S(1)}, u32[]{:S(2)}, u32[]{:S(2)}) async-start(bf16[128,32,128]{2,1,0:T(8,128)(2,1)} %bitcast.13), calls=%async_computation.2 | async-start | bytes 2097152 | tf_op jit(solution)/shard_map/all_to_all | solution.py:455
  90.8 1.6 %collective-permute-start.5 = (f32[56,128]{1,0:T(8,128)S(1)}, f32[56,128]{1,0:T(8,128)S(1)}, u32[]{:S(2)}, u32[]{:S(2)}) collective-permute-start(f32[56,128]{1,0:T(8,128)S(1)} %reduce_sum.9), channel_id=1, source_target_pairs={{0,6},{2,4},{4,2},{6,0},{8,14},{10,12},{12,10},{14,8},{16,22},{18,... | collective-permute-start | bytes 86024 | tf_op jit(solution)/shard_map/ppermute | solution.py:347
  92.3 1.5 %collective-permute-start.4 = (f32[56,128]{1,0:T(8,128)S(1)}, f32[56,128]{1,0:T(8,128)S(1)}, u32[]{:S(2)}, u32[]{:S(2)}) collective-permute-start(f32[56,128]{1,0:T(8,128)S(1)} %reduce_sum.9), channel_id=1, source_target_pairs={{0,4},{2,6},{4,0},{6,2},{8,12},{10,14},{12,8},{14,10},{16,20},{18,... | collective-permute-start | bytes 86024 | tf_op jit(solution)/shard_map/ppermute | solution.py:347
  93.8 1.1 collective-permute-start.3
  95.0 1.9 %copy.12 = f32[32,128,128]{2,1,0:T(8,128)S(1)} copy(f32[32,128,128]{1,2,0:T(8,128)} %bitcast.27) | data formatting | bytes 4194304 | tf_op jit(solution)/shard_map/transpose | solution.py:457
  98.0 3.5 %collective-permute-start.8 = (f32[56,128]{1,0:T(8,128)S(1)}, f32[56,128]{1,0:T(8,128)S(1)}, u32[]{:S(2)}, u32[]{:S(2)}) collective-permute-start(f32[56,128]{1,0:T(8,128)S(1)} %add_add_fusion.1), channel_id=1, source_target_pairs={{0,192},{2,194},{4,196},{6,198},{8,200},{10,202},{12,204},{14,206}... | collective-permute-start | bytes 86024 | tf_op jit(solution)/shard_map/ppermute | solution.py:347
  103.6 3.6 %collective-permute-done.7 = f32[56,128]{1,0:T(8,128)S(1)} collective-permute-done((f32[56,128]{1,0:T(8,128)S(1)}, f32[56,128]{1,0:T(8,128)S(1)}, u32[]{:S(2)}, u32[]{:S(2)}) %collective-permute-start.7) | collective-permute-done | bytes 28704 | tf_op jit(solution)/shard_map/ppermute | solution.py:347
  107.3 2.8 %collective-permute-start.15 = (f32[56,128]{1,0:T(8,128)S(1)}, f32[56,128]{1,0:T(8,128)S(1)}, u32[]{:S(2)}, u32[]{:S(2)}) collective-permute-start(f32[56,128]{1,0:T(8,128)S(1)} %add_add_fusion.refs_0_), channel_id=1, source_target_pairs={{0,56},{2,58},{4,60},{6,62},{8,0},{10,2},{12,4},{14,6},{16,8},{18,... | collective-permute-start | bytes 86024 | tf_op jit(solution)/shard_map/ppermute | solution.py:347
  110.0 2.3 %collective-permute-start.14 = (f32[56,128]{1,0:T(8,128)S(1)}, f32[56,128]{1,0:T(8,128)S(1)}, u32[]{:S(2)}, u32[]{:S(2)}) collective-permute-start(f32[56,128]{1,0:T(8,128)S(1)} %add_add_fusion.refs_0_), channel_id=1, source_target_pairs={{0,48},{2,50},{4,52},{6,54},{8,56},{10,58},{12,60},{14,62},{16,0},... | collective-permute-start | bytes 86024 | tf_op jit(solution)/shard_map/ppermute | solution.py:347
  112.4 1.4 %collective-permute-start.13 = (f32[56,128]{1,0:T(8,128)S(1)}, f32[56,128]{1,0:T(8,128)S(1)}, u32[]{:S(2)}, u32[]{:S(2)}) collective-permute-start(f32[56,128]{1,0:T(8,128)S(1)} %add_add_fusion.refs_0_), channel_id=1, source_target_pairs={{0,40},{2,42},{4,44},{6,46},{8,48},{10,50},{12,52},{14,54},{16,56}... | collective-permute-start | bytes 86024 | tf_op jit(solution)/shard_map/ppermute | solution.py:347
  113.8 3.8 %collective-permute-start.12 = (f32[56,128]{1,0:T(8,128)S(1)}, f32[56,128]{1,0:T(8,128)S(1)}, u32[]{:S(2)}, u32[]{:S(2)}) collective-permute-start(f32[56,128]{1,0:T(8,128)S(1)} %add_add_fusion.refs_0_), channel_id=1, source_target_pairs={{0,32},{2,34},{4,36},{6,38},{8,40},{10,42},{12,44},{14,46},{16,48}... | collective-permute-start | bytes 86024 | tf_op jit(solution)/shard_map/ppermute | solution.py:347
  117.6 3.7 %collective-permute-start.10 = (f32[56,128]{1,0:T(8,128)S(1)}, f32[56,128]{1,0:T(8,128)S(1)}, u32[]{:S(2)}, u32[]{:S(2)}) collective-permute-start(f32[56,128]{1,0:T(8,128)S(1)} %add_add_fusion.refs_0_), channel_id=1, source_target_pairs={{0,16},{2,18},{4,20},{6,22},{8,24},{10,26},{12,28},{14,30},{16,32}... | collective-permute-start | bytes 86024 | tf_op jit(solution)/shard_map/ppermute | solution.py:347
  121.3 1.2 collective-permute-start.9
  122.5 7.7 %scatter_rows.1 = bf16[4096,128]{1,0:T(8,128)(2,1)} custom-call(s32[32,128]{1,0:T(8,128)} %bitcast.29, bf16[4096,128]{1,0:T(8,128)(2,1)S(1)} %bitcast.18, f32[4096,128]{1,0:T(8,128)S(1)} %bitcast.17), custom_call_target="tpu_custom_call" | custom-call | bytes 8388608 | tf_op jit(solution)/shard_map/scatter_rows/pallas_call | solution.py:318
  130.3 1.3 %finish.1 = (f32[128,256]{1,0:T(8,128)}, f32[172,128]{1,0:T(8,128)}, f32[1,256]{1,0:T(1,128)}) custom-call(s32[2]{0:T(128)S(1)} %pad_add_fusion.refs_0_.ids, f32[56,128]{1,0:T(8,128)S(1)} %add_add_fusion.refs_0_, f32[56,128]{1,0:T(8,128)S(1)} %collective-permute-done.9.refs_1_, f32[56,128]{1,0:T(8,128)S(1)} %collective-permute-done.10.refs_2_, ...), custom_call_target="tpu_custom_call" | custom-call | tf_op jit(solution)/shard_map/finish/pallas_call | solution.py:396
  (39 shorter events, 4.8 us)
Async XLA Ops:
  0.6 22.7 %copy-start.4 = (bf16[128,172]{0,1:T(8,128)(2,1)S(1)}, bf16[128,172]{0,1:T(8,128)(2,1)}, u32[]{:S(2)}) copy-start(bf16[128,172]{0,1:T(8,128)(2,1)} %param.14) | copy-start | bytes 132100
  0.6 22.8 %copy-start.2 = (bf16[128,256]{1,0:T(8,128)(2,1)S(1)}, bf16[128,256]{1,0:T(8,128)(2,1)}, u32[]{:S(2)}) copy-start(bf16[128,256]{1,0:T(8,128)(2,1)} %refs_3_) | copy-start | bytes 196612
  0.7 23.4 %copy-start.5 = (s32[4096]{0:T(1024)S(1)}, s32[4096]{0:T(1024)}, u32[]{:S(2)}) copy-start(s32[4096]{0:T(1024)} %param.15) | copy-start | bytes 49156
  0.7 52.0 %copy-start = (bf16[4096,128]{1,0:T(8,128)(2,1)S(1)}, bf16[4096,128]{1,0:T(8,128)(2,1)}, u32[]{:S(2)}) copy-start(bf16[4096,128]{1,0:T(8,128)(2,1)} %feats_hbm.1) | copy-start | bytes 3145732
  0.7 52.0 %copy-start.1 = (s32[32,8]{0,1:T(8,128)S(1)}, s32[32,8]{0,1:T(8,128)}, u32[]{:S(2)}) copy-start(s32[32,8]{0,1:T(8,128)} %param.10) | copy-start | bytes 3076
  7.9 44.7 %all-to-all-start = ((bf16[128,32,128]{2,1,0:T(8,128)(2,1)}), bf16[128,32,128]{2,1,0:T(8,128)(2,1)S(1)}, u32[]{:S(2)}, u32[]{:S(2)}) async-start(bf16[128,32,128]{2,1,0:T(8,128)(2,1)} %bitcast.26), calls=%async_computation | async-start | bytes 2097152 | tf_op jit(solution)/shard_map/all_to_all | solution.py:424
  23.4 1.3 collective-permute-start.1
  23.5 1.4 %collective-permute-start = (bf16[128,256]{1,0:T(8,128)(2,1)S(1)}, bf16[128,256]{1,0:T(8,128)(2,1)S(1)}, u32[]{:S(2)}, u32[]{:S(2)}) collective-permute-start(bf16[128,256]{1,0:T(8,128)(2,1)S(1)} %copy-done.2), channel_id=1, source_target_pairs={{0,1},{1,0},{2,3},{3,2},{4,5},{5,4},{6,7},{7,6},{8,9},{9,8},{10,11... | collective-permute-start | bytes 196616 | tf_op jit(solution)/shard_map/ppermute | solution.py:433
  58.0 2.7 %collective-permute-start.2 = (bf16[4096,128]{1,0:T(8,128)(2,1)S(1)}, bf16[4096,128]{1,0:T(8,128)(2,1)S(1)}, u32[]{:S(2)}, u32[]{:S(2)}) collective-permute-start(bf16[4096,128]{1,0:T(8,128)(2,1)S(1)} %bitcast.21), channel_id=1, source_target_pairs={{0,1},{1,0},{2,3},{3,2},{4,5},{5,4},{6,7},{7,6},{8,9},{9,8},{10,11... | collective-permute-start | bytes 3145736 | tf_op jit(solution)/shard_map/ppermute | solution.py:446
  66.7 15.5 %all-to-all-start.1 = ((f32[8,56,128]{2,1,0:T(8,128)}), f32[8,56,128]{2,1,0:T(8,128)S(1)}, u32[]{:S(2)}, u32[]{:S(2)}) async-start(f32[8,56,128]{2,1,0:T(8,128)} %bitcast.10), calls=%async_computation.1 | async-start | bytes 458752 | tf_op jit(solution)/shard_map/all_to_all | solution.py:369
  82.2 40.3 %all-to-all-start.2 = ((bf16[128,32,128]{2,1,0:T(8,128)(2,1)}), bf16[128,32,128]{2,1,0:T(8,128)(2,1)S(1)}, u32[]{:S(2)}, u32[]{:S(2)}) async-start(bf16[128,32,128]{2,1,0:T(8,128)(2,1)} %bitcast.13), calls=%async_computation.2 | async-start | bytes 2097152 | tf_op jit(solution)/shard_map/all_to_all | solution.py:455
  90.8 6.1 %collective-permute-start.5 = (f32[56,128]{1,0:T(8,128)S(1)}, f32[56,128]{1,0:T(8,128)S(1)}, u32[]{:S(2)}, u32[]{:S(2)}) collective-permute-start(f32[56,128]{1,0:T(8,128)S(1)} %reduce_sum.9), channel_id=1, source_target_pairs={{0,6},{2,4},{4,2},{6,0},{8,14},{10,12},{12,10},{14,8},{16,22},{18,... | collective-permute-start | bytes 86024 | tf_op jit(solution)/shard_map/ppermute | solution.py:347
  92.3 5.7 %collective-permute-start.4 = (f32[56,128]{1,0:T(8,128)S(1)}, f32[56,128]{1,0:T(8,128)S(1)}, u32[]{:S(2)}, u32[]{:S(2)}) collective-permute-start(f32[56,128]{1,0:T(8,128)S(1)} %reduce_sum.9), channel_id=1, source_target_pairs={{0,4},{2,6},{4,0},{6,2},{8,12},{10,14},{12,8},{14,10},{16,20},{18,... | collective-permute-start | bytes 86024 | tf_op jit(solution)/shard_map/ppermute | solution.py:347
  93.8 4.2 %collective-permute-start.3 = (f32[56,128]{1,0:T(8,128)S(1)}, f32[56,128]{1,0:T(8,128)S(1)}, u32[]{:S(2)}, u32[]{:S(2)}) collective-permute-start(f32[56,128]{1,0:T(8,128)S(1)} %reduce_sum.9), channel_id=1, source_target_pairs={{0,2},{2,0},{4,6},{6,4},{8,10},{10,8},{12,14},{14,12},{16,18},{18,... | collective-permute-start | bytes 86024 | tf_op jit(solution)/shard_map/ppermute | solution.py:347
  98.0 5.6 %collective-permute-start.8 = (f32[56,128]{1,0:T(8,128)S(1)}, f32[56,128]{1,0:T(8,128)S(1)}, u32[]{:S(2)}, u32[]{:S(2)}) collective-permute-start(f32[56,128]{1,0:T(8,128)S(1)} %add_add_fusion.1), channel_id=1, source_target_pairs={{0,192},{2,194},{4,196},{6,198},{8,200},{10,202},{12,204},{14,206}... | collective-permute-start | bytes 86024 | tf_op jit(solution)/shard_map/ppermute | solution.py:347
  101.5 5.7 %collective-permute-start.7 = (f32[56,128]{1,0:T(8,128)S(1)}, f32[56,128]{1,0:T(8,128)S(1)}, u32[]{:S(2)}, u32[]{:S(2)}) collective-permute-start(f32[56,128]{1,0:T(8,128)S(1)} %add_add_fusion.1), channel_id=1, source_target_pairs={{0,128},{2,130},{4,132},{6,134},{8,136},{10,138},{12,140},{14,142}... | collective-permute-start | bytes 86024 | tf_op jit(solution)/shard_map/ppermute | solution.py:347
  102.0 5.3 %collective-permute-start.6 = (f32[56,128]{1,0:T(8,128)S(1)}, f32[56,128]{1,0:T(8,128)S(1)}, u32[]{:S(2)}, u32[]{:S(2)}) collective-permute-start(f32[56,128]{1,0:T(8,128)S(1)} %add_add_fusion.1), channel_id=1, source_target_pairs={{0,64},{2,66},{4,68},{6,70},{8,72},{10,74},{12,76},{14,78},{16,80}... | collective-permute-start | bytes 86024 | tf_op jit(solution)/shard_map/ppermute | solution.py:347
  107.3 10.4 %collective-permute-start.15 = (f32[56,128]{1,0:T(8,128)S(1)}, f32[56,128]{1,0:T(8,128)S(1)}, u32[]{:S(2)}, u32[]{:S(2)}) collective-permute-start(f32[56,128]{1,0:T(8,128)S(1)} %add_add_fusion.refs_0_), channel_id=1, source_target_pairs={{0,56},{2,58},{4,60},{6,62},{8,0},{10,2},{12,4},{14,6},{16,8},{18,... | collective-permute-start | bytes 86024 | tf_op jit(solution)/shard_map/ppermute | solution.py:347
  110.0 11.3 %collective-permute-start.14 = (f32[56,128]{1,0:T(8,128)S(1)}, f32[56,128]{1,0:T(8,128)S(1)}, u32[]{:S(2)}, u32[]{:S(2)}) collective-permute-start(f32[56,128]{1,0:T(8,128)S(1)} %add_add_fusion.refs_0_), channel_id=1, source_target_pairs={{0,48},{2,50},{4,52},{6,54},{8,56},{10,58},{12,60},{14,62},{16,0},... | collective-permute-start | bytes 86024 | tf_op jit(solution)/shard_map/ppermute | solution.py:347
  112.4 17.9 %collective-permute-start.13 = (f32[56,128]{1,0:T(8,128)S(1)}, f32[56,128]{1,0:T(8,128)S(1)}, u32[]{:S(2)}, u32[]{:S(2)}) collective-permute-start(f32[56,128]{1,0:T(8,128)S(1)} %add_add_fusion.refs_0_), channel_id=1, source_target_pairs={{0,40},{2,42},{4,44},{6,46},{8,48},{10,50},{12,52},{14,54},{16,56}... | collective-permute-start | bytes 86024 | tf_op jit(solution)/shard_map/ppermute | solution.py:347
  113.8 16.4 %collective-permute-start.12 = (f32[56,128]{1,0:T(8,128)S(1)}, f32[56,128]{1,0:T(8,128)S(1)}, u32[]{:S(2)}, u32[]{:S(2)}) collective-permute-start(f32[56,128]{1,0:T(8,128)S(1)} %add_add_fusion.refs_0_), channel_id=1, source_target_pairs={{0,32},{2,34},{4,36},{6,38},{8,40},{10,42},{12,44},{14,46},{16,48}... | collective-permute-start | bytes 86024 | tf_op jit(solution)/shard_map/ppermute | solution.py:347
  117.6 12.6 %collective-permute-start.11 = (f32[56,128]{1,0:T(8,128)S(1)}, f32[56,128]{1,0:T(8,128)S(1)}, u32[]{:S(2)}, u32[]{:S(2)}) collective-permute-start(f32[56,128]{1,0:T(8,128)S(1)} %add_add_fusion.refs_0_), channel_id=1, source_target_pairs={{0,24},{2,26},{4,28},{6,30},{8,32},{10,34},{12,36},{14,38},{16,40}... | collective-permute-start | bytes 86024 | tf_op jit(solution)/shard_map/ppermute | solution.py:347
  117.6 12.6 %collective-permute-start.10 = (f32[56,128]{1,0:T(8,128)S(1)}, f32[56,128]{1,0:T(8,128)S(1)}, u32[]{:S(2)}, u32[]{:S(2)}) collective-permute-start(f32[56,128]{1,0:T(8,128)S(1)} %add_add_fusion.refs_0_), channel_id=1, source_target_pairs={{0,16},{2,18},{4,20},{6,22},{8,24},{10,26},{12,28},{14,30},{16,32}... | collective-permute-start | bytes 86024 | tf_op jit(solution)/shard_map/ppermute | solution.py:347
  121.3 9.0 %collective-permute-start.9 = (f32[56,128]{1,0:T(8,128)S(1)}, f32[56,128]{1,0:T(8,128)S(1)}, u32[]{:S(2)}, u32[]{:S(2)}) collective-permute-start(f32[56,128]{1,0:T(8,128)S(1)} %add_add_fusion.refs_0_), channel_id=1, source_target_pairs={{0,8},{2,10},{4,12},{6,14},{8,16},{10,18},{12,20},{14,22},{16,24},... | collective-permute-start | bytes 86024 | tf_op jit(solution)/shard_map/ppermute | solution.py:347
  (1 other events, 8.1 us)

commit v6 on v5

--- a/solution.py
+++ b/solution.py
@@ -13,8 +13,8 @@
 HBM = pl.BlockSpec(memory_space=pltpu.HBM)
 NX, NY, NZ = 4, 4, 8
 PACKED = 448
-TILE_STEPS = 8
-SPAN = 2048
+TILE_STEPS = 4
+SPAN = 4096
 
 
 def contract(a, b, da, db):

time: 133 us -> 132 us (level)
  no operation moved by 1% of the time
where the time goes in v6:
time: 132 us; the launch traced here: 131 us
  starting transfers between devices  52.2 us (40%)
  waiting for transfers between devices  41 us (31%)
  Pallas kernels  34.5 us (26%)
  local copies, waits for them, and re-layouts  1.95 us (1%)
    all_to_all x1, waiting for transfers between devices, on_device(): lax.all_to_all(outgoing, 'dom', split_axis=0, concat_axis=0, tiled=True)  27.8 us
    ppermute x13, starting transfers between devices, move(): return lax.ppermute(value, 'dom', pairs)  23.7 us
    all_to_all x1, starting transfers between devices, on_device(): lax.all_to_all(outgoing, 'dom', split_axis=0, concat_axis=0, tiled=True)  15.4 us
    all_to_all x1, starting transfers between devices, on_device(): lax.all_to_all(returned, 'dom', split_axis=0, concat_axis=0, tiled=True)  8.37 us
    pallas_call x1, Pallas kernels, scatter_rows(): pl.pallas_call(scatter_kernel, out_shape=pltpu.HBM((count, width), BF16),...  7.75 us
    pallas_call x1, Pallas kernels, spread_blocks(): pl.pallas_call(spread_kernel, out_shape=(jax.ShapeDtypeStruct((blocks, ti...  7.65 us
    pallas_call x1, Pallas kernels, gather_rows(): pl.pallas_call(gather_kernel, out_shape=pltpu.HBM((slots, width), BF16),...  7.2 us
    ppermute x13, waiting for transfers between devices, move(): return lax.ppermute(value, 'dom', pairs)  5.93 us
  transfers between devices with their start and end apart: 19, of which 8 were waited for; matrix products, arithmetic and copies ran while one was open for 2% of the time, Pallas kernels for 12%

profile of v6, /device:TPU:2, one launch (start us, length us, event | category | flops | bytes accessed | tf_op | source)
XLA Modules:
  0.0 130.7 jit_solution(2274082658040298104)
XLA Ops:
  0.7 7.2 %gather_rows.1 = bf16[4096,128]{1,0:T(8,128)(2,1)} custom-call(s32[32,128]{1,0:T(8,128)} %bitcast.30, bf16[4096,128]{1,0:T(8,128)(2,1)} %feats_hbm.1), custom_call_target="tpu_custom_call" | custom-call | bytes 8388608 | tf_op jit(solution)/shard_map/gather_rows/pallas_call | solution.py:71
  7.9 15.4 %all-to-all-start = ((bf16[128,32,128]{2,1,0:T(8,128)(2,1)}), bf16[128,32,128]{2,1,0:T(8,128)(2,1)S(1)}, u32[]{:S(2)}, u32[]{:S(2)}) async-start(bf16[128,32,128]{2,1,0:T(8,128)(2,1)} %bitcast.28), calls=%async_computation | async-start | bytes 2097152 | tf_op jit(solution)/shard_map/all_to_all | solution.py:424
  24.9 27.8 %all-to-all-done = bf16[128,32,128]{2,1,0:T(8,128)(2,1)S(1)} async-done(((bf16[128,32,128]{2,1,0:T(8,128)(2,1)}), bf16[128,32,128]{2,1,0:T(8,128)(2,1)S(1)}, u32[]{:S(2)}, u32[]{:S(2)}) %all-to-all-start) | async-done | bytes 1048608 | tf_op jit(solution)/shard_map/all_to_all | solution.py:424
  52.6 5.0 %aggregate_blocks.1 = bf16[32,128,128]{2,1,0:T(8,128)(2,1)S(1)} custom-call(s32[8,32]{1,0:T(8,128)S(1)} %bitcast.24, bf16[32,128,128]{2,1,0:T(8,128)(2,1)S(1)} %bitcast.20, bf16[32,128,128]{2,1,0:T(8,128)(2,1)S(1)} %bitcast.21, bf16[256,128,128]{2,1,0:T(8,128)(2,1)} %adj.3), custom_call_target="tpu_custom_call" | custom-call | flops 1073741824 | bytes 12582912 | tf_op jit(solution)/shard_map/aggregate_blocks/pallas_call | solution.py:119
  57.8 2.6 %collective-permute-done.2.refs_2_ = bf16[4096,128]{1,0:T(8,128)(2,1)S(1)} collective-permute-done((bf16[4096,128]{1,0:T(8,128)(2,1)S(1)}, bf16[4096,128]{1,0:T(8,128)(2,1)S(1)}, u32[]{:S(2)}, u32[]{:S(2)}) %collective-permute-start.2) | collective-permute-done | bytes 1048608 | tf_op jit(solution)/shard_map/ppermute | solution.py:446
  60.4 5.6 %dense.1 = (bf16[32,128,128]{2,1,0:T(8,128)(2,1)S(1)}, f32[448,128]{1,0:T(8,128)}) custom-call(s32[2]{0:T(128)S(1)} %pad_add_fusion.refs_0_.ids, bf16[4096,128]{1,0:T(8,128)(2,1)S(1)} %bitcast.23, bf16[4096,128]{1,0:T(8,128)(2,1)S(1)} %collective-permute-done.2.refs_2_, bf16[128,256]{1,0:T(8,128)(2,1)S(1)} %copy-done.2, ...), custom_call_target="tpu_custom_call" | custom-call | flops 5368709120 | bytes 4194304 | tf_op jit(solution)/shard_map/dense/pallas_call | solution.py:200
  66.0 4.0 %all-to-all-start.1 = ((f32[8,56,128]{2,1,0:T(8,128)}), f32[8,56,128]{2,1,0:T(8,128)S(1)}, u32[]{:S(2)}, u32[]{:S(2)}) async-start(f32[8,56,128]{2,1,0:T(8,128)} %bitcast.11), calls=%async_computation.1 | async-start | bytes 458752 | tf_op jit(solution)/shard_map/all_to_all | solution.py:369
  70.0 7.7 %spread_blocks.1 = (bf16[32,128,128]{2,1,0:T(8,128)(2,1)}, f32[32,128,128]{2,1,0:T(8,128)}) custom-call(s32[8,32]{1,0:T(8,128)S(1)} %bitcast.25, bf16[32,128,128]{2,1,0:T(8,128)(2,1)S(1)} %get-tuple-element.53.grads, bf16[256,128,128]{2,1,0:T(8,128)(2,1)} %adj.3), custom_call_target="tpu_custom_call" | custom-call | flops 1073741824 | bytes 12582912 | tf_op jit(solution)/shard_map/spread_blocks/pallas_call | solution.py:258
  77.7 3.8 %all-to-all-done.1 = f32[8,56,128]{2,1,0:T(8,128)S(1)} async-done(((f32[8,56,128]{2,1,0:T(8,128)}), f32[8,56,128]{2,1,0:T(8,128)S(1)}, u32[]{:S(2)}, u32[]{:S(2)}) %all-to-all-start.1) | async-done | bytes 229408 | tf_op jit(solution)/shard_map/all_to_all | solution.py:369
  81.5 8.4 %all-to-all-start.2 = ((bf16[128,32,128]{2,1,0:T(8,128)(2,1)}), bf16[128,32,128]{2,1,0:T(8,128)(2,1)S(1)}, u32[]{:S(2)}, u32[]{:S(2)}) async-start(bf16[128,32,128]{2,1,0:T(8,128)(2,1)} %bitcast.14), calls=%async_computation.2 | async-start | bytes 2097152 | tf_op jit(solution)/shard_map/all_to_all | solution.py:455
  89.9 1.6 %collective-permute-start.5 = (f32[56,128]{1,0:T(8,128)S(1)}, f32[56,128]{1,0:T(8,128)S(1)}, u32[]{:S(2)}, u32[]{:S(2)}) collective-permute-start(f32[56,128]{1,0:T(8,128)S(1)} %reduce_sum.9), channel_id=1, source_target_pairs={{0,6},{2,4},{4,2},{6,0},{8,14},{10,12},{12,10},{14,8},{16,22},{18,... | collective-permute-start | bytes 86024 | tf_op jit(solution)/shard_map/ppermute | solution.py:347
  91.5 1.5 %collective-permute-start.4 = (f32[56,128]{1,0:T(8,128)S(1)}, f32[56,128]{1,0:T(8,128)S(1)}, u32[]{:S(2)}, u32[]{:S(2)}) collective-permute-start(f32[56,128]{1,0:T(8,128)S(1)} %reduce_sum.9), channel_id=1, source_target_pairs={{0,4},{2,6},{4,0},{6,2},{8,12},{10,14},{12,8},{14,10},{16,20},{18,... | collective-permute-start | bytes 86024 | tf_op jit(solution)/shard_map/ppermute | solution.py:347
  94.1 1.9 %copy.12 = f32[32,128,128]{2,1,0:T(8,128)S(1)} copy(f32[32,128,128]{1,2,0:T(8,128)} %bitcast.29) | data formatting | bytes 4194304 | tf_op jit(solution)/shard_map/transpose | solution.py:457
  97.2 3.3 %collective-permute-start.8 = (f32[56,128]{1,0:T(8,128)S(1)}, f32[56,128]{1,0:T(8,128)S(1)}, u32[]{:S(2)}, u32[]{:S(2)}) collective-permute-start(f32[56,128]{1,0:T(8,128)S(1)} %add_add_fusion.1), channel_id=1, source_target_pairs={{0,192},{2,194},{4,196},{6,198},{8,200},{10,202},{12,204},{14,206}... | collective-permute-start | bytes 86024 | tf_op jit(solution)/shard_map/ppermute | solution.py:347
  101.5 1.2 collective-permute-done.8
  102.6 3.7 %collective-permute-done.7 = f32[56,128]{1,0:T(8,128)S(1)} collective-permute-done((f32[56,128]{1,0:T(8,128)S(1)}, f32[56,128]{1,0:T(8,128)S(1)}, u32[]{:S(2)}, u32[]{:S(2)}) %collective-permute-start.7) | collective-permute-done | bytes 28704 | tf_op jit(solution)/shard_map/ppermute | solution.py:347
  106.3 2.7 %collective-permute-start.15 = (f32[56,128]{1,0:T(8,128)S(1)}, f32[56,128]{1,0:T(8,128)S(1)}, u32[]{:S(2)}, u32[]{:S(2)}) collective-permute-start(f32[56,128]{1,0:T(8,128)S(1)} %add_add_fusion.refs_0_), channel_id=1, source_target_pairs={{0,56},{2,58},{4,60},{6,62},{8,0},{10,2},{12,4},{14,6},{16,8},{18,... | collective-permute-start | bytes 86024 | tf_op jit(solution)/shard_map/ppermute | solution.py:347
  109.0 2.4 %collective-permute-start.14 = (f32[56,128]{1,0:T(8,128)S(1)}, f32[56,128]{1,0:T(8,128)S(1)}, u32[]{:S(2)}, u32[]{:S(2)}) collective-permute-start(f32[56,128]{1,0:T(8,128)S(1)} %add_add_fusion.refs_0_), channel_id=1, source_target_pairs={{0,48},{2,50},{4,52},{6,54},{8,56},{10,58},{12,60},{14,62},{16,0},... | collective-permute-start | bytes 86024 | tf_op jit(solution)/shard_map/ppermute | solution.py:347
  111.4 1.2 collective-permute-start.13
  112.6 4.1 %collective-permute-start.12 = (f32[56,128]{1,0:T(8,128)S(1)}, f32[56,128]{1,0:T(8,128)S(1)}, u32[]{:S(2)}, u32[]{:S(2)}) collective-permute-start(f32[56,128]{1,0:T(8,128)S(1)} %add_add_fusion.refs_0_), channel_id=1, source_target_pairs={{0,32},{2,34},{4,36},{6,38},{8,40},{10,42},{12,44},{14,46},{16,48}... | collective-permute-start | bytes 86024 | tf_op jit(solution)/shard_map/ppermute | solution.py:347
  116.7 3.7 %collective-permute-start.10 = (f32[56,128]{1,0:T(8,128)S(1)}, f32[56,128]{1,0:T(8,128)S(1)}, u32[]{:S(2)}, u32[]{:S(2)}) collective-permute-start(f32[56,128]{1,0:T(8,128)S(1)} %add_add_fusion.refs_0_), channel_id=1, source_target_pairs={{0,16},{2,18},{4,20},{6,22},{8,24},{10,26},{12,28},{14,30},{16,32}... | collective-permute-start | bytes 86024 | tf_op jit(solution)/shard_map/ppermute | solution.py:347
  120.4 1.1 collective-permute-start.9
  121.5 7.7 %scatter_rows.1 = bf16[4096,128]{1,0:T(8,128)(2,1)} custom-call(s32[32,128]{1,0:T(8,128)} %bitcast.31, bf16[4096,128]{1,0:T(8,128)(2,1)S(1)} %bitcast.19, f32[4096,128]{1,0:T(8,128)S(1)} %bitcast.18), custom_call_target="tpu_custom_call" | custom-call | bytes 8388608 | tf_op jit(solution)/shard_map/scatter_rows/pallas_call | solution.py:318
  129.3 1.3 %finish.1 = (f32[128,256]{1,0:T(8,128)}, f32[172,128]{1,0:T(8,128)}, f32[1,256]{1,0:T(1,128)}) custom-call(s32[2]{0:T(128)S(1)} %pad_add_fusion.refs_0_.ids, f32[56,128]{1,0:T(8,128)S(1)} %add_add_fusion.refs_0_, f32[56,128]{1,0:T(8,128)S(1)} %collective-permute-done.9.refs_1_, f32[56,128]{1,0:T(8,128)S(1)} %collective-permute-done.10.refs_2_, ...), custom_call_target="tpu_custom_call" | custom-call | tf_op jit(solution)/shard_map/finish/pallas_call | solution.py:396
  (38 shorter events, 4.9 us)
Async XLA Ops:
  0.6 22.7 %copy-start.5 = (bf16[128,172]{0,1:T(8,128)(2,1)S(1)}, bf16[128,172]{0,1:T(8,128)(2,1)}, u32[]{:S(2)}) copy-start(bf16[128,172]{0,1:T(8,128)(2,1)} %param.14) | copy-start | bytes 132100
  0.6 22.8 %copy-start.2 = (bf16[128,256]{1,0:T(8,128)(2,1)S(1)}, bf16[128,256]{1,0:T(8,128)(2,1)}, u32[]{:S(2)}) copy-start(bf16[128,256]{1,0:T(8,128)(2,1)} %refs_3_) | copy-start | bytes 196612
  0.7 52.0 %copy-start = (bf16[4096,128]{1,0:T(8,128)(2,1)S(1)}, bf16[4096,128]{1,0:T(8,128)(2,1)}, u32[]{:S(2)}) copy-start(bf16[4096,128]{1,0:T(8,128)(2,1)} %feats_hbm.1) | copy-start | bytes 3145732
  0.7 52.0 %copy-start.1 = (s32[32,8]{0,1:T(8,128)S(1)}, s32[32,8]{0,1:T(8,128)}, u32[]{:S(2)}) copy-start(s32[32,8]{0,1:T(8,128)} %param.10) | copy-start | bytes 3076
  7.9 44.7 %all-to-all-start = ((bf16[128,32,128]{2,1,0:T(8,128)(2,1)}), bf16[128,32,128]{2,1,0:T(8,128)(2,1)S(1)}, u32[]{:S(2)}, u32[]{:S(2)}) async-start(bf16[128,32,128]{2,1,0:T(8,128)(2,1)} %bitcast.28), calls=%async_computation | async-start | bytes 2097152 | tf_op jit(solution)/shard_map/all_to_all | solution.py:424
  23.3 1.3 %collective-permute-start.1 = (bf16[176,128]{1,0:T(8,128)(2,1)S(1)}, bf16[176,128]{1,0:T(8,128)(2,1)S(1)}, u32[]{:S(2)}, u32[]{:S(2)}) collective-permute-start(bf16[176,128]{1,0:T(8,128)(2,1)S(1)} %pad.4.refs_5_), channel_id=1, source_target_pairs={{0,1},{1,0},{2,3},{3,2},{4,5},{5,4},{6,7},{7,6},{8,9},{9,8},{10,11... | collective-permute-start | bytes 135176 | tf_op jit(solution)/shard_map/ppermute | solution.py:434
  23.5 1.4 %collective-permute-start = (bf16[128,256]{1,0:T(8,128)(2,1)S(1)}, bf16[128,256]{1,0:T(8,128)(2,1)S(1)}, u32[]{:S(2)}, u32[]{:S(2)}) collective-permute-start(bf16[128,256]{1,0:T(8,128)(2,1)S(1)} %copy-done.2), channel_id=1, source_target_pairs={{0,1},{1,0},{2,3},{3,2},{4,5},{5,4},{6,7},{7,6},{8,9},{9,8},{10,11... | collective-permute-start | bytes 196616 | tf_op jit(solution)/shard_map/ppermute | solution.py:433
  52.6 7.8 %copy-start.4 = (f32[256]{0:T(256)S(1)}, f32[256]{0:T(256)}, u32[]{:S(2)}) copy-start(f32[256]{0:T(256)} %param.13) | copy-start | bytes 3076
  57.7 2.7 %collective-permute-start.2 = (bf16[4096,128]{1,0:T(8,128)(2,1)S(1)}, bf16[4096,128]{1,0:T(8,128)(2,1)S(1)}, u32[]{:S(2)}, u32[]{:S(2)}) collective-permute-start(bf16[4096,128]{1,0:T(8,128)(2,1)S(1)} %bitcast.22), channel_id=1, source_target_pairs={{0,1},{1,0},{2,3},{3,2},{4,5},{5,4},{6,7},{7,6},{8,9},{9,8},{10,11... | collective-permute-start | bytes 3145736 | tf_op jit(solution)/shard_map/ppermute | solution.py:446
  66.0 15.5 %all-to-all-start.1 = ((f32[8,56,128]{2,1,0:T(8,128)}), f32[8,56,128]{2,1,0:T(8,128)S(1)}, u32[]{:S(2)}, u32[]{:S(2)}) async-start(f32[8,56,128]{2,1,0:T(8,128)} %bitcast.11), calls=%async_computation.1 | async-start | bytes 458752 | tf_op jit(solution)/shard_map/all_to_all | solution.py:369
  81.5 40.0 %all-to-all-start.2 = ((bf16[128,32,128]{2,1,0:T(8,128)(2,1)}), bf16[128,32,128]{2,1,0:T(8,128)(2,1)S(1)}, u32[]{:S(2)}, u32[]{:S(2)}) async-start(bf16[128,32,128]{2,1,0:T(8,128)(2,1)} %bitcast.14), calls=%async_computation.2 | async-start | bytes 2097152 | tf_op jit(solution)/shard_map/all_to_all | solution.py:455
  89.9 6.1 %collective-permute-start.5 = (f32[56,128]{1,0:T(8,128)S(1)}, f32[56,128]{1,0:T(8,128)S(1)}, u32[]{:S(2)}, u32[]{:S(2)}) collective-permute-start(f32[56,128]{1,0:T(8,128)S(1)} %reduce_sum.9), channel_id=1, source_target_pairs={{0,6},{2,4},{4,2},{6,0},{8,14},{10,12},{12,10},{14,8},{16,22},{18,... | collective-permute-start | bytes 86024 | tf_op jit(solution)/shard_map/ppermute | solution.py:347
  91.5 5.7 %collective-permute-start.4 = (f32[56,128]{1,0:T(8,128)S(1)}, f32[56,128]{1,0:T(8,128)S(1)}, u32[]{:S(2)}, u32[]{:S(2)}) collective-permute-start(f32[56,128]{1,0:T(8,128)S(1)} %reduce_sum.9), channel_id=1, source_target_pairs={{0,4},{2,6},{4,0},{6,2},{8,12},{10,14},{12,8},{14,10},{16,20},{18,... | collective-permute-start | bytes 86024 | tf_op jit(solution)/shard_map/ppermute | solution.py:347
  93.0 4.2 %collective-permute-start.3 = (f32[56,128]{1,0:T(8,128)S(1)}, f32[56,128]{1,0:T(8,128)S(1)}, u32[]{:S(2)}, u32[]{:S(2)}) collective-permute-start(f32[56,128]{1,0:T(8,128)S(1)} %reduce_sum.9), channel_id=1, source_target_pairs={{0,2},{2,0},{4,6},{6,4},{8,10},{10,8},{12,14},{14,12},{16,18},{18,... | collective-permute-start | bytes 86024 | tf_op jit(solution)/shard_map/ppermute | solution.py:347
  97.2 5.5 %collective-permute-start.8 = (f32[56,128]{1,0:T(8,128)S(1)}, f32[56,128]{1,0:T(8,128)S(1)}, u32[]{:S(2)}, u32[]{:S(2)}) collective-permute-start(f32[56,128]{1,0:T(8,128)S(1)} %add_add_fusion.1), channel_id=1, source_target_pairs={{0,192},{2,194},{4,196},{6,198},{8,200},{10,202},{12,204},{14,206}... | collective-permute-start | bytes 86024 | tf_op jit(solution)/shard_map/ppermute | solution.py:347
  100.5 5.8 %collective-permute-start.7 = (f32[56,128]{1,0:T(8,128)S(1)}, f32[56,128]{1,0:T(8,128)S(1)}, u32[]{:S(2)}, u32[]{:S(2)}) collective-permute-start(f32[56,128]{1,0:T(8,128)S(1)} %add_add_fusion.1), channel_id=1, source_target_pairs={{0,128},{2,130},{4,132},{6,134},{8,136},{10,138},{12,140},{14,142}... | collective-permute-start | bytes 86024 | tf_op jit(solution)/shard_map/ppermute | solution.py:347
  100.9 5.3 %collective-permute-start.6 = (f32[56,128]{1,0:T(8,128)S(1)}, f32[56,128]{1,0:T(8,128)S(1)}, u32[]{:S(2)}, u32[]{:S(2)}) collective-permute-start(f32[56,128]{1,0:T(8,128)S(1)} %add_add_fusion.1), channel_id=1, source_target_pairs={{0,64},{2,66},{4,68},{6,70},{8,72},{10,74},{12,76},{14,78},{16,80}... | collective-permute-start | bytes 86024 | tf_op jit(solution)/shard_map/ppermute | solution.py:347
  106.3 10.4 %collective-permute-start.15 = (f32[56,128]{1,0:T(8,128)S(1)}, f32[56,128]{1,0:T(8,128)S(1)}, u32[]{:S(2)}, u32[]{:S(2)}) collective-permute-start(f32[56,128]{1,0:T(8,128)S(1)} %add_add_fusion.refs_0_), channel_id=1, source_target_pairs={{0,56},{2,58},{4,60},{6,62},{8,0},{10,2},{12,4},{14,6},{16,8},{18,... | collective-permute-start | bytes 86024 | tf_op jit(solution)/shard_map/ppermute | solution.py:347
  109.0 11.4 %collective-permute-start.14 = (f32[56,128]{1,0:T(8,128)S(1)}, f32[56,128]{1,0:T(8,128)S(1)}, u32[]{:S(2)}, u32[]{:S(2)}) collective-permute-start(f32[56,128]{1,0:T(8,128)S(1)} %add_add_fusion.refs_0_), channel_id=1, source_target_pairs={{0,48},{2,50},{4,52},{6,54},{8,56},{10,58},{12,60},{14,62},{16,0},... | collective-permute-start | bytes 86024 | tf_op jit(solution)/shard_map/ppermute | solution.py:347
  111.4 17.9 %collective-permute-start.13 = (f32[56,128]{1,0:T(8,128)S(1)}, f32[56,128]{1,0:T(8,128)S(1)}, u32[]{:S(2)}, u32[]{:S(2)}) collective-permute-start(f32[56,128]{1,0:T(8,128)S(1)} %add_add_fusion.refs_0_), channel_id=1, source_target_pairs={{0,40},{2,42},{4,44},{6,46},{8,48},{10,50},{12,52},{14,54},{16,56}... | collective-permute-start | bytes 86024 | tf_op jit(solution)/shard_map/ppermute | solution.py:347
  112.6 16.7 %collective-permute-start.12 = (f32[56,128]{1,0:T(8,128)S(1)}, f32[56,128]{1,0:T(8,128)S(1)}, u32[]{:S(2)}, u32[]{:S(2)}) collective-permute-start(f32[56,128]{1,0:T(8,128)S(1)} %add_add_fusion.refs_0_), channel_id=1, source_target_pairs={{0,32},{2,34},{4,36},{6,38},{8,40},{10,42},{12,44},{14,46},{16,48}... | collective-permute-start | bytes 86024 | tf_op jit(solution)/shard_map/ppermute | solution.py:347
  116.7 12.6 %collective-permute-start.11 = (f32[56,128]{1,0:T(8,128)S(1)}, f32[56,128]{1,0:T(8,128)S(1)}, u32[]{:S(2)}, u32[]{:S(2)}) collective-permute-start(f32[56,128]{1,0:T(8,128)S(1)} %add_add_fusion.refs_0_), channel_id=1, source_target_pairs={{0,24},{2,26},{4,28},{6,30},{8,32},{10,34},{12,36},{14,38},{16,40}... | collective-permute-start | bytes 86024 | tf_op jit(solution)/shard_map/ppermute | solution.py:347
  116.7 12.6 %collective-permute-start.10 = (f32[56,128]{1,0:T(8,128)S(1)}, f32[56,128]{1,0:T(8,128)S(1)}, u32[]{:S(2)}, u32[]{:S(2)}) collective-permute-start(f32[56,128]{1,0:T(8,128)S(1)} %add_add_fusion.refs_0_), channel_id=1, source_target_pairs={{0,16},{2,18},{4,20},{6,22},{8,24},{10,26},{12,28},{14,30},{16,32}... | collective-permute-start | bytes 86024 | tf_op jit(solution)/shard_map/ppermute | solution.py:347
  120.4 8.9 %collective-permute-start.9 = (f32[56,128]{1,0:T(8,128)S(1)}, f32[56,128]{1,0:T(8,128)S(1)}, u32[]{:S(2)}, u32[]{:S(2)}) collective-permute-start(f32[56,128]{1,0:T(8,128)S(1)} %add_add_fusion.refs_0_), channel_id=1, source_target_pairs={{0,8},{2,10},{4,12},{6,14},{8,16},{10,18},{12,20},{14,22},{16,24},... | collective-permute-start | bytes 86024 | tf_op jit(solution)/shard_map/ppermute | solution.py:347
  (1 other events, 7.8 us)

commit v7 on v6

--- a/solution.py
+++ b/solution.py
@@ -155,6 +155,7 @@
     sum_c[...] = jnp.zeros_like(sum_c)
     sum_b[...] = jnp.zeros_like(sum_b)
     class_id = lax.broadcasted_iota(jnp.int32, (class_rows, SPAN), 0)
+    class_full = classes // 8 * 8
 
     def one_step(i, carry):
         nodes = pl.ds(pl.multiple_of(i * SPAN, SPAN), SPAN)
@@ -163,7 +164,8 @@
         preact = preact + jnp.tile(bias[...], (1, SPAN // bias.shape[1]))
         hidden = jnp.maximum(preact, 0.0).astype(BF16)
         logits = contract(cls_t[...], hidden, 1, 0)
-        logits = jnp.where(class_id < classes, logits, -jnp.inf)
+        tail = jnp.where(class_id[class_full:] < classes, logits[class_full:], -jnp.inf)
+        logits = jnp.concatenate([logits[:class_full], tail], 0)
         powers = jnp.exp(logits - jnp.max(logits, 0, keepdims=True))
         share = powers * (1.0 / jnp.sum(powers, 0, keepdims=True))
         label = labels[pl.ds(i, 1), :]
@@ -314,7 +316,7 @@
 
 def scatter_rows(rows, arrived, own):
     count, width = own.shape
-    lanes = 8
+    lanes = 6
     return pl.pallas_call(
         scatter_kernel,
         out_shape=pltpu.HBM((count, width), BF16),

time: 132 us -> 131 us (level)
  no operation moved by 1% of the time
where the time goes in v7:
time: 131 us; the launch traced here: 130 us
  starting transfers between devices  52.2 us (40%)
  waiting for transfers between devices  41 us (31%)
  Pallas kernels  34.2 us (26%)
  local copies, waits for them, and re-layouts  1.95 us (1%)
    all_to_all x1, waiting for transfers between devices, on_device(): lax.all_to_all(outgoing, 'dom', split_axis=0, concat_axis=0, tiled=True)  27.8 us
    ppermute x13, starting transfers between devices, move(): return lax.ppermute(value, 'dom', pairs)  23.7 us
    all_to_all x1, starting transfers between devices, on_device(): lax.all_to_all(outgoing, 'dom', split_axis=0, concat_axis=0, tiled=True)  15.4 us
    all_to_all x1, starting transfers between devices, on_device(): lax.all_to_all(returned, 'dom', split_axis=0, concat_axis=0, tiled=True)  8.37 us
    pallas_call x1, Pallas kernels, spread_blocks(): pl.pallas_call(spread_kernel, out_shape=(jax.ShapeDtypeStruct((blocks, ti...  7.65 us
    pallas_call x1, Pallas kernels, scatter_rows(): pl.pallas_call(scatter_kernel, out_shape=pltpu.HBM((count, width), BF16),...  7.41 us
    pallas_call x1, Pallas kernels, gather_rows(): pl.pallas_call(gather_kernel, out_shape=pltpu.HBM((slots, width), BF16),...  7.2 us
    ppermute x13, waiting for transfers between devices, move(): return lax.ppermute(value, 'dom', pairs)  5.93 us
  transfers between devices with their start and end apart: 19, of which 8 were waited for; matrix products, arithmetic and copies ran while one was open for 2% of the time, Pallas kernels for 12%

profile of v7, /device:TPU:2, one launch (start us, length us, event | category | flops | bytes accessed | tf_op | source)
XLA Modules:
  0.0 130.3 jit_solution(16420335278824736257)
XLA Ops:
  0.7 7.2 %gather_rows.1 = bf16[4096,128]{1,0:T(8,128)(2,1)} custom-call(s32[32,128]{1,0:T(8,128)} %bitcast.30, bf16[4096,128]{1,0:T(8,128)(2,1)} %feats_hbm.1), custom_call_target="tpu_custom_call" | custom-call | bytes 8388608 | tf_op jit(solution)/shard_map/gather_rows/pallas_call | solution.py:71
  7.9 15.4 %all-to-all-start = ((bf16[128,32,128]{2,1,0:T(8,128)(2,1)}), bf16[128,32,128]{2,1,0:T(8,128)(2,1)S(1)}, u32[]{:S(2)}, u32[]{:S(2)}) async-start(bf16[128,32,128]{2,1,0:T(8,128)(2,1)} %bitcast.28), calls=%async_computation | async-start | bytes 2097152 | tf_op jit(solution)/shard_map/all_to_all | solution.py:426
  24.9 27.8 %all-to-all-done = bf16[128,32,128]{2,1,0:T(8,128)(2,1)S(1)} async-done(((bf16[128,32,128]{2,1,0:T(8,128)(2,1)}), bf16[128,32,128]{2,1,0:T(8,128)(2,1)S(1)}, u32[]{:S(2)}, u32[]{:S(2)}) %all-to-all-start) | async-done | bytes 1048608 | tf_op jit(solution)/shard_map/all_to_all | solution.py:426
  52.6 5.0 %aggregate_blocks.1 = bf16[32,128,128]{2,1,0:T(8,128)(2,1)S(1)} custom-call(s32[8,32]{1,0:T(8,128)S(1)} %bitcast.24, bf16[32,128,128]{2,1,0:T(8,128)(2,1)S(1)} %bitcast.20, bf16[32,128,128]{2,1,0:T(8,128)(2,1)S(1)} %bitcast.21, bf16[256,128,128]{2,1,0:T(8,128)(2,1)} %adj.3), custom_call_target="tpu_custom_call" | custom-call | flops 1073741824 | bytes 12582912 | tf_op jit(solution)/shard_map/aggregate_blocks/pallas_call | solution.py:119
  57.8 2.6 %collective-permute-done.2.refs_2_ = bf16[4096,128]{1,0:T(8,128)(2,1)S(1)} collective-permute-done((bf16[4096,128]{1,0:T(8,128)(2,1)S(1)}, bf16[4096,128]{1,0:T(8,128)(2,1)S(1)}, u32[]{:S(2)}, u32[]{:S(2)}) %collective-permute-start.2) | collective-permute-done | bytes 1048608 | tf_op jit(solution)/shard_map/ppermute | solution.py:448
  60.4 5.6 %dense.1 = (bf16[32,128,128]{2,1,0:T(8,128)(2,1)S(1)}, f32[448,128]{1,0:T(8,128)}) custom-call(s32[2]{0:T(128)S(1)} %pad_add_fusion.refs_0_.ids, bf16[4096,128]{1,0:T(8,128)(2,1)S(1)} %bitcast.23, bf16[4096,128]{1,0:T(8,128)(2,1)S(1)} %collective-permute-done.2.refs_2_, bf16[128,256]{1,0:T(8,128)(2,1)S(1)} %copy-done.2, ...), custom_call_target="tpu_custom_call" | custom-call | flops 5368709120 | bytes 4194304 | tf_op jit(solution)/shard_map/dense/pallas_call | solution.py:202
  66.0 4.0 %all-to-all-start.1 = ((f32[8,56,128]{2,1,0:T(8,128)}), f32[8,56,128]{2,1,0:T(8,128)S(1)}, u32[]{:S(2)}, u32[]{:S(2)}) async-start(f32[8,56,128]{2,1,0:T(8,128)} %bitcast.11), calls=%async_computation.1 | async-start | bytes 458752 | tf_op jit(solution)/shard_map/all_to_all | solution.py:371
  70.0 7.7 %spread_blocks.1 = (bf16[32,128,128]{2,1,0:T(8,128)(2,1)}, f32[32,128,128]{2,1,0:T(8,128)}) custom-call(s32[8,32]{1,0:T(8,128)S(1)} %bitcast.25, bf16[32,128,128]{2,1,0:T(8,128)(2,1)S(1)} %get-tuple-element.53.grads, bf16[256,128,128]{2,1,0:T(8,128)(2,1)} %adj.3), custom_call_target="tpu_custom_call" | custom-call | flops 1073741824 | bytes 12582912 | tf_op jit(solution)/shard_map/spread_blocks/pallas_call | solution.py:260
  77.7 3.8 %all-to-all-done.1 = f32[8,56,128]{2,1,0:T(8,128)S(1)} async-done(((f32[8,56,128]{2,1,0:T(8,128)}), f32[8,56,128]{2,1,0:T(8,128)S(1)}, u32[]{:S(2)}, u32[]{:S(2)}) %all-to-all-start.1) | async-done | bytes 229408 | tf_op jit(solution)/shard_map/all_to_all | solution.py:371
  81.5 8.4 %all-to-all-start.2 = ((bf16[128,32,128]{2,1,0:T(8,128)(2,1)}), bf16[128,32,128]{2,1,0:T(8,128)(2,1)S(1)}, u32[]{:S(2)}, u32[]{:S(2)}) async-start(bf16[128,32,128]{2,1,0:T(8,128)(2,1)} %bitcast.14), calls=%async_computation.2 | async-start | bytes 2097152 | tf_op jit(solution)/shard_map/all_to_all | solution.py:457
  89.9 1.6 %collective-permute-start.5 = (f32[56,128]{1,0:T(8,128)S(1)}, f32[56,128]{1,0:T(8,128)S(1)}, u32[]{:S(2)}, u32[]{:S(2)}) collective-permute-start(f32[56,128]{1,0:T(8,128)S(1)} %reduce_sum.9), channel_id=1, source_target_pairs={{0,6},{2,4},{4,2},{6,0},{8,14},{10,12},{12,10},{14,8},{16,22},{18,... | collective-permute-start | bytes 86024 | tf_op jit(solution)/shard_map/ppermute | solution.py:349
  91.5 1.5 %collective-permute-start.4 = (f32[56,128]{1,0:T(8,128)S(1)}, f32[56,128]{1,0:T(8,128)S(1)}, u32[]{:S(2)}, u32[]{:S(2)}) collective-permute-start(f32[56,128]{1,0:T(8,128)S(1)} %reduce_sum.9), channel_id=1, source_target_pairs={{0,4},{2,6},{4,0},{6,2},{8,12},{10,14},{12,8},{14,10},{16,20},{18,... | collective-permute-start | bytes 86024 | tf_op jit(solution)/shard_map/ppermute | solution.py:349
  94.1 1.9 %copy.12 = f32[32,128,128]{2,1,0:T(8,128)S(1)} copy(f32[32,128,128]{1,2,0:T(8,128)} %bitcast.29) | data formatting | bytes 4194304 | tf_op jit(solution)/shard_map/transpose | solution.py:459
  97.2 3.3 %collective-permute-start.8 = (f32[56,128]{1,0:T(8,128)S(1)}, f32[56,128]{1,0:T(8,128)S(1)}, u32[]{:S(2)}, u32[]{:S(2)}) collective-permute-start(f32[56,128]{1,0:T(8,128)S(1)} %add_add_fusion.1), channel_id=1, source_target_pairs={{0,192},{2,194},{4,196},{6,198},{8,200},{10,202},{12,204},{14,206}... | collective-permute-start | bytes 86024 | tf_op jit(solution)/shard_map/ppermute | solution.py:349
  101.5 1.2 collective-permute-done.8
  102.6 3.7 %collective-permute-done.7 = f32[56,128]{1,0:T(8,128)S(1)} collective-permute-done((f32[56,128]{1,0:T(8,128)S(1)}, f32[56,128]{1,0:T(8,128)S(1)}, u32[]{:S(2)}, u32[]{:S(2)}) %collective-permute-start.7) | collective-permute-done | bytes 28704 | tf_op jit(solution)/shard_map/ppermute | solution.py:349
  106.3 2.7 %collective-permute-start.15 = (f32[56,128]{1,0:T(8,128)S(1)}, f32[56,128]{1,0:T(8,128)S(1)}, u32[]{:S(2)}, u32[]{:S(2)}) collective-permute-start(f32[56,128]{1,0:T(8,128)S(1)} %add_add_fusion.refs_0_), channel_id=1, source_target_pairs={{0,56},{2,58},{4,60},{6,62},{8,0},{10,2},{12,4},{14,6},{16,8},{18,... | collective-permute-start | bytes 86024 | tf_op jit(solution)/shard_map/ppermute | solution.py:349
  109.0 2.4 %collective-permute-start.14 = (f32[56,128]{1,0:T(8,128)S(1)}, f32[56,128]{1,0:T(8,128)S(1)}, u32[]{:S(2)}, u32[]{:S(2)}) collective-permute-start(f32[56,128]{1,0:T(8,128)S(1)} %add_add_fusion.refs_0_), channel_id=1, source_target_pairs={{0,48},{2,50},{4,52},{6,54},{8,56},{10,58},{12,60},{14,62},{16,0},... | collective-permute-start | bytes 86024 | tf_op jit(solution)/shard_map/ppermute | solution.py:349
  111.4 1.2 collective-permute-start.13
  112.6 4.1 %collective-permute-start.12 = (f32[56,128]{1,0:T(8,128)S(1)}, f32[56,128]{1,0:T(8,128)S(1)}, u32[]{:S(2)}, u32[]{:S(2)}) collective-permute-start(f32[56,128]{1,0:T(8,128)S(1)} %add_add_fusion.refs_0_), channel_id=1, source_target_pairs={{0,32},{2,34},{4,36},{6,38},{8,40},{10,42},{12,44},{14,46},{16,48}... | collective-permute-start | bytes 86024 | tf_op jit(solution)/shard_map/ppermute | solution.py:349
  116.7 3.7 %collective-permute-start.10 = (f32[56,128]{1,0:T(8,128)S(1)}, f32[56,128]{1,0:T(8,128)S(1)}, u32[]{:S(2)}, u32[]{:S(2)}) collective-permute-start(f32[56,128]{1,0:T(8,128)S(1)} %add_add_fusion.refs_0_), channel_id=1, source_target_pairs={{0,16},{2,18},{4,20},{6,22},{8,24},{10,26},{12,28},{14,30},{16,32}... | collective-permute-start | bytes 86024 | tf_op jit(solution)/shard_map/ppermute | solution.py:349
  120.4 1.1 collective-permute-start.9
  121.5 7.4 %scatter_rows.1 = bf16[4096,128]{1,0:T(8,128)(2,1)} custom-call(s32[32,128]{1,0:T(8,128)} %bitcast.31, bf16[4096,128]{1,0:T(8,128)(2,1)S(1)} %bitcast.19, f32[4096,128]{1,0:T(8,128)S(1)} %bitcast.18), custom_call_target="tpu_custom_call" | custom-call | bytes 8388608 | tf_op jit(solution)/shard_map/scatter_rows/pallas_call | solution.py:320
  129.0 1.3 %finish.1 = (f32[128,256]{1,0:T(8,128)}, f32[172,128]{1,0:T(8,128)}, f32[1,256]{1,0:T(1,128)}) custom-call(s32[2]{0:T(128)S(1)} %pad_add_fusion.refs_0_.ids, f32[56,128]{1,0:T(8,128)S(1)} %add_add_fusion.refs_0_, f32[56,128]{1,0:T(8,128)S(1)} %collective-permute-done.9.refs_1_, f32[56,128]{1,0:T(8,128)S(1)} %collective-permute-done.10.refs_2_, ...), custom_call_target="tpu_custom_call" | custom-call | tf_op jit(solution)/shard_map/finish/pallas_call | solution.py:398
  (38 shorter events, 4.9 us)
Async XLA Ops:
  0.6 22.7 %copy-start.5 = (bf16[128,172]{0,1:T(8,128)(2,1)S(1)}, bf16[128,172]{0,1:T(8,128)(2,1)}, u32[]{:S(2)}) copy-start(bf16[128,172]{0,1:T(8,128)(2,1)} %param.14) | copy-start | bytes 132100
  0.6 22.8 %copy-start.2 = (bf16[128,256]{1,0:T(8,128)(2,1)S(1)}, bf16[128,256]{1,0:T(8,128)(2,1)}, u32[]{:S(2)}) copy-start(bf16[128,256]{1,0:T(8,128)(2,1)} %refs_3_) | copy-start | bytes 196612
  0.7 52.0 %copy-start = (bf16[4096,128]{1,0:T(8,128)(2,1)S(1)}, bf16[4096,128]{1,0:T(8,128)(2,1)}, u32[]{:S(2)}) copy-start(bf16[4096,128]{1,0:T(8,128)(2,1)} %feats_hbm.1) | copy-start | bytes 3145732
  0.7 52.0 %copy-start.1 = (s32[32,8]{0,1:T(8,128)S(1)}, s32[32,8]{0,1:T(8,128)}, u32[]{:S(2)}) copy-start(s32[32,8]{0,1:T(8,128)} %param.10) | copy-start | bytes 3076
  7.9 44.7 %all-to-all-start = ((bf16[128,32,128]{2,1,0:T(8,128)(2,1)}), bf16[128,32,128]{2,1,0:T(8,128)(2,1)S(1)}, u32[]{:S(2)}, u32[]{:S(2)}) async-start(bf16[128,32,128]{2,1,0:T(8,128)(2,1)} %bitcast.28), calls=%async_computation | async-start | bytes 2097152 | tf_op jit(solution)/shard_map/all_to_all | solution.py:426
  23.3 1.3 %collective-permute-start.1 = (bf16[176,128]{1,0:T(8,128)(2,1)S(1)}, bf16[176,128]{1,0:T(8,128)(2,1)S(1)}, u32[]{:S(2)}, u32[]{:S(2)}) collective-permute-start(bf16[176,128]{1,0:T(8,128)(2,1)S(1)} %pad.4.refs_5_), channel_id=1, source_target_pairs={{0,1},{1,0},{2,3},{3,2},{4,5},{5,4},{6,7},{7,6},{8,9},{9,8},{10,11... | collective-permute-start | bytes 135176 | tf_op jit(solution)/shard_map/ppermute | solution.py:436
  23.5 1.4 %collective-permute-start = (bf16[128,256]{1,0:T(8,128)(2,1)S(1)}, bf16[128,256]{1,0:T(8,128)(2,1)S(1)}, u32[]{:S(2)}, u32[]{:S(2)}) collective-permute-start(bf16[128,256]{1,0:T(8,128)(2,1)S(1)} %copy-done.2), channel_id=1, source_target_pairs={{0,1},{1,0},{2,3},{3,2},{4,5},{5,4},{6,7},{7,6},{8,9},{9,8},{10,11... | collective-permute-start | bytes 196616 | tf_op jit(solution)/shard_map/ppermute | solution.py:435
  52.6 7.8 %copy-start.4 = (f32[256]{0:T(256)S(1)}, f32[256]{0:T(256)}, u32[]{:S(2)}) copy-start(f32[256]{0:T(256)} %param.13) | copy-start | bytes 3076
  57.7 2.7 %collective-permute-start.2 = (bf16[4096,128]{1,0:T(8,128)(2,1)S(1)}, bf16[4096,128]{1,0:T(8,128)(2,1)S(1)}, u32[]{:S(2)}, u32[]{:S(2)}) collective-permute-start(bf16[4096,128]{1,0:T(8,128)(2,1)S(1)} %bitcast.22), channel_id=1, source_target_pairs={{0,1},{1,0},{2,3},{3,2},{4,5},{5,4},{6,7},{7,6},{8,9},{9,8},{10,11... | collective-permute-start | bytes 3145736 | tf_op jit(solution)/shard_map/ppermute | solution.py:448
  66.0 15.5 %all-to-all-start.1 = ((f32[8,56,128]{2,1,0:T(8,128)}), f32[8,56,128]{2,1,0:T(8,128)S(1)}, u32[]{:S(2)}, u32[]{:S(2)}) async-start(f32[8,56,128]{2,1,0:T(8,128)} %bitcast.11), calls=%async_computation.1 | async-start | bytes 458752 | tf_op jit(solution)/shard_map/all_to_all | solution.py:371
  81.5 40.0 %all-to-all-start.2 = ((bf16[128,32,128]{2,1,0:T(8,128)(2,1)}), bf16[128,32,128]{2,1,0:T(8,128)(2,1)S(1)}, u32[]{:S(2)}, u32[]{:S(2)}) async-start(bf16[128,32,128]{2,1,0:T(8,128)(2,1)} %bitcast.14), calls=%async_computation.2 | async-start | bytes 2097152 | tf_op jit(solution)/shard_map/all_to_all | solution.py:457
  89.9 6.1 %collective-permute-start.5 = (f32[56,128]{1,0:T(8,128)S(1)}, f32[56,128]{1,0:T(8,128)S(1)}, u32[]{:S(2)}, u32[]{:S(2)}) collective-permute-start(f32[56,128]{1,0:T(8,128)S(1)} %reduce_sum.9), channel_id=1, source_target_pairs={{0,6},{2,4},{4,2},{6,0},{8,14},{10,12},{12,10},{14,8},{16,22},{18,... | collective-permute-start | bytes 86024 | tf_op jit(solution)/shard_map/ppermute | solution.py:349
  91.5 5.7 %collective-permute-start.4 = (f32[56,128]{1,0:T(8,128)S(1)}, f32[56,128]{1,0:T(8,128)S(1)}, u32[]{:S(2)}, u32[]{:S(2)}) collective-permute-start(f32[56,128]{1,0:T(8,128)S(1)} %reduce_sum.9), channel_id=1, source_target_pairs={{0,4},{2,6},{4,0},{6,2},{8,12},{10,14},{12,8},{14,10},{16,20},{18,... | collective-permute-start | bytes 86024 | tf_op jit(solution)/shard_map/ppermute | solution.py:349
  93.0 4.2 %collective-permute-start.3 = (f32[56,128]{1,0:T(8,128)S(1)}, f32[56,128]{1,0:T(8,128)S(1)}, u32[]{:S(2)}, u32[]{:S(2)}) collective-permute-start(f32[56,128]{1,0:T(8,128)S(1)} %reduce_sum.9), channel_id=1, source_target_pairs={{0,2},{2,0},{4,6},{6,4},{8,10},{10,8},{12,14},{14,12},{16,18},{18,... | collective-permute-start | bytes 86024 | tf_op jit(solution)/shard_map/ppermute | solution.py:349
  97.2 5.5 %collective-permute-start.8 = (f32[56,128]{1,0:T(8,128)S(1)}, f32[56,128]{1,0:T(8,128)S(1)}, u32[]{:S(2)}, u32[]{:S(2)}) collective-permute-start(f32[56,128]{1,0:T(8,128)S(1)} %add_add_fusion.1), channel_id=1, source_target_pairs={{0,192},{2,194},{4,196},{6,198},{8,200},{10,202},{12,204},{14,206}... | collective-permute-start | bytes 86024 | tf_op jit(solution)/shard_map/ppermute | solution.py:349
  100.5 5.8 %collective-permute-start.7 = (f32[56,128]{1,0:T(8,128)S(1)}, f32[56,128]{1,0:T(8,128)S(1)}, u32[]{:S(2)}, u32[]{:S(2)}) collective-permute-start(f32[56,128]{1,0:T(8,128)S(1)} %add_add_fusion.1), channel_id=1, source_target_pairs={{0,128},{2,130},{4,132},{6,134},{8,136},{10,138},{12,140},{14,142}... | collective-permute-start | bytes 86024 | tf_op jit(solution)/shard_map/ppermute | solution.py:349
  100.9 5.3 %collective-permute-start.6 = (f32[56,128]{1,0:T(8,128)S(1)}, f32[56,128]{1,0:T(8,128)S(1)}, u32[]{:S(2)}, u32[]{:S(2)}) collective-permute-start(f32[56,128]{1,0:T(8,128)S(1)} %add_add_fusion.1), channel_id=1, source_target_pairs={{0,64},{2,66},{4,68},{6,70},{8,72},{10,74},{12,76},{14,78},{16,80}... | collective-permute-start | bytes 86024 | tf_op jit(solution)/shard_map/ppermute | solution.py:349
  106.3 10.4 %collective-permute-start.15 = (f32[56,128]{1,0:T(8,128)S(1)}, f32[56,128]{1,0:T(8,128)S(1)}, u32[]{:S(2)}, u32[]{:S(2)}) collective-permute-start(f32[56,128]{1,0:T(8,128)S(1)} %add_add_fusion.refs_0_), channel_id=1, source_target_pairs={{0,56},{2,58},{4,60},{6,62},{8,0},{10,2},{12,4},{14,6},{16,8},{18,... | collective-permute-start | bytes 86024 | tf_op jit(solution)/shard_map/ppermute | solution.py:349
  109.0 11.4 %collective-permute-start.14 = (f32[56,128]{1,0:T(8,128)S(1)}, f32[56,128]{1,0:T(8,128)S(1)}, u32[]{:S(2)}, u32[]{:S(2)}) collective-permute-start(f32[56,128]{1,0:T(8,128)S(1)} %add_add_fusion.refs_0_), channel_id=1, source_target_pairs={{0,48},{2,50},{4,52},{6,54},{8,56},{10,58},{12,60},{14,62},{16,0},... | collective-permute-start | bytes 86024 | tf_op jit(solution)/shard_map/ppermute | solution.py:349
  111.4 17.6 %collective-permute-start.13 = (f32[56,128]{1,0:T(8,128)S(1)}, f32[56,128]{1,0:T(8,128)S(1)}, u32[]{:S(2)}, u32[]{:S(2)}) collective-permute-start(f32[56,128]{1,0:T(8,128)S(1)} %add_add_fusion.refs_0_), channel_id=1, source_target_pairs={{0,40},{2,42},{4,44},{6,46},{8,48},{10,50},{12,52},{14,54},{16,56}... | collective-permute-start | bytes 86024 | tf_op jit(solution)/shard_map/ppermute | solution.py:349
  112.6 16.4 %collective-permute-start.12 = (f32[56,128]{1,0:T(8,128)S(1)}, f32[56,128]{1,0:T(8,128)S(1)}, u32[]{:S(2)}, u32[]{:S(2)}) collective-permute-start(f32[56,128]{1,0:T(8,128)S(1)} %add_add_fusion.refs_0_), channel_id=1, source_target_pairs={{0,32},{2,34},{4,36},{6,38},{8,40},{10,42},{12,44},{14,46},{16,48}... | collective-permute-start | bytes 86024 | tf_op jit(solution)/shard_map/ppermute | solution.py:349
  116.7 12.3 %collective-permute-start.11 = (f32[56,128]{1,0:T(8,128)S(1)}, f32[56,128]{1,0:T(8,128)S(1)}, u32[]{:S(2)}, u32[]{:S(2)}) collective-permute-start(f32[56,128]{1,0:T(8,128)S(1)} %add_add_fusion.refs_0_), channel_id=1, source_target_pairs={{0,24},{2,26},{4,28},{6,30},{8,32},{10,34},{12,36},{14,38},{16,40}... | collective-permute-start | bytes 86024 | tf_op jit(solution)/shard_map/ppermute | solution.py:349
  116.7 12.3 %collective-permute-start.10 = (f32[56,128]{1,0:T(8,128)S(1)}, f32[56,128]{1,0:T(8,128)S(1)}, u32[]{:S(2)}, u32[]{:S(2)}) collective-permute-start(f32[56,128]{1,0:T(8,128)S(1)} %add_add_fusion.refs_0_), channel_id=1, source_target_pairs={{0,16},{2,18},{4,20},{6,22},{8,24},{10,26},{12,28},{14,30},{16,32}... | collective-permute-start | bytes 86024 | tf_op jit(solution)/shard_map/ppermute | solution.py:349
  120.4 8.6 %collective-permute-start.9 = (f32[56,128]{1,0:T(8,128)S(1)}, f32[56,128]{1,0:T(8,128)S(1)}, u32[]{:S(2)}, u32[]{:S(2)}) collective-permute-start(f32[56,128]{1,0:T(8,128)S(1)} %add_add_fusion.refs_0_), channel_id=1, source_target_pairs={{0,8},{2,10},{4,12},{6,14},{8,16},{10,18},{12,20},{14,22},{16,24},... | collective-permute-start | bytes 86024 | tf_op jit(solution)/shard_map/ppermute | solution.py:349
  (1 other events, 7.8 us)
